TPU v7x, 512 devices: a whole 4x4x16 slice. The times are simulated.
512 devices in a mesh: dp: 64 (over z, y_lo, core), tensor: 8 (over x, y_hi).
Axes of the slice: x: 4, y: 4 (y_hi: 2, y_lo: 2; y = y_hi * 2 + y_lo), z: 16, core: 2. Of those that a mesh axis runs over, the one named last changes fastest.
Arguments:
- inputs: bfloat16 [16384, 4096], P('dp', 'tensor'), may hold values from -6 to 6
- cotangent: bfloat16 [16384, 4096], P('dp', 'tensor'), may hold values from -6 to 6
- gate_pre: bfloat16 [16384, 11008], P('dp', 'tensor'), may hold values from -6 to 6
- up_pre: bfloat16 [16384, 11008], P('dp', 'tensor'), may hold values from -6 to 6
- down_weight: bfloat16 [11008, 4096], P('tensor', 'dp'), may hold values from -0.0546875 to 0.0546875
- proj_in_x: bfloat16 [4096, 128], P('tensor'), may hold values from -0.09375 to 0.09375
- proj_in_h: bfloat16 [11008, 64], P('tensor'), may hold values from -0.0546875 to 0.0546875
- proj_out_ff: bfloat16 [11008, 128], P('tensor'), may hold values from -0.0546875 to 0.0546875
- proj_out_d: bfloat16 [4096, 64], P('tensor'), may hold values from -0.09375 to 0.09375
- queries: bfloat16 [8192, 12288], P('dp', 'tensor'), may hold values from -0.0546875 to 0.0546875
- lengths: int32 [8], replicated, may hold values from 512 to 2048
Outputs:
- scores: float32 [8, 8192], P(None, 'dp')
All inputs are finite; a program needn't handle non-finite values.
Results may differ from a plain program's by a relative error of at most 0.0029.
Values may be sent and summed in bfloat16 or wider, within the bound.
No kernel may reach another device: no remote copies, remote signals or barrier semaphores. Data moves between devices by JAX's collectives and lax.ppermute only.
A program may use at most 64 MiB of HBM per device.

v0:
```python
import math

import jax
import jax.numpy as jnp
from jax import lax
from jax.sharding import PartitionSpec as P

LEN = 2048


def on_device(
    inputs,
    cotangent,
    gate_pre,
    up_pre,
    down_weight,
    proj_in_x,
    proj_in_h,
    proj_out_ff,
    proj_out_d,
    queries,
    lengths,
):
    tok_rows = inputs.shape[0]
    proj_rank = proj_in_h.shape[1]
    full_cot = lax.all_gather(cotangent, "tensor", axis=1, tiled=True)
    grad_hidden = lax.dot_general(
        full_cot,
        lax.all_gather(down_weight, "dp", axis=1, tiled=True),
        (((1,), (1,)), ((), ())),
        preferred_element_type=jnp.float32,
    )
    gate_float = gate_pre.astype(jnp.float32)
    up_float = up_pre.astype(jnp.float32)
    gate_sigmoid = jax.nn.sigmoid(gate_float)
    gate_silu = gate_float * gate_sigmoid
    hidden = (gate_silu * up_float).astype(jnp.bfloat16)
    grad_gate = (
        grad_hidden * up_float * gate_sigmoid * (1.0 + gate_float * (1.0 - gate_sigmoid))
    ).astype(jnp.bfloat16)
    grad_up = (grad_hidden * gate_silu).astype(jnp.bfloat16)
    part_h = jnp.dot(hidden, proj_in_h, preferred_element_type=jnp.float32)
    part_gate = jnp.dot(grad_gate, proj_out_ff[:, :proj_rank], preferred_element_type=jnp.float32)
    part_up = jnp.dot(grad_up, proj_out_ff[:, proj_rank:], preferred_element_type=jnp.float32)
    part_d = jnp.dot(cotangent, proj_out_d, preferred_element_type=jnp.float32)
    whole_inputs, whole_proj = (
        lax.all_gather(inputs, "tensor", axis=1, tiled=True),
        lax.all_gather(proj_in_x, "tensor", axis=0, tiled=True),
    )
    proj_x = jnp.dot(whole_inputs, whole_proj, preferred_element_type=jnp.float32)
    proj_h, proj_gate, proj_up, proj_d = lax.psum((part_h, part_gate, part_up, part_d), "tensor")
    first_event = lax.axis_index("dp") * tok_rows
    own_session = first_event // LEN
    positions = first_event % LEN + jnp.arange(tok_rows, dtype=jnp.int32)
    live_mask = (positions < lengths[own_session]).astype(jnp.float32)[:, None]
    inputs_side = jnp.stack([proj_x[:, :proj_rank], proj_x[:, proj_rank:], proj_h])
    outputs_side = jnp.stack([proj_gate, proj_up, proj_d]) * live_mask[None]
    blocks = jnp.einsum(
        "ltr,lts->lrs", inputs_side, outputs_side, precision=lax.Precision.HIGHEST
    ).reshape(-1)
    share_width = blocks.shape[0] // lax.axis_size("tensor")
    tensor_share = lax.dynamic_slice_in_dim(
        blocks, lax.axis_index("tensor") * share_width, share_width, 0
    )
    group_span = LEN // tok_rows
    sessions = lax.axis_size("dp") // group_span
    every_piece = lax.all_gather(tensor_share[None, :], "dp", axis=0, tiled=True)
    session_grads = every_piece.reshape(sessions, group_span, share_width).sum(axis=1)
    score_scale = 1.0 / math.sqrt(LEN)
    partial_scores = (
        lax.dot_general(
            session_grads,
            queries.astype(jnp.float32),
            (((1,), (1,)), ((), ())),
            precision=lax.Precision.HIGHEST,
        )
        * score_scale
    )
    return lax.psum(partial_scores, "tensor")


def solution(mesh):
    return jax.shard_map(
        on_device,
        mesh=mesh,
        in_specs=(
            P("dp", "tensor"),
            P("dp", "tensor"),
            P("dp", "tensor"),
            P("dp", "tensor"),
            P("tensor", "dp"),
            P("tensor", None),
            P("tensor", None),
            P("tensor", None),
            P("tensor", None),
            P("dp", "tensor"),
            P(),
        ),
        out_specs=P(None, "dp"),
        check_vma=False,
    )
```

profile of v0, /device:TPU:1, one launch (start us, length us, event | category | flops | bytes accessed | tf_op | source)
XLA Modules:
  0.0 554.6 jit_solution(8868360081886069722)
XLA Ops:
  6.5 0.0 copy-start
  6.5 0.0 all-gather.11.cloned.1.call-start
  6.5 0.7 all-gather.11.cloned.1.call-update
  7.3 0.0 all-gather.13.cloned.1.call-start
  7.3 0.7 all-gather.13.cloned.1.call-update
  8.0 0.0 all-gather.9.cloned.1.call-start
  8.1 0.7 all-gather.9.cloned.1.call-update
  8.7 0.0 all-gather.7.cloned.1.call-start
  8.8 0.5 all-gather.7.cloned.1.call-update
  9.3 0.0 all-reduce.3.cloned.1.call-start
  9.4 1.2 dynamic_slice.6
  10.6 0.6 compare_convert_fusion
  11.3 1.8 convolution_bitcast_fusion.1
  13.1 2.6 convolution_bitcast_fusion
  15.6 72.1 %all-gather.11.cloned.1.call-done = bf16[256,4096]{1,0:T(8,128)(2,1)} async-done(((bf16[256,512]{1,0:T(8,128)(2,1)}), bf16[256,4096]{1,0:T(8,128)(2,1)}) %all-gather.11.cloned.1.call-update) | async-done | bytes 2097168 | tf_op jit(solution)/shard_map/all_gather | solution.py:26
  87.8 136.3 %all-gather.13.cloned.1.call-done = bf16[1376,4096]{0,1:T(8,128)(2,1)} async-done(((bf16[1376,64]{0,1:T(8,128)(2,1)}), bf16[1376,4096]{0,1:T(8,128)(2,1)}) %all-gather.13.cloned.1.call-update) | async-done | bytes 11272208 | tf_op jit(solution)/shard_map/all_gather | solution.py:29
  224.1 9.5 %fusion.28 = f32[256,1376]{0,1:T(8,128)S(1)} fusion(bf16[256,4096]{1,0:T(8,128)(2,1)} %all-gather.11.cloned.1.call-done, bf16[1376,4096]{0,1:T(8,128)(2,1)} %all-gather.13.cloned.1.call-done), kind=kOutput, calls=%fused_computation.42 | convolution fusion | flops 2885681152 | bytes 14778368 | tf_op jit(solution)/shard_map/dot_general | solution.py:27
  233.6 0.0 copy-start.1
  233.6 1.2 convolution_bitcast_fusion.2
  234.9 1.4 convolution_bitcast_fusion.3
  236.3 0.0 all-reduce.3.cloned.1.call-update
  236.3 49.0 %all-gather.9.cloned.1.call-done = bf16[4096,128]{1,0:T(8,128)(2,1)} async-done(((bf16[512,128]{1,0:T(8,128)(2,1)}), bf16[4096,128]{1,0:T(8,128)(2,1)}) %all-gather.9.cloned.1.call-update) | async-done | bytes 1048592 | tf_op jit(solution)/shard_map/all_gather | solution.py:48
  285.3 74.8 %all-gather.7.cloned.1.call-done = bf16[256,4096]{1,0:T(8,128)(2,1)} async-done(((bf16[256,512]{1,0:T(8,128)(2,1)}), bf16[256,4096]{1,0:T(8,128)(2,1)}) %all-gather.7.cloned.1.call-update) | async-done | bytes 2097168 | tf_op jit(solution)/shard_map/all_gather | solution.py:47
  360.1 2.7 fusion.27
  362.8 94.5 %all-reduce.3.cloned.1.call-done = (f32[1,256,64]{1,2,0:T(8,128)}, f32[1,256,64]{1,2,0:T(8,128)}, f32[1,256,64]{1,2,0:T(8,128)}, f32[1,256,64]{1,2,0:T(8,128)}) async-done(((f32[1,256,64]{1,2,0:T(8,128)}, f32[1,256,64]{1,2,0:T(8,128)}, f32[1,256,64]{1,2,0:T(8,128)}, f32[1,256,64]{1,2,0:T(8,128)}), (f32[1,256,64]{1,2,0:T(8,128)}, f32[1,256,64]{1,2,0:T(8,128)}, f32[1,256,64]{1,2,0:T(8,128)}, ...) | async-done | bytes 262160 | tf_op jit(solution)/shard_map/psum | solution.py:51
  457.3 1.2 fusion.12
  458.6 0.1 reshape.12
  458.7 0.1 dynamic_slice.7
  458.8 70.2 %all-gather.1 = f32[64,1,1536]{2,1,0:T(1,128)S(1)} all-gather(f32[1,1,1536]{2,1,0:T(1,128)S(1)} %reshape.16), channel_id=2, replica_groups=mesh['dp'=64,'tensor'=8] {'dp'}, dimensions={0}, use_global_device_ids=true | all-gather | bytes 399360 | tf_op jit(solution)/shard_map/all_gather | solution.py:67
  529.0 0.1 bitcast_reduce_fusion
  529.1 0.4 convolution_multiply_fusion
  529.5 18.6 %psum.39 = f32[8,128]{1,0:T(8,128)} all-reduce(f32[8,128]{1,0:T(8,128)S(1)} %convolution_multiply_fusion), channel_id=1, replica_groups=mesh['dp'=64,'tensor'=8] {'tensor'}, use_global_device_ids=true, to_apply=%region_5.6 | all-reduce | flops 1024 | bytes 8192 | tf_op jit(solution)/shard_map/psum | solution.py:79
  (8 shorter events, 0.0 us)
Async XLA Ops:
  6.5 522.6 %copy-start = (bf16[128,1536]{1,0:T(8,128)(2,1)S(1)}, bf16[128,1536]{1,0:T(8,128)(2,1)}, u32[]{:S(2)}) copy-start(bf16[128,1536]{1,0:T(8,128)(2,1)} %param.20) | copy-start | bytes 1179652
  6.5 81.2 %all-gather.11.cloned.1.call-start = ((), (), s32[]{:S(2)}) async-start(), calls=%async_computation.2 | async-start | bytes 2359296 | tf_op jit(solution)/shard_map/all_gather | solution.py:26
  7.3 216.9 %all-gather.13.cloned.1.call-start = ((), (), s32[]{:S(2)}) async-start(), calls=%async_computation.3 | async-start | bytes 11714560 | tf_op jit(solution)/shard_map/all_gather | solution.py:29
  8.0 277.3 %all-gather.9.cloned.1.call-start = ((), (), s32[]{:S(2)}) async-start(), calls=%async_computation.1 | async-start | bytes 1179648 | tf_op jit(solution)/shard_map/all_gather | solution.py:48
  8.7 351.4 %all-gather.7.cloned.1.call-start = ((), (), s32[]{:S(2)}) async-start(), calls=%async_computation | async-start | bytes 2359296 | tf_op jit(solution)/shard_map/all_gather | solution.py:47
  9.3 448.0 %all-reduce.3.cloned.1.call-start = ((), (), s32[]{:S(2)}) async-start(), calls=%async_computation.4 | async-start | bytes 524288 | tf_op jit(solution)/shard_map/psum | solution.py:51
  15.6 218.0 %copy-start.2 = (bf16[256,1376]{0,1:T(8,128)(2,1)S(1)}, bf16[256,1376]{0,1:T(8,128)(2,1)}, u32[]{:S(2)}) copy-start(bf16[256,1376]{0,1:T(8,128)(2,1)} %param.13) | copy-start | bytes 2113540
  15.6 218.0 %copy-start.3 = (bf16[1376,128]{1,0:T(8,128)(2,1)S(1)}, bf16[1376,128]{1,0:T(8,128)(2,1)}, u32[]{:S(2)}) copy-start(bf16[1376,128]{1,0:T(8,128)(2,1)} %param.18) | copy-start | bytes 1056772
  233.6 1.3 copy-start.1
Sparse Core Ops, SparseCore 0:
  10.4 77.3 all-gather.10
  89.9 134.1 all-gather.12
  227.3 57.8 all-gather.8
  288.2 71.8 all-gather.6
  363.1 94.1 all-reduce.2
where the time goes:
time: 555 us
  waiting for transfers between devices  429 us (77%)
  blocking collectives  88.8 us (16%)
  matrix products  20.8 us (4%)
  between operations  13.2 us (2%)
    all_gather x1, waiting for transfers between devices, on_device(): lax.all_gather(down_weight, 'dp', axis=1, tiled=True)  136 us
    psum x1, waiting for transfers between devices, on_device(): lax.psum((part_h, part_gate, part_up, part_d), 'tensor')  94.5 us
    all_gather x1, waiting for transfers between devices, on_device(): lax.all_gather(inputs, 'tensor', axis=1, tiled=True)  74.8 us
    all_gather x1, waiting for transfers between devices, on_device(): full_cot = lax.all_gather(cotangent, 'tensor', axis=1, tiled=True)  72.1 us
    all_gather x1, blocking collectives, on_device(): lax.all_gather(tensor_share[None, :], 'dp', axis=0, tiled=True)  70.2 us
    all_gather x1, waiting for transfers between devices, on_device(): lax.all_gather(proj_in_x, 'tensor', axis=0, tiled=True)  49 us
    psum x1, blocking collectives, on_device(): return lax.psum(partial_scores, 'tensor')  18.6 us
  transfers between devices with their start and end apart: 5, of which 5 were waited for; matrix products, arithmetic and copies ran while one was open for 4% of the time, Pallas kernels for 0%

commit v1 on v0

v1 whole, which is shorter than its diff:
```python
import math

import jax
import jax.numpy as jnp
from jax import lax
from jax.sharding import Mesh
from jax.sharding import PartitionSpec as P

LEN = 2048
DP = ("zh", "zl", "yl", "c")
TENSOR = ("x", "yh")
SWAP = [(0, 1), (1, 0)]
HIGHEST = lax.Precision.HIGHEST


def dot(a, b):
    return jnp.dot(a, b, preferred_element_type=jnp.float32)


def split_dot(a, b):
    high = a.astype(jnp.bfloat16)
    low = (a - high.astype(jnp.float32)).astype(jnp.bfloat16)
    return dot(high, b) + dot(low, b)


def give_all(block, axes):
    n = lax.axis_size(axes)
    return lax.all_to_all(jnp.broadcast_to(block[None], (n,) + block.shape), axes, 0, 0)


def on_device(
    inputs,
    cotangent,
    gate_pre,
    up_pre,
    down_weight,
    proj_in_x,
    proj_in_h,
    proj_out_ff,
    proj_out_d,
    queries,
    lengths,
):
    rows, width = cotangent.shape
    hid = gate_pre.shape[1]
    rank = proj_in_h.shape[1]
    own_yl = lax.axis_index("yl")
    tensor_size = lax.axis_size(TENSOR)

    weight = lax.all_gather(down_weight.T, ("zh", "zl", "c"), axis=0, tiled=True)

    halves = cotangent.reshape(rows, -1, 2, 2 * down_weight.shape[1])
    first, second = (halves[:, :, i].reshape(rows, width // 2) for i in (0, 1))
    mine = jnp.where(own_yl == 0, first, second)
    theirs = jnp.where(own_yl == 0, second, first)
    both_cot = jnp.concatenate([mine, lax.ppermute(theirs, "yl", SWAP)], axis=0)
    partner_pre = lax.ppermute(jnp.concatenate([gate_pre, up_pre], axis=0), "yl", SWAP)
    full_cot = give_all(both_cot, TENSOR)

    gate_float = jnp.concatenate([gate_pre, partner_pre[:rows]], axis=0).astype(jnp.float32)
    up_float = jnp.concatenate([up_pre, partner_pre[rows:]], axis=0).astype(jnp.float32)
    sig = jax.nn.sigmoid(gate_float)
    silu = gate_float * sig
    gate_slope = up_float * sig * (1.0 + gate_float * (1.0 - sig))
    own_gate = gate_pre.astype(jnp.float32)
    hidden = (own_gate * jax.nn.sigmoid(own_gate) * up_pre.astype(jnp.float32)).astype(jnp.bfloat16)

    parts = jnp.concatenate(
        [dot(inputs, proj_in_x), dot(hidden, proj_in_h), dot(cotangent, proj_out_d)], axis=1
    )
    some = rows // tensor_size
    sums = lax.all_to_all(parts.reshape(tensor_size, some, 4 * rank), TENSOR, 0, 0).sum(axis=0)
    first_event = lax.axis_index(DP) * rows + lax.axis_index(TENSOR) * some
    positions = first_event % LEN + jnp.arange(some, dtype=jnp.int32)
    live = (positions < lengths[first_event // LEN]).astype(jnp.float32)[:, None]
    sums_x, sums_h, sums_d = sums[:, : 2 * rank] * live, sums[:, 2 * rank : 3 * rank], sums[:, 3 * rank :]
    block_d = jnp.einsum("tr,ts->rs", sums_h, sums_d * live, precision=HIGHEST)
    proj_x = give_all(sums_x, ("yl",) + TENSOR).reshape(2, rows, 2 * rank)
    proj_x = jnp.where(own_yl == 0, proj_x, proj_x[::-1]).reshape(2 * rows, 2 * rank)

    grad_hidden = lax.dot_general(
        full_cot,
        weight.reshape(tensor_size, width // 2, hid),
        (((0, 2), (0, 1)), ((), ())),
        preferred_element_type=jnp.float32,
    )
    proj_gate = split_dot(grad_hidden * gate_slope, proj_out_ff[:, :rank])
    proj_up = split_dot(grad_hidden * silu, proj_out_ff[:, rank:])
    block_g = jnp.einsum("tr,ts->rs", proj_x[:, :rank], proj_gate, precision=HIGHEST)
    block_u = jnp.einsum("tr,ts->rs", proj_x[:, rank:], proj_up, precision=HIGHEST)

    blocks = jnp.concatenate([block_g, block_u, block_d], axis=0)
    group = ("zl", "yl", "c")
    members = tensor_size * lax.axis_size(group)
    piece = lax.all_to_all(blocks.reshape(members, -1), TENSOR + group, 0, 0).sum(axis=0)
    pieces = give_all(piece, ("zh",))
    session_grads = give_all(pieces, group).transpose(1, 0, 2).reshape(pieces.shape[0], -1)
    partial_scores = lax.dot_general(
        session_grads,
        queries.astype(jnp.float32),
        (((1,), (1,)), ((), ())),
        precision=HIGHEST,
    ) * (1.0 / math.sqrt(LEN))
    return give_all(partial_scores, TENSOR).sum(axis=0)


def solution(mesh):
    fine = Mesh(mesh.devices.reshape(8, 2, 2, 2, 4, 2), DP + TENSOR)
    return jax.shard_map(
        on_device,
        mesh=fine,
        in_specs=(
            P(DP, TENSOR),
            P(DP, TENSOR),
            P(DP, TENSOR),
            P(DP, TENSOR),
            P(TENSOR, DP),
            P(TENSOR, None),
            P(TENSOR, None),
            P(TENSOR, None),
            P(TENSOR, None),
            P(DP, TENSOR),
            P(),
        ),
        out_specs=P(None, DP),
        check_vma=False,
    )
```

time: 555 us -> 170 us (0.31)
  waiting for transfers between devices: 429 us -> 51.4 us
  blocking collectives: 88.8 us -> 59.2 us
  starting transfers between devices: 0.15 us -> 20.5 us
    all_gather x4 -> x1, waiting for transfers between devices: 332 us -> 0.78 us  [on_device(): lax.all_gather(down_weight.T, ('zh', 'zl', 'c'), axis=0, tiled=True)]
    psum x1 -> x0, waiting for transfers between devices: 94.5 us -> none  [on_device(): lax.psum((part_h, part_gate, part_up, part_d), 'tensor')]
    all_gather x1 -> x0, blocking collectives: 70.2 us -> none  [on_device(): lax.all_gather(tensor_share[None, :], 'dp', axis=0, tiled=True)]
    all_to_all x0 -> x4, blocking collectives: none -> 59.2 us  [the longest x3 42.8 us: give_all(): lax.all_to_all(jnp.broadcast_to(block[None], (n,) + block.shape), axes, 0...]
    ppermute x0 -> x2, waiting for transfers between devices: none -> 39 us  [the longest x1 39 us: on_device(): lax.ppermute(jnp.concatenate([gate_pre, up_pre], axis=0), 'yl', SWAP)]
    psum x1 -> x0, blocking collectives: 18.6 us -> none  [on_device(): return lax.psum(partial_scores, 'tensor')]
    all_to_all x0 -> x3, starting transfers between devices: none -> 14.9 us  [the longest x1 7.48 us: on_device(): lax.all_to_all(parts.reshape(tensor_size, some, 4 * rank), TENSOR, 0, 0)]
    all_to_all x0 -> x3, waiting for transfers between devices: none -> 11 us  [the longest x2 7.42 us: give_all(): lax.all_to_all(jnp.broadcast_to(block[None], (n,) + block.shape), axes, 0...]
  transfers between devices with their start and end apart: 5 -> 6, of which waited for: 5 -> 5; matrix products, arithmetic and copies ran while one was open for 4% -> 8% of each run, Pallas kernels for 0% -> 0%
where the time goes in v1:
time: 170 us
  blocking collectives  59.2 us (35%)
  waiting for transfers between devices  51.4 us (30%)
  starting transfers between devices  20.5 us (12%)
  matrix products  15.4 us (9%)
  between operations  13.7 us (8%)
  local copies, waits for them, and re-layouts  6.78 us (4%)
  other arithmetic  2.82 us (2%)
    all_to_all x3, blocking collectives, give_all(): lax.all_to_all(jnp.broadcast_to(block[None], (n,) + block.shape), axes, 0...  42.8 us
    ppermute x1, waiting for transfers between devices, on_device(): lax.ppermute(jnp.concatenate([gate_pre, up_pre], axis=0), 'yl', SWAP)  39 us
    all_to_all x1, blocking collectives, on_device(): lax.all_to_all(blocks.reshape(members, -1), TENSOR + group, 0, 0)  16.4 us
    dot_general x1, matrix products, on_device(): lax.dot_general(full_cot, weight.reshape(tensor_size, width // 2, hid), (...  7.74 us
    all_to_all x1, starting transfers between devices, on_device(): lax.all_to_all(parts.reshape(tensor_size, some, 4 * rank), TENSOR, 0, 0)  7.48 us
    all_to_all x2, starting transfers between devices, give_all(): lax.all_to_all(jnp.broadcast_to(block[None], (n,) + block.shape), axes, 0...  7.44 us
    all_to_all x2, waiting for transfers between devices, give_all(): lax.all_to_all(jnp.broadcast_to(block[None], (n,) + block.shape), axes, 0...  7.42 us
    dot_general x7, matrix products, dot(): return jnp.dot(a, b, preferred_element_type=jnp.float32)  6.25 us
  transfers between devices with their start and end apart: 6, of which 5 were waited for; matrix products, arithmetic and copies ran while one was open for 8% of the time, Pallas kernels for 0%

profile of v1, /device:TPU:1, one launch (start us, length us, event | category | flops | bytes accessed | tf_op | source)
XLA Modules:
  0.0 169.8 jit_solution(16041220638129999025)
XLA Ops:
  6.5 0.7 all-gather.2.cloned.1.call-update
  7.3 1.2 fusion.34
  8.4 1.2 fusion.33
  9.7 2.0 %fusion.18 = f32[256,64]{0,1:T(8,128)S(1)} fusion(bf16[1376,64]{0,1:T(8,128)(2,1)} %param.17, bf16[256,1376]{0,1:T(8,128)(2,1)} %param.14, bf16[256,1376]{0,1:T(8,128)(2,1)} %param.13), kind=kOutput, calls=%fused_computation.31 | convolution fusion | flops 47906816 | bytes 1650688 | tf_op jit(solution)/shard_map/dot_general | solution.py:17
  11.7 0.8 copy.28
  12.5 7.5 %all-to-all-start = ((f32[8,32,256]{2,1,0:T(8,128)}), f32[8,32,256]{2,1,0:T(8,128)S(1)}, u32[]{:S(2)}, u32[]{:S(2)}) async-start(f32[8,32,256]{2,1,0:T(8,128)} %bitcast), calls=%async_computation | async-start | bytes 524288 | tf_op jit(solution)/shard_map/all_to_all | solution.py:72
  20.2 2.3 %collective-permute-start = (bf16[256,256]{0,1:T(8,128)(2,1)S(1)}, bf16[256,256]{0,1:T(8,128)(2,1)S(1)}, u32[]{:S(2)}, u32[]{:S(2)}) collective-permute-start(bf16[256,256]{0,1:T(8,128)(2,1)S(1)} %bitcast.33), channel_id=1, source_target_pairs={{0,16},{16,0},{1,17},{17,1},{2,18},{18,2},{3,19},{19,3},{4,20},{20... | collective-permute-start | bytes 393224 | tf_op jit(solution)/shard_map/ppermute | solution.py:56
  22.6 0.6 dynamic_slice.3
  23.2 0.6 compare_convert_fusion
  23.8 3.5 %all-to-all-done = f32[8,32,256]{2,1,0:T(8,128)S(1)} async-done(((f32[8,32,256]{2,1,0:T(8,128)}), f32[8,32,256]{2,1,0:T(8,128)S(1)}, u32[]{:S(2)}, u32[]{:S(2)}) %all-to-all-start) | async-done | bytes 262176 | tf_op jit(solution)/shard_map/all_to_all | solution.py:72
  27.4 0.7 broadcast_in_dim.12
  28.2 3.8 %all-to-all-start.1 = ((f32[16,32,128]{2,1,0:T(8,128)}), f32[16,32,128]{2,1,0:T(8,128)S(1)}, u32[]{:S(2)}, u32[]{:S(2)}) async-start(f32[16,32,128]{2,1,0:T(8,128)} %broadcast_in_dim.12), calls=%async_computation.1 | async-start | bytes 524288 | tf_op jit(solution)/shard_map/all_to_all | solution.py:28
  32.0 1.2 pad_maximum_fusion.1
  33.3 3.3 %collective-permute-start.1 = (bf16[512,1376]{0,1:T(8,128)(2,1)}, bf16[512,1376]{0,1:T(8,128)(2,1)}, u32[]{:S(2)}, u32[]{:S(2)}) collective-permute-start(bf16[512,1376]{0,1:T(8,128)(2,1)} %pad_maximum_fusion.1), channel_id=1, source_target_pairs={{0,16},{16,0},{1,17},{17,1},{2,18},{18,2},{3,19},{19,3},{4,20},{20... | collective-permute-start | bytes 4227080 | tf_op jit(solution)/shard_map/ppermute | solution.py:57
  36.7 3.0 %all-to-all-done.1 = f32[16,32,128]{2,1,0:T(8,128)S(1)} async-done(((f32[16,32,128]{2,1,0:T(8,128)}), f32[16,32,128]{2,1,0:T(8,128)S(1)}, u32[]{:S(2)}, u32[]{:S(2)}) %all-to-all-start.1) | async-done | bytes 262176 | tf_op jit(solution)/shard_map/all_to_all | solution.py:28
  39.7 1.5 broadcast_in_dim.13
  41.1 3.6 %all-to-all-start.2 = ((bf16[8,512,256]{2,1,0:T(8,128)(2,1)}), bf16[8,512,256]{2,1,0:T(8,128)(2,1)S(1)}, u32[]{:S(2)}, u32[]{:S(2)}) async-start(bf16[8,512,256]{2,1,0:T(8,128)(2,1)} %broadcast_in_dim.13), calls=%async_computation.2 | async-start | bytes 4194304 | tf_op jit(solution)/shard_map/all_to_all | solution.py:28
  45.1 39.0 %collective-permute-done.1 = bf16[512,1376]{0,1:T(8,128)(2,1)} collective-permute-done((bf16[512,1376]{0,1:T(8,128)(2,1)}, bf16[512,1376]{0,1:T(8,128)(2,1)}, u32[]{:S(2)}, u32[]{:S(2)}) %collective-permute-start.1) | collective-permute-done | bytes 1409056 | tf_op jit(solution)/shard_map/ppermute | solution.py:57
  84.1 2.5 %fusion.32 = (bf16[256,1376]{0,1:T(8,128)(2,1)}, bf16[256,1376]{0,1:T(8,128)(2,1)}) fusion(bf16[512,1376]{0,1:T(8,128)(2,1)} %collective-permute-done.1), kind=kLoop, calls=%fused_computation.54 | loop fusion | bytes 2818048 | tf_op jit(solution)/shard_map/slice | solution.py:61
  86.6 4.5 %all-to-all-done.2 = bf16[8,512,256]{2,1,0:T(8,128)(2,1)S(1)} async-done(((bf16[8,512,256]{2,1,0:T(8,128)(2,1)}), bf16[8,512,256]{2,1,0:T(8,128)(2,1)S(1)}, u32[]{:S(2)}, u32[]{:S(2)}) %all-to-all-start.2) | async-done | bytes 2097184 | tf_op jit(solution)/shard_map/all_to_all | solution.py:28
  91.1 0.8 all-gather.2.cloned.1.call-done
  91.8 7.7 %fusion.5 = (f32[512,1376]{0,1:T(8,128)S(1)}, f32[512,1376]{0,1:T(8,128)S(1)}) fusion(bf16[256,1376]{0,1:T(8,128)(2,1)} %get-tuple-element.7, bf16[256,1376]{0,1:T(8,128)(2,1)} %param.14, bf16[256,1376]{0,1:T(8,128)(2,1)} %get-tuple-element.8, bf16[256,1376]{0,1:T(8,128)(2,1)} %param.13, bf16[8,512,256]{2,1,0:T(8,128)(2,1)S(1)} %all-to-all-done.2, ...), kind=kOutput, calls=%fused_computation.9 | convolution fusion | flops 2899066880 | bytes 16187392 | tf_op jit(solution)/shard_map/dot_general | solution.py:81
  99.6 0.5 fusion.12
  100.2 0.5 convolution_add_fusion
  100.7 0.4 fusion.11
  101.1 0.4 convolution_add_fusion.1
  102.5 16.4 %all_to_all.41 = f32[64,1,192]{2,1,0:T(1,128)S(1)} all-to-all(f32[64,1,192]{2,1,0:T(1,128)S(1)} %all_to_all.33), channel_id=1, replica_groups=mesh['zh'=8,'zl'=2,'yl'=2,'c'=2,'x'=4,'yh'=2] {'x','yh','zl','yl','c'}, dimensions={0} | all-to-all | bytes 98304 | tf_op jit(solution)/shard_map/all_to_all | solution.py:95
  119.0 24.9 %all_to_all.42 = f32[8,1,192]{2,1,0:T(1,128)S(1)} all-to-all(f32[8,1,192]{2,1,0:T(1,128)S(1)} %broadcast_in_dim.14), channel_id=1, replica_groups=mesh['zh'=8,'zl'=2,'yl'=2,'c'=2,'x'=4,'yh'=2] {'zh'}, dimensions={0} | all-to-all | bytes 12288 | tf_op jit(solution)/shard_map/all_to_all | solution.py:28
  143.9 8.3 %all_to_all.43 = f32[8,8,192]{2,1,0:T(8,128)S(1)} all-to-all(f32[8,8,192]{2,1,0:T(8,128)S(1)} %broadcast_in_dim.16), channel_id=1, replica_groups=mesh['zh'=8,'zl'=2,'yl'=2,'c'=2,'x'=4,'yh'=2] {'zl','yl','c'}, dimensions={0} | all-to-all | bytes 98304 | tf_op jit(solution)/shard_map/all_to_all | solution.py:28
  152.3 0.4 convolution_multiply_fusion
  152.7 9.7 %all_to_all.44 = f32[8,8,128]{2,1,0:T(8,128)S(1)} all-to-all(f32[8,8,128]{2,1,0:T(8,128)S(1)} %broadcast_in_dim.17), channel_id=1, replica_groups=mesh['zh'=8,'zl'=2,'yl'=2,'c'=2,'x'=4,'yh'=2] {'x','yh'}, dimensions={0} | all-to-all | bytes 65536 | tf_op jit(solution)/shard_map/all_to_all | solution.py:28
  162.4 0.6 reduce_sum.29
  (35 shorter events, 2.0 us)
Async XLA Ops:
  6.5 145.8 %copy-start = (bf16[128,1536]{1,0:T(8,128)(2,1)S(1)}, bf16[128,1536]{1,0:T(8,128)(2,1)}, u32[]{:S(2)}) copy-start(bf16[128,1536]{1,0:T(8,128)(2,1)} %param.20) | copy-start | bytes 1179652
  6.5 85.3 %all-gather.2.cloned.1.call-start = ((), (), s32[]{:S(2)}) async-start(), calls=%async_computation.7 | async-start | bytes 5947392 | tf_op jit(solution)/shard_map/all_gather | solution.py:50
  9.6 10.4 %copy-start.2 = (bf16[256,512]{1,0:T(8,128)(2,1)S(1)}, bf16[256,512]{1,0:T(8,128)(2,1)}, u32[]{:S(2)}) copy-start(bf16[256,512]{1,0:T(8,128)(2,1)} %param.12) | copy-start | bytes 786436
  9.7 12.9 %copy-start.5 = (s32[8]{0:T(128)S(1)}, s32[8]{0:T(128)}, u32[]{:S(2)}) copy-start(s32[8]{0:T(128)} %param.21) | copy-start | bytes 100
  11.6 20.4 %copy-start.3 = (bf16[256,1376]{0,1:T(8,128)(2,1)S(1)}, bf16[256,1376]{0,1:T(8,128)(2,1)}, u32[]{:S(2)}) copy-start(bf16[256,1376]{0,1:T(8,128)(2,1)} %param.14) | copy-start | bytes 2113540
  11.7 20.4 %copy-start.4 = (bf16[256,1376]{0,1:T(8,128)(2,1)S(1)}, bf16[256,1376]{0,1:T(8,128)(2,1)}, u32[]{:S(2)}) copy-start(bf16[256,1376]{0,1:T(8,128)(2,1)} %param.13) | copy-start | bytes 2113540
  12.5 14.8 %all-to-all-start = ((f32[8,32,256]{2,1,0:T(8,128)}), f32[8,32,256]{2,1,0:T(8,128)S(1)}, u32[]{:S(2)}, u32[]{:S(2)}) async-start(f32[8,32,256]{2,1,0:T(8,128)} %bitcast), calls=%async_computation | async-start | bytes 524288 | tf_op jit(solution)/shard_map/all_to_all | solution.py:72
  20.2 16.3 %collective-permute-start = (bf16[256,256]{0,1:T(8,128)(2,1)S(1)}, bf16[256,256]{0,1:T(8,128)(2,1)S(1)}, u32[]{:S(2)}, u32[]{:S(2)}) collective-permute-start(bf16[256,256]{0,1:T(8,128)(2,1)S(1)} %bitcast.33), channel_id=1, source_target_pairs={{0,16},{16,0},{1,17},{17,1},{2,18},{18,2},{3,19},{19,3},{4,20},{20... | collective-permute-start | bytes 393224 | tf_op jit(solution)/shard_map/ppermute | solution.py:56
  28.2 11.5 %all-to-all-start.1 = ((f32[16,32,128]{2,1,0:T(8,128)}), f32[16,32,128]{2,1,0:T(8,128)S(1)}, u32[]{:S(2)}, u32[]{:S(2)}) async-start(f32[16,32,128]{2,1,0:T(8,128)} %broadcast_in_dim.12), calls=%async_computation.1 | async-start | bytes 524288 | tf_op jit(solution)/shard_map/all_to_all | solution.py:28
  33.3 50.8 %collective-permute-start.1 = (bf16[512,1376]{0,1:T(8,128)(2,1)}, bf16[512,1376]{0,1:T(8,128)(2,1)}, u32[]{:S(2)}, u32[]{:S(2)}) collective-permute-start(bf16[512,1376]{0,1:T(8,128)(2,1)} %pad_maximum_fusion.1), channel_id=1, source_target_pairs={{0,16},{16,0},{1,17},{17,1},{2,18},{18,2},{3,19},{19,3},{4,20},{20... | collective-permute-start | bytes 4227080 | tf_op jit(solution)/shard_map/ppermute | solution.py:57
  41.1 49.9 %all-to-all-start.2 = ((bf16[8,512,256]{2,1,0:T(8,128)(2,1)}), bf16[8,512,256]{2,1,0:T(8,128)(2,1)S(1)}, u32[]{:S(2)}, u32[]{:S(2)}) async-start(bf16[8,512,256]{2,1,0:T(8,128)(2,1)} %broadcast_in_dim.13), calls=%async_computation.2 | async-start | bytes 4194304 | tf_op jit(solution)/shard_map/all_to_all | solution.py:28
  91.8 7.8 %copy-start.1 = (bf16[1376,128]{1,0:T(8,128)(2,1)S(1)}, bf16[1376,128]{1,0:T(8,128)(2,1)}, u32[]{:S(2)}) copy-start(bf16[1376,128]{1,0:T(8,128)(2,1)} %param.18) | copy-start | bytes 1056772
Sparse Core Ops, SparseCore 0:
  9.5 82.3 all-gather.1

commit v2 on v1

--- a/solution.py
+++ b/solution.py
@@ -1,16 +1,23 @@
+import functools
 import math
 
 import jax
 import jax.numpy as jnp
 from jax import lax
+from jax.experimental import pallas as pl
+from jax.experimental.pallas import tpu as pltpu
 from jax.sharding import Mesh
 from jax.sharding import PartitionSpec as P
 
 LEN = 2048
+TILE = 384
 DP = ("zh", "zl", "yl", "c")
 TENSOR = ("x", "yh")
+QUERY_GROUP = ("yl", "c")
+SHARE = TENSOR + QUERY_GROUP
 SWAP = [(0, 1), (1, 0)]
 HIGHEST = lax.Precision.HIGHEST
+VMEM = pl.BlockSpec(memory_space=pltpu.VMEM)
 
 
 def dot(a, b):
@@ -21,6 +28,108 @@
     high = a.astype(jnp.bfloat16)
     low = (a - high.astype(jnp.float32)).astype(jnp.bfloat16)
     return dot(high, b) + dot(low, b)
+
+
+def gradient_kernel(cot_ref, weight_ref, slope_ref, silu_ref, proj_ref, x_ref, down_ref, out_ref, held, part, rows_ref, sems):
+    pieces, events, depth = cot_ref.shape
+    hid = slope_ref.shape[1]
+    rank = down_ref.shape[0]
+    chunks = sems.shape[0]
+    span = pieces * depth // chunks
+    copies = [
+        pltpu.make_async_copy(weight_ref.at[pl.ds(i * span, span)], held.at[pl.ds(i * span, span)], sems.at[i])
+        for i in range(chunks)
+    ]
+    for copy in copies:
+        copy.start()
+    starts = list(range(0, hid, TILE))
+
+    def product(tile, which):
+        total = None
+        for i in which:
+            term = dot(cot_ref[i], held[pl.ds(i * depth, depth), tile])
+            total = term if total is None else total + term
+        return total
+
+    early = pieces // 2
+    for copy in copies[: chunks // 2]:
+        copy.wait()
+    for start in starts:
+        tile = slice(start, min(start + TILE, hid))
+        part[:, tile] = product(tile, range(early))
+    for copy in copies[chunks // 2 :]:
+        copy.wait()
+    gate_sum = up_sum = None
+    for start in starts:
+        tile = slice(start, min(start + TILE, hid))
+        grad = part[:, tile] + product(tile, range(early, pieces))
+        proj = proj_ref[tile, :]
+        gate_term = split_dot(grad * slope_ref[:, tile], proj)
+        up_term = split_dot(grad * silu_ref[:, tile], proj)
+        gate_sum = gate_term if gate_sum is None else gate_sum + gate_term
+        up_sum = up_term if up_sum is None else up_sum + up_term
+    lane = lax.broadcasted_iota(jnp.int32, gate_sum.shape, 1)
+    both = jnp.where(lane < rank, gate_sum, up_sum)
+    square = jnp.dot(x_ref[...], both, precision=HIGHEST, preferred_element_type=jnp.float32)
+    rows_ref[:rank, :rank] = square[:rank, :rank]
+    rows_ref[rank : 2 * rank, :rank] = square[rank:, rank:]
+    rows_ref[2 * rank :, :rank] = down_ref[...]
+    rows_ref[:, rank:] = jnp.zeros_like(rows_ref[:, rank:])
+    members = out_ref.shape[0]
+    each = rows_ref.shape[0] // members
+    for i in range(each):
+        row = rows_ref[pl.ds(i, members, stride=each), :]
+        out_ref[:, :, i * rank : (i + 1) * rank] = row[:, None, :rank]
+
+
+def gradient_blocks(cot, weight, slope, silu, proj, proj_x, block_d, members):
+    rank = block_d.shape[0]
+    return pl.pallas_call(
+        gradient_kernel,
+        out_shape=jax.ShapeDtypeStruct((members, 1, 3 * rank * rank // members), jnp.float32),
+        in_specs=[VMEM, pl.BlockSpec(memory_space=pltpu.HBM)] + [VMEM] * 5,
+        out_specs=VMEM,
+        scratch_shapes=[
+            pltpu.VMEM(weight.shape, jnp.bfloat16),
+            pltpu.VMEM(slope.shape, jnp.float32),
+            pltpu.VMEM((3 * rank, 2 * rank), jnp.float32),
+            pltpu.SemaphoreType.DMA((4,)),
+        ],
+        compiler_params=pltpu.CompilerParams(vmem_limit_bytes=40 * 2**20),
+        cost_estimate=pl.CostEstimate(
+            flops=2 * slope.shape[0] * weight.shape[0] * weight.shape[1],
+            bytes_accessed=weight.size * 2,
+            transcendentals=0,
+        ),
+        name="gradient_blocks",
+    )(cot, weight, slope, silu, proj, proj_x, block_d)
+
+
+def score_kernel(scale, rows_ref, query_ref, out_ref):
+    copies, sessions, width = out_ref.shape
+    groups = query_ref.shape[0] // width
+    grads = (rows_ref[:, 0] + rows_ref[:, 1]).reshape(sessions, -1)
+    scores = lax.dot_general(
+        grads,
+        query_ref[...].astype(jnp.float32),
+        (((1,), (1,)), ((), ())),
+        precision=HIGHEST,
+        preferred_element_type=jnp.float32,
+    )
+    scores = scores * scale
+    for i in range(copies):
+        first = i % groups * width
+        out_ref[i] = scores[:, first : first + width]
+
+
+def score_blocks(rows, query, copies, width, scale):
+    return pl.pallas_call(
+        functools.partial(score_kernel, scale),
+        out_shape=jax.ShapeDtypeStruct((copies, rows.shape[0], width), jnp.float32),
+        in_specs=[VMEM, VMEM],
+        out_specs=VMEM,
+        name="score_blocks",
+    )(rows, query)
 
 
 def give_all(block, axes):
@@ -65,6 +174,11 @@
     own_gate = gate_pre.astype(jnp.float32)
     hidden = (own_gate * jax.nn.sigmoid(own_gate) * up_pre.astype(jnp.float32)).astype(jnp.bfloat16)
 
+    groups = lax.axis_size(QUERY_GROUP)
+    own_queries = queries.reshape(queries.shape[0], groups, -1).transpose(1, 0, 2)
+    own_queries = lax.all_to_all(own_queries, QUERY_GROUP, 0, 0)
+    own_queries = own_queries.reshape(groups * queries.shape[0], -1)
+
     parts = jnp.concatenate(
         [dot(inputs, proj_in_x), dot(hidden, proj_in_h), dot(cotangent, proj_out_d)], axis=1
     )
@@ -78,30 +192,14 @@
     proj_x = give_all(sums_x, ("yl",) + TENSOR).reshape(2, rows, 2 * rank)
     proj_x = jnp.where(own_yl == 0, proj_x, proj_x[::-1]).reshape(2 * rows, 2 * rank)
 
-    grad_hidden = lax.dot_general(
-        full_cot,
-        weight.reshape(tensor_size, width // 2, hid),
-        (((0, 2), (0, 1)), ((), ())),
-        preferred_element_type=jnp.float32,
-    )
-    proj_gate = split_dot(grad_hidden * gate_slope, proj_out_ff[:, :rank])
-    proj_up = split_dot(grad_hidden * silu, proj_out_ff[:, rank:])
-    block_g = jnp.einsum("tr,ts->rs", proj_x[:, :rank], proj_gate, precision=HIGHEST)
-    block_u = jnp.einsum("tr,ts->rs", proj_x[:, rank:], proj_up, precision=HIGHEST)
-
-    blocks = jnp.concatenate([block_g, block_u, block_d], axis=0)
-    group = ("zl", "yl", "c")
-    members = tensor_size * lax.axis_size(group)
-    piece = lax.all_to_all(blocks.reshape(members, -1), TENSOR + group, 0, 0).sum(axis=0)
-    pieces = give_all(piece, ("zh",))
-    session_grads = give_all(pieces, group).transpose(1, 0, 2).reshape(pieces.shape[0], -1)
-    partial_scores = lax.dot_general(
-        session_grads,
-        queries.astype(jnp.float32),
-        (((1,), (1,)), ((), ())),
-        precision=HIGHEST,
-    ) * (1.0 / math.sqrt(LEN))
-    return give_all(partial_scores, TENSOR).sum(axis=0)
+    members = tensor_size * groups
+    blocks = gradient_blocks(full_cot, weight, gate_slope, silu, proj_out_ff, proj_x.T, block_d, members)
+
+    entries = lax.all_to_all(blocks, SHARE, 0, 0).sum(axis=0)
+    entries = give_all(entries, ("zh", "zl"))
+    entries = entries.reshape(-1, lax.axis_size("zl"), *entries.shape[1:])
+    partial_scores = score_blocks(entries, own_queries, members, queries.shape[0], 1.0 / math.sqrt(LEN))
+    return lax.all_to_all(partial_scores, SHARE, 0, 0).sum(axis=0)
 
 
 def solution(mesh):

time: 170 us -> 188 us (1.11)
  blocking collectives: 59.2 us -> 39.4 us
  matrix products: 15.4 us -> 1.24 us
  Pallas kernels: 0 us -> 13 us
  local copies, waits for them, and re-layouts: 6.78 us -> 17.9 us
  starting transfers between devices: 20.5 us -> 31.4 us
  other arithmetic: 2.82 us -> 12.1 us
  waiting for transfers between devices: 51.4 us -> 57.8 us
    ppermute x1, waiting for transfers between devices: 39 us -> 0.01 us  [on_device(): lax.ppermute(jnp.concatenate([gate_pre, up_pre], axis=0), 'yl', SWAP)]
    all_to_all x1, waiting for transfers between devices: 3.53 us -> 22.4 us  [on_device(): lax.all_to_all(parts.reshape(tensor_size, some, 4 * rank), TENSOR, 0, 0)]
    all_to_all x3 -> x1, blocking collectives: 42.8 us -> 25.8 us  [give_all(): lax.all_to_all(jnp.broadcast_to(block[None], (n,) + block.shape), axes, 0...]
    all_to_all x2, waiting for transfers between devices: 7.42 us -> 22.5 us  [give_all(): lax.all_to_all(jnp.broadcast_to(block[None], (n,) + block.shape), axes, 0...]
    pallas_call x0 -> x2, Pallas kernels: none -> 13 us  [the longest x1 10.6 us: gradient_blocks(): pl.pallas_call(gradient_kernel, out_shape=jax.ShapeDtypeStruct((members,...]
    all_to_all x0 -> x2, waiting for transfers between devices: none -> 12.2 us  [the longest x1 6.51 us: on_device(): own_queries = lax.all_to_all(own_queries, QUERY_GROUP, 0, 0)]
    unnamed x14 -> x29, local copies, waits for them, and re-layouts: 0.17 us -> 11.2 us
    all_to_all x0 -> x2, starting transfers between devices: none -> 10.2 us  [the longest x1 6.38 us: on_device(): entries = lax.all_to_all(blocks, SHARE, 0, 0).sum(axis=0)]
  transfers between devices with their start and end apart: 6 -> 8, of which waited for: 5 -> 5; matrix products, arithmetic and copies ran while one was open for 8% -> 13% of each run, Pallas kernels for 0% -> 0%
where the time goes in v2:
time: 188 us; the launch traced here: 187 us
  waiting for transfers between devices  57.8 us (31%)
  blocking collectives  39.4 us (21%)
  starting transfers between devices  31.4 us (17%)
  local copies, waits for them, and re-layouts  17.9 us (10%)
  between operations  13.7 us (7%)
  Pallas kernels  13 us (7%)
  other arithmetic  12.1 us (6%)
    all_to_all x1, blocking collectives, give_all(): lax.all_to_all(jnp.broadcast_to(block[None], (n,) + block.shape), axes, 0...  25.8 us
    all_to_all x2, waiting for transfers between devices, give_all(): lax.all_to_all(jnp.broadcast_to(block[None], (n,) + block.shape), axes, 0...  22.5 us
    all_to_all x1, waiting for transfers between devices, on_device(): lax.all_to_all(parts.reshape(tensor_size, some, 4 * rank), TENSOR, 0, 0)  22.4 us
    all_to_all x1, blocking collectives, on_device(): return lax.all_to_all(partial_scores, SHARE, 0, 0).sum(axis=0)  13.6 us
    unnamed x29, local copies, waits for them, and re-layouts  11.2 us
    pallas_call x1, Pallas kernels, gradient_blocks(): pl.pallas_call(gradient_kernel, out_shape=jax.ShapeDtypeStruct((members,...  10.6 us
    all_to_all x2, starting transfers between devices, give_all(): lax.all_to_all(jnp.broadcast_to(block[None], (n,) + block.shape), axes, 0...  8.9 us
    all_to_all x1, waiting for transfers between devices, on_device(): own_queries = lax.all_to_all(own_queries, QUERY_GROUP, 0, 0)  6.51 us
  transfers between devices with their start and end apart: 8, of which 5 were waited for; matrix products, arithmetic and copies ran while one was open for 13% of the time, Pallas kernels for 0%

profile of v2, /device:TPU:1, one launch (start us, length us, event | category | flops | bytes accessed | tf_op | source)
XLA Modules:
  0.0 186.5 jit_solution(11825153239768460739)
XLA Ops:
  7.3 2.6 %pad_maximum_fusion.1 = bf16[512,1376]{0,1:T(8,128)(2,1)} fusion(bf16[256,1376]{0,1:T(8,128)(2,1)} %param.14, bf16[256,1376]{0,1:T(8,128)(2,1)} %param.13), kind=kLoop, calls=%fused_computation.15 | loop fusion | flops 2818048 | bytes 2818048 | tf_op jit(solution)/shard_map/concatenate | solution.py:166
  9.9 4.0 %collective-permute-start.1 = (bf16[512,1376]{0,1:T(8,128)(2,1)}, bf16[512,1376]{0,1:T(8,128)(2,1)S(1)}, u32[]{:S(2)}, u32[]{:S(2)}) collective-permute-start(bf16[512,1376]{0,1:T(8,128)(2,1)} %pad_maximum_fusion.1), channel_id=1, source_target_pairs={{0,16},{16,0},{1,17},{17,1},{2,18},{18,2},{3,19},{19,3},{4,20},{20... | collective-permute-start | bytes 4227080 | tf_op jit(solution)/shard_map/ppermute | solution.py:166
  15.0 0.8 copy.40
  15.9 6.4 %all-to-all-start.1 = ((f32[8,32,256]{2,1,0:T(8,128)}), f32[8,32,256]{2,1,0:T(8,128)}, u32[]{:S(2)}, u32[]{:S(2)}) async-start(f32[8,32,256]{2,1,0:T(8,128)} %bitcast.4), calls=%async_computation.1 | async-start | bytes 524288 | tf_op jit(solution)/shard_map/all_to_all | solution.py:186
  22.2 1.1 copy.34
  24.0 1.9 %collective-permute-start = (bf16[256,256]{0,1:T(8,128)(2,1)}, bf16[256,256]{0,1:T(8,128)(2,1)S(1)}, u32[]{:S(2)}, u32[]{:S(2)}) collective-permute-start(bf16[256,256]{0,1:T(8,128)(2,1)} %bitcast.2), channel_id=1, source_target_pairs={{0,16},{16,0},{1,17},{17,1},{2,18},{18,2},{3,19},{19,3},{4,20},{20... | collective-permute-start | bytes 393224 | tf_op jit(solution)/shard_map/ppermute | solution.py:165
  27.2 22.4 %all-to-all-done.1 = f32[8,32,256]{2,1,0:T(8,128)} async-done(((f32[8,32,256]{2,1,0:T(8,128)}), f32[8,32,256]{2,1,0:T(8,128)}, u32[]{:S(2)}, u32[]{:S(2)}) %all-to-all-start.1) | async-done | bytes 262176 | tf_op jit(solution)/shard_map/all_to_all | solution.py:186
  49.6 1.0 reduce_sum.27
  51.4 4.5 %all-to-all-start.2 = ((f32[16,32,128]{2,1,0:T(8,128)}), f32[16,32,128]{2,1,0:T(8,128)}, u32[]{:S(2)}, u32[]{:S(2)}) async-start(f32[16,32,128]{2,1,0:T(8,128)} %broadcast_in_dim.7), calls=%async_computation.2 | async-start | bytes 524288 | tf_op jit(solution)/shard_map/all_to_all | solution.py:137
  56.7 1.1 copy.35
  57.7 6.0 %all-to-all-done.2 = f32[16,32,128]{2,1,0:T(8,128)} async-done(((f32[16,32,128]{2,1,0:T(8,128)}), f32[16,32,128]{2,1,0:T(8,128)}, u32[]{:S(2)}, u32[]{:S(2)}) %all-to-all-start.2) | async-done | bytes 262176 | tf_op jit(solution)/shard_map/all_to_all | solution.py:137
  63.7 1.5 broadcast_in_dim.6
  65.2 4.4 %all-to-all-start = ((bf16[8,512,256]{2,1,0:T(8,128)(2,1)}), bf16[8,512,256]{2,1,0:T(8,128)(2,1)}, u32[]{:S(2)}, u32[]{:S(2)}) async-start(bf16[8,512,256]{2,1,0:T(8,128)(2,1)} %broadcast_in_dim.6), calls=%async_computation | async-start | bytes 4194304 | tf_op jit(solution)/shard_map/all_to_all | solution.py:137
  69.6 1.1 copy.37
  70.8 1.2 copy.39
  72.2 1.1 reverse_select_fusion
  73.6 1.1 copy.44
  74.7 1.2 copy.45
  75.9 4.7 %convert_multiply_fusion = (f32[512,1376]{1,0:T(8,128)S(1)}, f32[512,1376]{1,0:T(8,128)}) fusion(bf16[256,1376]{1,0:T(8,128)(2,1)} %copy.45, bf16[256,1376]{1,0:T(8,128)(2,1)} %copy.39, bf16[256,1376]{1,0:T(8,128)(2,1)} %copy.44, bf16[256,1376]{1,0:T(8,128)(2,1)} %copy.37), kind=kLoop, calls=%fused_computation | loop fusion | flops 11976704 | bytes 8454144 | tf_op jit(solution)/shard_map/mul | solution.py:172
  80.5 16.5 %all-to-all-done.cot_ref = bf16[8,512,256]{2,1,0:T(8,128)(2,1)} async-done(((bf16[8,512,256]{2,1,0:T(8,128)(2,1)}), bf16[8,512,256]{2,1,0:T(8,128)(2,1)}, u32[]{:S(2)}, u32[]{:S(2)}) %all-to-all-start) | async-done | bytes 2097184 | tf_op jit(solution)/shard_map/all_to_all | solution.py:137
  97.0 1.8 copy-done.1
  98.8 2.6 %copy-done.2 = bf16[2048,1376]{1,0:T(8,128)(2,1)S(1)} copy-done((bf16[2048,1376]{1,0:T(8,128)(2,1)S(1)}, bf16[2048,1376]{1,0:T(8,128)(2,1)}, u32[]{:S(2)}) %copy-start.2) | copy-done | bytes 5636120
  101.5 1.0 copy-done.3
  102.4 10.6 %gradient_blocks.1 = f32[32,1,384]{2,1,0:T(1,128)} custom-call(bf16[8,512,256]{2,1,0:T(8,128)(2,1)} %all-to-all-done.cot_ref, bf16[2048,1376]{1,0:T(8,128)(2,1)S(1)} %copy-done.2, f32[512,1376]{1,0:T(8,128)S(1)} %copy-done.1, f32[512,1376]{1,0:T(8,128)S(1)} %get-tuple-element.5.silu_ref, bf16[1376,128]{1,0:T(8,128)(2,1)S(1)} %copy-done.3, ...), custom_call_target="tpu_custom_call" | custom-call | flops 2885681152 | bytes 5636096 | tf_op jit(solution)/shard_map/gradient_blocks/pallas_call | solution.py:87
  113.1 6.4 %all-to-all-start.3 = ((f32[32,1,384]{2,1,0:T(1,128)}), f32[32,1,384]{2,1,0:T(1,128)S(1)}, u32[]{:S(2)}, u32[]{:S(2)}) async-start(f32[32,1,384]{2,1,0:T(1,128)} %gradient_blocks.1), calls=%async_computation.3 | async-start | bytes 98304 | tf_op jit(solution)/shard_map/all_to_all | solution.py:198
  119.4 1.8 copy.48
  121.2 5.6 %all-to-all-done.3 = f32[32,1,384]{2,1,0:T(1,128)S(1)} async-done(((f32[32,1,384]{2,1,0:T(1,128)}), f32[32,1,384]{2,1,0:T(1,128)S(1)}, u32[]{:S(2)}, u32[]{:S(2)}) %all-to-all-start.3) | async-done | bytes 49184 | tf_op jit(solution)/shard_map/all_to_all | solution.py:198
  126.9 3.8 %all-to-all-start.5 = ((bf16[4,128,384]{2,1,0:T(8,128)(2,1)}), bf16[4,128,384]{2,1,0:T(8,128)(2,1)S(1)}, u32[]{:S(2)}, u32[]{:S(2)}) async-start(bf16[4,128,384]{2,1,0:T(8,128)(2,1)} %bitcast.22), calls=%async_computation.5 | async-start | bytes 786432 | tf_op jit(solution)/shard_map/all_to_all | solution.py:179
  130.8 6.5 %all-to-all-done.5 = bf16[4,128,384]{2,1,0:T(8,128)(2,1)S(1)} async-done(((bf16[4,128,384]{2,1,0:T(8,128)(2,1)}), bf16[4,128,384]{2,1,0:T(8,128)(2,1)S(1)}, u32[]{:S(2)}, u32[]{:S(2)}) %all-to-all-start.5) | async-done | bytes 393248 | tf_op jit(solution)/shard_map/all_to_all | solution.py:179
  137.3 25.8 %all_to_all.35 = f32[16,1,384]{2,1,0:T(1,128)} all-to-all(f32[16,1,384]{2,1,0:T(1,128)S(1)} %broadcast_in_dim.8), channel_id=1, replica_groups=mesh['zh'=8,'zl'=2,'yl'=2,'c'=2,'x'=4,'yh'=2] {'zh','zl'}, dimensions={0} | all-to-all | bytes 49152 | tf_op jit(solution)/shard_map/all_to_all | solution.py:137
  163.1 2.4 %score_blocks.1 = f32[32,8,128]{2,1,0:T(8,128)} custom-call(f32[8,2,1,384]{3,2,1,0:T(1,128)} %bitcast.30, bf16[512,384]{1,0:T(8,128)(2,1)} %bitcast.24), custom_call_target="tpu_custom_call" | custom-call | tf_op jit(solution)/shard_map/score_blocks/pallas_call | solution.py:126
  165.5 13.6 %all_to_all.36 = f32[32,8,128]{2,1,0:T(8,128)S(1)} all-to-all(f32[32,8,128]{2,1,0:T(8,128)} %score_blocks.1), channel_id=1, replica_groups=mesh['zh'=8,'zl'=2,'yl'=2,'c'=2,'x'=4,'yh'=2] {'x','yh','yl','c'}, dimensions={0} | all-to-all | bytes 262144 | tf_op jit(solution)/shard_map/all_to_all | solution.py:202
  (42 shorter events, 6.4 us)
Async XLA Ops:
  6.5 7.6 %copy-start = (bf16[256,512]{1,0:T(8,128)(2,1)S(1)}, bf16[256,512]{1,0:T(8,128)(2,1)}, u32[]{:S(2)}) copy-start(bf16[256,512]{1,0:T(8,128)(2,1)} %param.11) | copy-start | bytes 786436
  6.5 7.8 %copy-start.5 = (bf16[256,1376]{0,1:T(8,128)(2,1)S(1)}, bf16[256,1376]{0,1:T(8,128)(2,1)}, u32[]{:S(2)}) copy-start(bf16[256,1376]{0,1:T(8,128)(2,1)} %param.13) | copy-start | bytes 2113540
  6.5 7.8 %copy-start.4 = (bf16[256,1376]{0,1:T(8,128)(2,1)S(1)}, bf16[256,1376]{0,1:T(8,128)(2,1)}, u32[]{:S(2)}) copy-start(bf16[256,1376]{0,1:T(8,128)(2,1)} %param.14) | copy-start | bytes 2113540
  6.5 7.4 %copy-start.7 = (bf16[256,512]{1,0:T(8,128)(2,1)S(1)}, bf16[256,512]{1,0:T(8,128)(2,1)}, u32[]{:S(2)}) copy-start(bf16[256,512]{1,0:T(8,128)(2,1)} %param.12) | copy-start | bytes 786436
  6.5 7.6 %copy-start.8 = (bf16[512,128]{1,0:T(8,128)(2,1)S(1)}, bf16[512,128]{1,0:T(8,128)(2,1)}, u32[]{:S(2)}) copy-start(bf16[512,128]{1,0:T(8,128)(2,1)} %param.16) | copy-start | bytes 393220
  6.5 90.5 %all-gather.2.cloned.1.call-start = ((), (), s32[]{:S(2)}) async-start(), calls=%async_computation.7 | async-start | bytes 5947392 | tf_op jit(solution)/shard_map/all_gather | solution.py:159
  7.3 6.6 %copy-start.9 = (bf16[512,64]{0,1:T(8,128)(2,1)S(1)}, bf16[512,64]{0,1:T(8,128)(2,1)}, u32[]{:S(2)}) copy-start(bf16[512,64]{0,1:T(8,128)(2,1)} %param.19) | copy-start | bytes 196612
  7.3 7.1 %copy-start.10 = (bf16[1376,64]{0,1:T(8,128)(2,1)S(1)}, bf16[1376,64]{0,1:T(8,128)(2,1)}, u32[]{:S(2)}) copy-start(bf16[1376,64]{0,1:T(8,128)(2,1)} %param.17) | copy-start | bytes 528388
  9.9 63.6 %collective-permute-start.1 = (bf16[512,1376]{0,1:T(8,128)(2,1)}, bf16[512,1376]{0,1:T(8,128)(2,1)S(1)}, u32[]{:S(2)}, u32[]{:S(2)}) collective-permute-start(bf16[512,1376]{0,1:T(8,128)(2,1)} %pad_maximum_fusion.1), channel_id=1, source_target_pairs={{0,16},{16,0},{1,17},{17,1},{2,18},{18,2},{3,19},{19,3},{4,20},{20... | collective-permute-start | bytes 4227080 | tf_op jit(solution)/shard_map/ppermute | solution.py:166
  14.4 11.5 %copy-start.11 = (s32[8]{0:T(128)S(1)}, s32[8]{0:T(128)}, u32[]{:S(2)}) copy-start(s32[8]{0:T(128)} %param.21) | copy-start | bytes 100
  15.9 33.8 %all-to-all-start.1 = ((f32[8,32,256]{2,1,0:T(8,128)}), f32[8,32,256]{2,1,0:T(8,128)}, u32[]{:S(2)}, u32[]{:S(2)}) async-start(f32[8,32,256]{2,1,0:T(8,128)} %bitcast.4), calls=%async_computation.1 | async-start | bytes 524288 | tf_op jit(solution)/shard_map/all_to_all | solution.py:186
  24.0 32.0 %collective-permute-start = (bf16[256,256]{0,1:T(8,128)(2,1)}, bf16[256,256]{0,1:T(8,128)(2,1)S(1)}, u32[]{:S(2)}, u32[]{:S(2)}) collective-permute-start(bf16[256,256]{0,1:T(8,128)(2,1)} %bitcast.2), channel_id=1, source_target_pairs={{0,16},{16,0},{1,17},{17,1},{2,18},{18,2},{3,19},{19,3},{4,20},{20... | collective-permute-start | bytes 393224 | tf_op jit(solution)/shard_map/ppermute | solution.py:165
  51.4 12.4 %all-to-all-start.2 = ((f32[16,32,128]{2,1,0:T(8,128)}), f32[16,32,128]{2,1,0:T(8,128)}, u32[]{:S(2)}, u32[]{:S(2)}) async-start(f32[16,32,128]{2,1,0:T(8,128)} %broadcast_in_dim.7), calls=%async_computation.2 | async-start | bytes 524288 | tf_op jit(solution)/shard_map/all_to_all | solution.py:137
  65.2 31.8 %all-to-all-start = ((bf16[8,512,256]{2,1,0:T(8,128)(2,1)}), bf16[8,512,256]{2,1,0:T(8,128)(2,1)}, u32[]{:S(2)}, u32[]{:S(2)}) async-start(bf16[8,512,256]{2,1,0:T(8,128)(2,1)} %broadcast_in_dim.6), calls=%async_computation | async-start | bytes 4194304 | tf_op jit(solution)/shard_map/all_to_all | solution.py:137
  97.0 1.8 copy-start.1
  98.8 2.6 %copy-start.2 = (bf16[2048,1376]{1,0:T(8,128)(2,1)S(1)}, bf16[2048,1376]{1,0:T(8,128)(2,1)}, u32[]{:S(2)}) copy-start(bf16[2048,1376]{1,0:T(8,128)(2,1)} %all-gather.2.cloned.1.call-done.weight_ref) | copy-start | bytes 16908292
  101.5 1.0 copy-start.3
  113.1 13.8 %all-to-all-start.3 = ((f32[32,1,384]{2,1,0:T(1,128)}), f32[32,1,384]{2,1,0:T(1,128)S(1)}, u32[]{:S(2)}, u32[]{:S(2)}) async-start(f32[32,1,384]{2,1,0:T(1,128)} %gradient_blocks.1), calls=%async_computation.3 | async-start | bytes 98304 | tf_op jit(solution)/shard_map/all_to_all | solution.py:198
  126.9 10.4 %all-to-all-start.5 = ((bf16[4,128,384]{2,1,0:T(8,128)(2,1)}), bf16[4,128,384]{2,1,0:T(8,128)(2,1)S(1)}, u32[]{:S(2)}, u32[]{:S(2)}) async-start(bf16[4,128,384]{2,1,0:T(8,128)(2,1)} %bitcast.22), calls=%async_computation.5 | async-start | bytes 786432 | tf_op jit(solution)/shard_map/all_to_all | solution.py:179
  137.3 25.8 %copy-start.6 = (bf16[4,128,384]{2,1,0:T(8,128)(2,1)}, bf16[4,128,384]{2,1,0:T(8,128)(2,1)S(1)}, u32[]{:S(2)}) copy-start(bf16[4,128,384]{2,1,0:T(8,128)(2,1)S(1)} %all-to-all-done.5) | copy-start | bytes 1179652
Sparse Core Ops, SparseCore 0:
  9.5 81.9 all-gather.1

commit v3 on v2

v3 whole, which is shorter than its diff:
```python
import functools
import math

import jax
import jax.numpy as jnp
from jax import lax
from jax.experimental import pallas as pl
from jax.experimental.pallas import tpu as pltpu
from jax.sharding import Mesh
from jax.sharding import PartitionSpec as P

LEN = 2048
TILE = 512
DP = ("zh", "zl", "yl", "c")
TENSOR = ("x", "yh")
QUERY_GROUP = ("yl", "c")
SHARE = TENSOR + QUERY_GROUP
SWAP = [(0, 1), (1, 0)]
HIGHEST = lax.Precision.HIGHEST
VMEM = pl.BlockSpec(memory_space=pltpu.VMEM)


def dot(a, b):
    return jnp.dot(a, b, preferred_element_type=jnp.float32)


def gradient_kernel(
    cot_ref, weight_ref, slope_ref, silu_ref, proj_ref, x_ref, down_ref, _, out_ref, held, part, rows_ref, sems
):
    hid = slope_ref.shape[1]
    rank = down_ref.shape[0]
    chunks = sems.shape[0]
    depth = weight_ref.shape[0]
    span = depth // chunks
    copies = [
        pltpu.make_async_copy(weight_ref.at[pl.ds(i * span, span)], held.at[pl.ds(i * span, span)], sems.at[i])
        for i in range(chunks)
    ]
    for copy in copies:
        copy.start()
    tiles = [slice(start, min(start + TILE, hid)) for start in range(0, hid, TILE)]
    half = depth // 2
    for copy in copies[: chunks // 2]:
        copy.wait()
    for tile in tiles:
        part[:, tile] = dot(cot_ref[:, :half], held[:half, tile])
    for copy in copies[chunks // 2 :]:
        copy.wait()
    gate_sum = up_sum = None
    for tile in tiles:
        grad = part[:, tile] + dot(cot_ref[:, half:], held[half:, tile])
        proj = proj_ref[tile, :]
        gate_term = dot((grad * slope_ref[:, tile].astype(jnp.float32)).astype(jnp.bfloat16), proj)
        up_term = dot((grad * silu_ref[:, tile].astype(jnp.float32)).astype(jnp.bfloat16), proj)
        gate_sum = gate_term if gate_sum is None else gate_sum + gate_term
        up_sum = up_term if up_sum is None else up_sum + up_term
    lane = lax.broadcasted_iota(jnp.int32, gate_sum.shape, 1)
    both = jnp.where(lane < rank, gate_sum, up_sum)
    square = jnp.dot(x_ref[...], both, precision=HIGHEST, preferred_element_type=jnp.float32)
    rows_ref[:rank, :rank] = square[:rank, :rank]
    rows_ref[rank : 2 * rank, :rank] = square[rank:, rank:]
    rows_ref[2 * rank :, :rank] = down_ref[...]
    rows_ref[:, rank:] = jnp.zeros_like(rows_ref[:, rank:])
    members = out_ref.shape[0]
    each = rows_ref.shape[0] // members
    for i in range(each):
        row = rows_ref[pl.ds(i, members, stride=each), :]
        out_ref[:, :, i * rank : (i + 1) * rank] = row[:, None, :rank]


def gradient_blocks(cot, weight, slope, silu, proj, proj_x, block_d, queries, members):
    rank = block_d.shape[0]
    anywhere = pl.BlockSpec(memory_space=pl.ANY)
    return pl.pallas_call(
        gradient_kernel,
        out_shape=jax.ShapeDtypeStruct((members, 1, 3 * rank * rank // members), jnp.float32),
        in_specs=[VMEM, anywhere] + [VMEM] * 5 + [anywhere],
        out_specs=VMEM,
        scratch_shapes=[
            pltpu.VMEM(weight.shape, jnp.bfloat16),
            pltpu.VMEM(slope.shape, jnp.float32),
            pltpu.VMEM((3 * rank, 2 * rank), jnp.float32),
            pltpu.SemaphoreType.DMA((4,)),
        ],
        compiler_params=pltpu.CompilerParams(vmem_limit_bytes=54 * 2**20),
        cost_estimate=pl.CostEstimate(
            flops=2 * slope.shape[0] * weight.shape[0] * weight.shape[1],
            bytes_accessed=weight.size * 2,
            transcendentals=0,
        ),
        name="gradient_blocks",
    )(cot, weight, slope, silu, proj, proj_x, block_d, queries)


def score_kernel(scale, rows_ref, query_ref, out_ref):
    copies, sessions, width = out_ref.shape
    groups = query_ref.shape[1] // width
    left = (rows_ref[:, 0] + rows_ref[:, 1]).reshape(sessions, -1)
    terms = []
    for _ in range(3):
        terms.append(left.astype(jnp.bfloat16).astype(jnp.float32))
        left = left - terms[-1]
    products = dot(jnp.concatenate(terms, axis=0).astype(jnp.bfloat16), query_ref[...])
    scores = products[:sessions] + (products[sessions : 2 * sessions] + products[2 * sessions :])
    scores = scores * scale
    for i in range(copies):
        first = i % groups * width
        out_ref[i] = scores[:, first : first + width]


def score_blocks(rows, query, copies, width, scale):
    return pl.pallas_call(
        functools.partial(score_kernel, scale),
        out_shape=jax.ShapeDtypeStruct((copies, rows.shape[0], width), jnp.float32),
        in_specs=[VMEM, VMEM],
        out_specs=VMEM,
        name="score_blocks",
    )(rows, query)


def give_all(block, axes):
    n = lax.axis_size(axes)
    return lax.all_to_all(jnp.broadcast_to(block[None], (n,) + block.shape), axes, 0, 0)


def on_device(
    inputs,
    cotangent,
    gate_pre,
    up_pre,
    down_weight,
    proj_in_x,
    proj_in_h,
    proj_out_ff,
    proj_out_d,
    queries,
    lengths,
):
    rows, width = cotangent.shape
    hid = gate_pre.shape[1]
    rank = proj_in_h.shape[1]
    own_yl = lax.axis_index("yl")
    tensor_size = lax.axis_size(TENSOR)

    weight = lax.all_gather(down_weight.T, ("zh", "zl", "c"), axis=0, tiled=True)

    per_half = cotangent.reshape(rows, -1, 2, 2 * down_weight.shape[1]).transpose(2, 0, 1, 3)
    per_half = per_half.reshape(2, 1, rows, width // 2)
    pieces = jnp.broadcast_to(per_half, (2, tensor_size, rows, width // 2))
    full_cot = lax.all_to_all(pieces.reshape(-1, rows, width // 2), ("yl",) + TENSOR, 0, 0)
    full_cot = full_cot.reshape(2, tensor_size, rows, width // 2).transpose(0, 2, 1, 3)
    full_cot = full_cot.reshape(2 * rows, -1)

    partner_pre = lax.ppermute(jnp.concatenate([gate_pre, up_pre], axis=0), "yl", SWAP)

    def in_order(own, partner):
        swapped = own_yl == 1
        return jnp.concatenate([jnp.where(swapped, partner, own), jnp.where(swapped, own, partner)], axis=0)

    gate_float = in_order(gate_pre, partner_pre[:rows]).astype(jnp.float32)
    up_float = in_order(up_pre, partner_pre[rows:]).astype(jnp.float32)
    sig = jax.nn.sigmoid(gate_float)
    silu = (gate_float * sig).astype(jnp.bfloat16)
    gate_slope = (up_float * sig * (1.0 + gate_float * (1.0 - sig))).astype(jnp.bfloat16)
    own_gate = gate_pre.astype(jnp.float32)
    hidden = (own_gate * jax.nn.sigmoid(own_gate) * up_pre.astype(jnp.float32)).astype(jnp.bfloat16)

    groups = lax.axis_size(QUERY_GROUP)
    member = lax.axis_index(QUERY_GROUP)
    quarters = queries.reshape(queries.shape[0], groups, -1).transpose(1, 0, 2)
    arrivals = []
    for flip in range(groups):
        piece = lax.dynamic_index_in_dim(quarters, member ^ flip, 0, keepdims=False)
        pairs = [(i, i ^ flip) for i in range(groups)]
        arrivals.append(lax.ppermute(piece, QUERY_GROUP, pairs) if flip else piece)
    for bit in (1, 2):
        arrivals = [jnp.where(member & bit, arrivals[i ^ bit], arrivals[i]) for i in range(groups)]
    own_queries = jnp.concatenate(arrivals, axis=0).T

    parts = jnp.concatenate(
        [dot(inputs, proj_in_x), dot(hidden, proj_in_h), dot(cotangent, proj_out_d)], axis=1
    )
    parts, full_cot = lax.optimization_barrier((parts, full_cot))
    some = rows // tensor_size
    sums = lax.all_to_all(parts.reshape(tensor_size, some, 4 * rank), TENSOR, 0, 0).sum(axis=0)
    first_event = lax.axis_index(DP) * rows + lax.axis_index(TENSOR) * some
    positions = first_event % LEN + jnp.arange(some, dtype=jnp.int32)
    live = (positions < lengths[first_event // LEN]).astype(jnp.float32)[:, None]
    sums_x, sums_h, sums_d = sums[:, : 2 * rank] * live, sums[:, 2 * rank : 3 * rank], sums[:, 3 * rank :]
    block_d = jnp.einsum("tr,ts->rs", sums_h, sums_d * live, precision=HIGHEST)
    proj_x = give_all(sums_x, ("yl",) + TENSOR).reshape(2 * rows, 2 * rank)

    members = tensor_size * groups
    blocks = gradient_blocks(
        full_cot, weight, gate_slope, silu, proj_out_ff, proj_x.T, block_d, own_queries, members
    )

    entries = lax.all_to_all(blocks, SHARE, 0, 0).sum(axis=0)
    entries = give_all(entries, ("zh", "zl"))
    entries = entries.reshape(-1, lax.axis_size("zl"), *entries.shape[1:])
    partial_scores = score_blocks(entries, own_queries, members, queries.shape[0], 1.0 / math.sqrt(LEN))
    return lax.all_to_all(partial_scores, SHARE, 0, 0).sum(axis=0)


def solution(mesh):
    fine = Mesh(mesh.devices.reshape(8, 2, 2, 2, 4, 2), DP + TENSOR)
    return jax.shard_map(
        on_device,
        mesh=fine,
        in_specs=(
            P(DP, TENSOR),
            P(DP, TENSOR),
            P(DP, TENSOR),
            P(DP, TENSOR),
            P(TENSOR, DP),
            P(TENSOR, None),
            P(TENSOR, None),
            P(TENSOR, None),
            P(TENSOR, None),
            P(DP, TENSOR),
            P(),
        ),
        out_specs=P(None, DP),
        check_vma=False,
    )
```

time: 188 us -> 199 us (1.059)
  waiting for transfers between devices: 57.8 us -> 37.5 us
  blocking collectives: 39.4 us -> 57.9 us
  starting transfers between devices: 31.4 us -> 35.7 us
  local copies, waits for them, and re-layouts: 17.9 us -> 21.9 us
  matrix products: 1.24 us -> 5.1 us
    ppermute x1 -> x3, waiting for transfers between devices: 0.01 us -> 30.5 us  [on_device(): arrivals.append(lax.ppermute(piece, QUERY_GROUP, pairs) if flip else piece)]
    all_to_all x2 -> x1, waiting for transfers between devices: 22.5 us -> 1.8 us  [give_all(): lax.all_to_all(jnp.broadcast_to(block[None], (n,) + block.shape), axes, 0...]
    all_to_all x1, waiting for transfers between devices: 22.4 us -> 4.53 us  [on_device(): lax.all_to_all(parts.reshape(tensor_size, some, 4 * rank), TENSOR, 0, 0)]
    all_to_all x0 -> x1, blocking collectives: none -> 15.4 us  [on_device(): entries = lax.all_to_all(blocks, SHARE, 0, 0).sum(axis=0)]
    all_to_all x2 -> x1, waiting for transfers between devices: 12.2 us -> 0.01 us  [on_device(): lax.all_to_all(pieces.reshape(-1, rows, width // 2), ('yl',) + TENSOR, 0, 0)]
    ppermute x1 -> x3, starting transfers between devices: 1.91 us -> 10.6 us  [on_device(): arrivals.append(lax.ppermute(piece, QUERY_GROUP, pairs) if flip else piece)]
    all_to_all x2 -> x1, starting transfers between devices: 8.9 us -> 3.71 us  [give_all(): lax.all_to_all(jnp.broadcast_to(block[None], (n,) + block.shape), axes, 0...]
    convert_element_type x0 -> x1, other arithmetic: none -> 4.75 us  [on_device(): silu = (gate_float * sig).astype(jnp.bfloat16)]
  transfers between devices with their start and end apart: 8 -> 8, of which waited for: 5 -> 3; matrix products, arithmetic and copies ran while one was open for 13% -> 20% of each run, Pallas kernels for 0% -> 0%
where the time goes in v3:
time: 199 us; the launch traced here: 197 us
  blocking collectives  57.9 us (29%)
  waiting for transfers between devices  37.5 us (19%)
  starting transfers between devices  35.7 us (18%)
  local copies, waits for them, and re-layouts  21.9 us (11%)
  other arithmetic  13.8 us (7%)
  between operations  13.7 us (7%)
  Pallas kernels  11.9 us (6%)
  matrix products  5.1 us (3%)
    ppermute x3, waiting for transfers between devices, on_device(): arrivals.append(lax.ppermute(piece, QUERY_GROUP, pairs) if flip else piece)  30.5 us
    all_to_all x1, blocking collectives, give_all(): lax.all_to_all(jnp.broadcast_to(block[None], (n,) + block.shape), axes, 0...  29.4 us
    all_to_all x1, blocking collectives, on_device(): entries = lax.all_to_all(blocks, SHARE, 0, 0).sum(axis=0)  15.4 us
    all_to_all x1, blocking collectives, on_device(): return lax.all_to_all(partial_scores, SHARE, 0, 0).sum(axis=0)  13.1 us
    unnamed x20, local copies, waits for them, and re-layouts  11.4 us
    ppermute x3, starting transfers between devices, on_device(): arrivals.append(lax.ppermute(piece, QUERY_GROUP, pairs) if flip else piece)  10.6 us
    all_to_all x1, starting transfers between devices, on_device(): lax.all_to_all(parts.reshape(tensor_size, some, 4 * rank), TENSOR, 0, 0)  10.4 us
    pallas_call x1, Pallas kernels, gradient_blocks(): pl.pallas_call(gradient_kernel, out_shape=jax.ShapeDtypeStruct((members,...  10 us
  transfers between devices with their start and end apart: 8, of which 3 were waited for; matrix products, arithmetic and copies ran while one was open for 20% of the time, Pallas kernels for 0%

profile of v3, /device:TPU:1, one launch (start us, length us, event | category | flops | bytes accessed | tf_op | source)
XLA Modules:
  0.0 197.4 jit_solution(4212049550447680273)
XLA Ops:
  7.3 1.1 copy.52
  8.5 1.6 broadcast_in_dim.9
  10.1 7.7 %all-to-all-start = ((bf16[16,256,256]{2,1,0:T(8,128)(2,1)}), bf16[16,256,256]{2,1,0:T(8,128)(2,1)S(1)}, u32[]{:S(2)}, u32[]{:S(2)}) async-start(bf16[16,256,256]{2,1,0:T(8,128)(2,1)} %bitcast.44), calls=%async_computation | async-start | bytes 4194304 | tf_op jit(solution)/shard_map/all_to_all | solution.py:150
  17.8 2.3 %pad_maximum_fusion.1 = bf16[512,1376]{0,1:T(8,128)(2,1)} fusion(bf16[256,1376]{0,1:T(8,128)(2,1)S(1)} %copy-done.3, bf16[256,1376]{0,1:T(8,128)(2,1)} %param.13), kind=kLoop, calls=%fused_computation.17 | loop fusion | flops 2818048 | bytes 2818048 | tf_op jit(solution)/shard_map/concatenate | solution.py:154
  20.1 3.3 %collective-permute-start = (bf16[512,1376]{0,1:T(8,128)(2,1)}, bf16[512,1376]{0,1:T(8,128)(2,1)}, u32[]{:S(2)}, u32[]{:S(2)}) collective-permute-start(bf16[512,1376]{0,1:T(8,128)(2,1)} %pad_maximum_fusion.1), channel_id=1, source_target_pairs={{0,16},{16,0},{1,17},{17,1},{2,18},{18,2},{3,19},{19,3},{4,20},{20... | collective-permute-start | bytes 4227080 | tf_op jit(solution)/shard_map/ppermute | solution.py:154
  23.4 1.2 copy.68
  25.4 5.2 %collective-permute-start.1 = (bf16[128,384]{0,1:T(8,128)(2,1)}, bf16[128,384]{0,1:T(8,128)(2,1)}, u32[]{:S(2)}, u32[]{:S(2)}) collective-permute-start(bf16[128,384]{0,1:T(8,128)(2,1)} %get-tuple-element.23), channel_id=1, source_target_pairs={{0,24},{8,16},{16,8},{24,0},{1,25},{9,17},{17,9},{25,1},{2,26},{10... | collective-permute-start | bytes 294920 | tf_op jit(solution)/shard_map/ppermute | solution.py:175
  30.6 3.5 %collective-permute-start.2 = (bf16[128,384]{0,1:T(8,128)(2,1)}, bf16[128,384]{0,1:T(8,128)(2,1)}, u32[]{:S(2)}, u32[]{:S(2)}) collective-permute-start(bf16[128,384]{0,1:T(8,128)(2,1)} %get-tuple-element.22), channel_id=1, source_target_pairs={{0,16},{8,24},{16,0},{24,8},{1,17},{9,25},{17,1},{25,9},{2,18},{10... | collective-permute-start | bytes 294920 | tf_op jit(solution)/shard_map/ppermute | solution.py:175
  34.1 1.9 collective-permute-start.3
  36.1 1.4 copy.57
  37.5 2.3 %copy.60 = bf16[256,1376]{1,0:T(8,128)(2,1)} copy(bf16[256,1376]{0,1:T(8,128)(2,1)} %param.13) | data formatting | bytes 1409024 | tf_op args[2]
  40.4 1.2 fusion.20
  41.6 1.1 fusion.19
  42.7 2.0 fusion.12
  46.1 30.5 %collective-permute-done.1 = bf16[128,384]{0,1:T(8,128)(2,1)} collective-permute-done((bf16[128,384]{0,1:T(8,128)(2,1)}, bf16[128,384]{0,1:T(8,128)(2,1)}, u32[]{:S(2)}, u32[]{:S(2)}) %collective-permute-start.1) | collective-permute-done | bytes 98336 | tf_op jit(solution)/shard_map/ppermute | solution.py:175
  76.6 1.0 broadcast_select_fusion.9
  78.4 2.6 %fusion.18 = (bf16[256,1376]{0,1:T(8,128)(2,1)}, bf16[256,1376]{0,1:T(8,128)(2,1)}) fusion(bf16[512,1376]{0,1:T(8,128)(2,1)} %collective-permute-done), kind=kLoop, calls=%fused_computation.44 | loop fusion | bytes 2818048 | tf_op jit(solution)/shard_map/slice | solution.py:160
  80.9 2.2 %copy.69 = bf16[256,1376]{1,0:T(8,128)(2,1)} copy(bf16[256,1376]{0,1:T(8,128)(2,1)} %get-tuple-element.16) | data formatting | bytes 1409024
  83.2 2.2 %copy.70 = bf16[256,1376]{1,0:T(8,128)(2,1)} copy(bf16[256,1376]{0,1:T(8,128)(2,1)} %get-tuple-element.15) | data formatting | bytes 1409024
  85.4 1.2 copy.55
  86.6 2.0 %copy.71 = bf16[64,8,8,256]{3,1,2,0:T(8,128)(2,1)} copy(bf16[64,8,8,256]{3,2,1,0:T(8,128)(2,1)S(1)} %bitcast.45) | data formatting | bytes 4194304
  89.5 10.4 %all-to-all-start.1 = ((f32[8,32,256]{2,1,0:T(8,128)}), f32[8,32,256]{2,1,0:T(8,128)S(1)}, u32[]{:S(2)}, u32[]{:S(2)}) async-start(f32[8,32,256]{2,1,0:T(8,128)} %bitcast.7), calls=%async_computation.1 | async-start | bytes 524288 | tf_op jit(solution)/shard_map/all_to_all | solution.py:185
  100.0 2.8 %broadcast_select_fusion.1 = (bf16[256,1376]{1,0:T(8,128)(2,1)}, bf16[256,1376]{1,0:T(8,128)(2,1)}, bf16[256,1376]{1,0:T(8,128)(2,1)}, bf16[256,1376]{1,0:T(8,128)(2,1)}) fusion(bf16[256,1376]{1,0:T(8,128)(2,1)} %copy.70, bf16[256,1376]{1,0:T(8,128)(2,1)S(1)} %copy-done.1, pred[]{:T(512)S(6)} %eq.6, bf16[256,1376]{1,0:T(8,128)(2,1)S(1)} %copy.57, ...), kind=kLoop, calls=%fused_computation.20 | loop fusion | flops 1409024 | bytes 5636097 | tf_op jit(solution)/shard_map/jit(_where)/select_n | solution.py:158
  102.7 4.5 %all-to-all-done.1 = f32[8,32,256]{2,1,0:T(8,128)S(1)} async-done(((f32[8,32,256]{2,1,0:T(8,128)}), f32[8,32,256]{2,1,0:T(8,128)S(1)}, u32[]{:S(2)}, u32[]{:S(2)}) %all-to-all-start.1) | async-done | bytes 262176 | tf_op jit(solution)/shard_map/all_to_all | solution.py:185
  108.1 3.7 %all-to-all-start.2 = ((f32[16,32,128]{2,1,0:T(8,128)}), f32[16,32,128]{2,1,0:T(8,128)S(1)}, u32[]{:S(2)}, u32[]{:S(2)}) async-start(f32[16,32,128]{2,1,0:T(8,128)} %broadcast_in_dim.10), calls=%async_computation.2 | async-start | bytes 524288 | tf_op jit(solution)/shard_map/all_to_all | solution.py:123
  111.8 4.7 %fusion.6 = (bf16[512,1376]{1,0:T(8,128)(2,1)}, bf16[512,1376]{1,0:T(8,128)(2,1)}) fusion(bf16[256,1376]{1,0:T(8,128)(2,1)} %get-tuple-element.12, bf16[256,1376]{1,0:T(8,128)(2,1)} %get-tuple-element.11, bf16[256,1376]{1,0:T(8,128)(2,1)} %get-tuple-element.24, bf16[256,1376]{1,0:T(8,128)(2,1)} %get-tuple-element.25), kind=kLoop, calls=%fused_computation.9 | loop fusion | flops 13385728 | bytes 5636096 | tf_op jit(solution)/shard_map/convert_element_type | solution.py:163
  117.4 1.8 all-to-all-done.2
  120.1 10.0 %gradient_blocks.1 = f32[32,1,384]{2,1,0:T(1,128)} custom-call(bf16[512,2048]{1,0:T(8,128)(2,1)} %bitcast.42, bf16[2048,1376]{1,0:T(8,128)(2,1)} %all-gather.2.cloned.1.call-done.weight_ref, bf16[512,1376]{1,0:T(8,128)(2,1)} %get-tuple-element.10.slope_ref, bf16[512,1376]{1,0:T(8,128)(2,1)} %get-tuple-element.9.silu_ref, bf16[1376,128]{1,0:T(8,128)(2,1)} %proj_ref.1, ...), custom_call_target="tpu_custom_call" | custom-call | flops 2885681152 | bytes 5636096 | tf_op jit(solution)/shard_map/gradient_blocks/pallas_call | solution.py:74
  130.1 15.4 %all_to_all.30 = f32[32,1,384]{2,1,0:T(1,128)S(1)} all-to-all(f32[32,1,384]{2,1,0:T(1,128)} %gradient_blocks.1), channel_id=1, replica_groups=mesh['zh'=8,'zl'=2,'yl'=2,'c'=2,'x'=4,'yh'=2] {'x','yh','yl','c'}, dimensions={0} | all-to-all | bytes 98304 | tf_op jit(solution)/shard_map/all_to_all | solution.py:198
  145.6 29.4 %all_to_all.31 = f32[16,1,384]{2,1,0:T(1,128)} all-to-all(f32[16,1,384]{2,1,0:T(1,128)S(1)} %broadcast_in_dim.11), channel_id=1, replica_groups=mesh['zh'=8,'zl'=2,'yl'=2,'c'=2,'x'=4,'yh'=2] {'zh','zl'}, dimensions={0} | all-to-all | bytes 49152 | tf_op jit(solution)/shard_map/all_to_all | solution.py:123
  174.9 1.9 score_blocks.1
  176.8 13.1 %all_to_all.32 = f32[32,8,128]{2,1,0:T(8,128)S(1)} all-to-all(f32[32,8,128]{2,1,0:T(8,128)} %score_blocks.1), channel_id=1, replica_groups=mesh['zh'=8,'zl'=2,'yl'=2,'c'=2,'x'=4,'yh'=2] {'x','yh','yl','c'}, dimensions={0} | all-to-all | bytes 262144 | tf_op jit(solution)/shard_map/all_to_all | solution.py:202
  (37 shorter events, 8.5 us)
Async XLA Ops:
  6.5 35.0 %copy-start = (bf16[256,512]{1,0:T(8,128)(2,1)S(1)}, bf16[256,512]{1,0:T(8,128)(2,1)}, u32[]{:S(2)}) copy-start(bf16[256,512]{1,0:T(8,128)(2,1)} %param.11) | copy-start | bytes 786436
  6.5 113.6 %all-gather.2.cloned.1.call-start = ((), (), s32[]{:S(2)}) async-start(), calls=%async_computation.6 | async-start | bytes 5947392 | tf_op jit(solution)/shard_map/all_gather | solution.py:145
  10.1 7.7 %copy-start.3 = (bf16[256,1376]{0,1:T(8,128)(2,1)S(1)}, bf16[256,1376]{0,1:T(8,128)(2,1)}, u32[]{:S(2)}) copy-start(bf16[256,1376]{0,1:T(8,128)(2,1)} %param.14) | copy-start | bytes 2113540
  10.1 75.4 %all-to-all-start = ((bf16[16,256,256]{2,1,0:T(8,128)(2,1)}), bf16[16,256,256]{2,1,0:T(8,128)(2,1)S(1)}, u32[]{:S(2)}, u32[]{:S(2)}) async-start(bf16[16,256,256]{2,1,0:T(8,128)(2,1)} %bitcast.44), calls=%async_computation | async-start | bytes 4194304 | tf_op jit(solution)/shard_map/all_to_all | solution.py:150
  20.1 58.3 %collective-permute-start = (bf16[512,1376]{0,1:T(8,128)(2,1)}, bf16[512,1376]{0,1:T(8,128)(2,1)}, u32[]{:S(2)}, u32[]{:S(2)}) collective-permute-start(bf16[512,1376]{0,1:T(8,128)(2,1)} %pad_maximum_fusion.1), channel_id=1, source_target_pairs={{0,16},{16,0},{1,17},{17,1},{2,18},{18,2},{3,19},{19,3},{4,20},{20... | collective-permute-start | bytes 4227080 | tf_op jit(solution)/shard_map/ppermute | solution.py:154
  23.4 16.4 %copy-start.6 = (s32[8]{0:T(128)S(1)}, s32[8]{0:T(128)}, u32[]{:S(2)}) copy-start(s32[8]{0:T(128)} %param.21) | copy-start | bytes 100
  23.4 17.0 %copy-start.5 = (bf16[512,64]{0,1:T(8,128)(2,1)S(1)}, bf16[512,64]{0,1:T(8,128)(2,1)}, u32[]{:S(2)}) copy-start(bf16[512,64]{0,1:T(8,128)(2,1)} %param.19) | copy-start | bytes 196612
  25.4 51.1 %collective-permute-start.1 = (bf16[128,384]{0,1:T(8,128)(2,1)}, bf16[128,384]{0,1:T(8,128)(2,1)}, u32[]{:S(2)}, u32[]{:S(2)}) collective-permute-start(bf16[128,384]{0,1:T(8,128)(2,1)} %get-tuple-element.23), channel_id=1, source_target_pairs={{0,24},{8,16},{16,8},{24,0},{1,25},{9,17},{17,9},{25,1},{2,26},{10... | collective-permute-start | bytes 294920 | tf_op jit(solution)/shard_map/ppermute | solution.py:175
  30.6 45.9 %collective-permute-start.2 = (bf16[128,384]{0,1:T(8,128)(2,1)}, bf16[128,384]{0,1:T(8,128)(2,1)}, u32[]{:S(2)}, u32[]{:S(2)}) collective-permute-start(bf16[128,384]{0,1:T(8,128)(2,1)} %get-tuple-element.22), channel_id=1, source_target_pairs={{0,16},{8,24},{16,0},{24,8},{1,17},{9,25},{17,1},{25,9},{2,18},{10... | collective-permute-start | bytes 294920 | tf_op jit(solution)/shard_map/ppermute | solution.py:175
  34.1 42.4 %collective-permute-start.3 = (bf16[128,384]{0,1:T(8,128)(2,1)}, bf16[128,384]{0,1:T(8,128)(2,1)}, u32[]{:S(2)}, u32[]{:S(2)}) collective-permute-start(bf16[128,384]{0,1:T(8,128)(2,1)} %get-tuple-element.21), channel_id=1, source_target_pairs={{0,8},{8,0},{16,24},{24,16},{1,9},{9,1},{17,25},{25,17},{2,10},{10... | collective-permute-start | bytes 294920 | tf_op jit(solution)/shard_map/ppermute | solution.py:175
  86.6 2.1 %copy-start.4 = (f32[256,256]{0,1:T(8,128)S(1)}, f32[256,256]{0,1:T(8,128)}, u32[]{:S(2)}) copy-start(f32[256,256]{0,1:T(8,128)} %pad_maximum_fusion.2) | copy-start | bytes 786436
  86.6 13.3 %copy-start.1 = (bf16[256,1376]{1,0:T(8,128)(2,1)S(1)}, bf16[256,1376]{1,0:T(8,128)(2,1)}, u32[]{:S(2)}) copy-start(bf16[256,1376]{1,0:T(8,128)(2,1)} %copy.60) | copy-start | bytes 2113540
  86.6 13.3 %copy-start.2 = (bf16[256,1376]{1,0:T(8,128)(2,1)S(1)}, bf16[256,1376]{1,0:T(8,128)(2,1)}, u32[]{:S(2)}) copy-start(bf16[256,1376]{1,0:T(8,128)(2,1)} %copy.69) | copy-start | bytes 2113540
  89.5 17.7 %all-to-all-start.1 = ((f32[8,32,256]{2,1,0:T(8,128)}), f32[8,32,256]{2,1,0:T(8,128)S(1)}, u32[]{:S(2)}, u32[]{:S(2)}) async-start(f32[8,32,256]{2,1,0:T(8,128)} %bitcast.7), calls=%async_computation.1 | async-start | bytes 524288 | tf_op jit(solution)/shard_map/all_to_all | solution.py:185
  108.1 11.1 %all-to-all-start.2 = ((f32[16,32,128]{2,1,0:T(8,128)}), f32[16,32,128]{2,1,0:T(8,128)S(1)}, u32[]{:S(2)}, u32[]{:S(2)}) async-start(f32[16,32,128]{2,1,0:T(8,128)} %broadcast_in_dim.10), calls=%async_computation.2 | async-start | bytes 524288 | tf_op jit(solution)/shard_map/all_to_all | solution.py:123
Sparse Core Ops, SparseCore 0:
  9.5 82.2 all-gather.1

commit v4 on v3

v4 whole, which is shorter than its diff:
```python
import functools
import math

import jax
import jax.numpy as jnp
from jax import lax
from jax.experimental import pallas as pl
from jax.experimental.pallas import tpu as pltpu
from jax.sharding import Mesh
from jax.sharding import PartitionSpec as P

LEN = 2048
STEP = 32
CHUNKS = 4
DP = ("zh", "zl", "yl", "c")
TENSOR = ("x", "yh")
QUERY_GROUP = ("yl", "c")
SHARE = TENSOR + QUERY_GROUP
SWAP = [(0, 1), (1, 0)]
HIGHEST = lax.Precision.HIGHEST
VMEM = pl.BlockSpec(memory_space=pltpu.VMEM)


def dot(a, b):
    return jnp.dot(a, b, preferred_element_type=jnp.float32)


def prepare_kernel(yl_ref, blocks_ref, own_ref, partner_ref, cot_ref, slope_ref, silu_ref):
    across, _, along, rows, depth = blocks_ref.shape
    yl = yl_ref[0]
    for i, source in enumerate((yl, 1 - yl)):
        for x in range(across):
            for y in range(along):
                start = (x * along + y) * depth
                cot_ref[i * rows : (i + 1) * rows, start : start + depth] = blocks_ref[x, source, y]
    for i, pre_ref in enumerate((own_ref, partner_ref)):

        def some_rows(step, _, i=i, pre_ref=pre_ref):
            first = pl.multiple_of(step * STEP, STEP)
            gate = pre_ref[pl.ds(first, STEP), :].astype(jnp.float32)
            up = pre_ref[pl.ds(rows + first, STEP), :].astype(jnp.float32)
            sig = 1.0 / (1.0 + jnp.exp(-gate))
            here = pl.ds(i * rows + first, STEP)
            silu_ref[here, :] = (gate * sig).astype(jnp.bfloat16)
            slope_ref[here, :] = (up * sig * (1.0 + gate * (1.0 - sig))).astype(jnp.bfloat16)
            return 0

        lax.fori_loop(0, rows // STEP, some_rows, 0)


def prepare(yl, blocks, own, partner):
    rows, depth = blocks.shape[3:]
    hid = own.shape[1]
    return pl.pallas_call(
        prepare_kernel,
        out_shape=(
            jax.ShapeDtypeStruct((2 * rows, blocks.shape[0] * blocks.shape[2] * depth), jnp.bfloat16),
            jax.ShapeDtypeStruct((2 * rows, hid), jnp.bfloat16),
            jax.ShapeDtypeStruct((2 * rows, hid), jnp.bfloat16),
        ),
        in_specs=[pl.BlockSpec(memory_space=pltpu.SMEM)] + [VMEM] * 3,
        out_specs=(VMEM,) * 3,
        compiler_params=pltpu.CompilerParams(vmem_limit_bytes=56 * 2**20),
        cost_estimate=pl.CostEstimate(flops=20 * rows * hid, bytes_accessed=8 * rows * hid, transcendentals=4 * rows * hid),
        name="prepare",
    )(yl, blocks, own, partner)


def gradient_kernel(
    yl_ref, cot_hbm, weight_hbm, slope_hbm, silu_hbm, proj_ref, x_ref, down_ref, _,
    out_ref, cot, weight, slope, silu, total, rows_ref, sems,
):
    rank = down_ref.shape[0]
    span = weight.shape[0] // CHUNKS
    chunks = [pl.ds(i * span, span) for i in range(CHUNKS)]
    moves = [(cot_hbm, cot)] + [(weight_hbm.at[chunk], weight.at[chunk]) for chunk in chunks]
    moves += [(slope_hbm, slope), (silu_hbm, silu)]
    copies = [pltpu.make_async_copy(source, target, sems.at[i]) for i, (source, target) in enumerate(moves)]
    for copy in copies:
        copy.start()
    copies[0].wait()
    for i, chunk in enumerate(chunks):
        copies[1 + i].wait()
        term = dot(cot[:, chunk], weight[chunk, :])
        if i == 0:
            total[...] = term
        elif i < CHUNKS - 1:
            total[...] += term
    grad = total[...] + term
    copies[-2].wait()
    copies[-1].wait()
    gate_sum = dot((grad * slope[...].astype(jnp.float32)).astype(jnp.bfloat16), proj_ref[...])
    up_sum = dot((grad * silu[...].astype(jnp.float32)).astype(jnp.bfloat16), proj_ref[...])
    lane = lax.broadcasted_iota(jnp.int32, gate_sum.shape, 1)
    both = jnp.where(lane < rank, gate_sum, up_sum)
    events = x_ref.shape[2]
    yl = yl_ref[0]
    square = jnp.dot(x_ref[yl], both[:events], precision=HIGHEST, preferred_element_type=jnp.float32)
    square += jnp.dot(x_ref[1 - yl], both[events:], precision=HIGHEST, preferred_element_type=jnp.float32)
    rows_ref[:rank, :rank] = square[:rank, :rank]
    rows_ref[rank : 2 * rank, :rank] = square[rank:, rank:]
    rows_ref[2 * rank :, :rank] = down_ref[...]
    rows_ref[:, rank:] = jnp.zeros_like(rows_ref[:, rank:])
    members = out_ref.shape[0]
    each = rows_ref.shape[0] // members
    for i in range(each):
        row = rows_ref[pl.ds(i, members, stride=each), :]
        out_ref[:, :, i * rank : (i + 1) * rank] = row[:, None, :rank]


def gradient_blocks(yl, cot, weight, slope, silu, proj, proj_x, block_d, queries, members):
    rank = block_d.shape[0]
    anywhere = pl.BlockSpec(memory_space=pl.ANY)
    return pl.pallas_call(
        gradient_kernel,
        out_shape=jax.ShapeDtypeStruct((members, 1, 3 * rank * rank // members), jnp.float32),
        in_specs=[pl.BlockSpec(memory_space=pltpu.SMEM)] + [anywhere] * 4 + [VMEM] * 3 + [anywhere],
        out_specs=VMEM,
        scratch_shapes=[
            pltpu.VMEM(cot.shape, jnp.bfloat16),
            pltpu.VMEM(weight.shape, jnp.bfloat16),
            pltpu.VMEM(slope.shape, jnp.bfloat16),
            pltpu.VMEM(silu.shape, jnp.bfloat16),
            pltpu.VMEM(slope.shape, jnp.float32),
            pltpu.VMEM((3 * rank, 2 * rank), jnp.float32),
            pltpu.SemaphoreType.DMA((CHUNKS + 3,)),
        ],
        compiler_params=pltpu.CompilerParams(vmem_limit_bytes=56 * 2**20),
        cost_estimate=pl.CostEstimate(
            flops=2 * slope.shape[0] * weight.shape[0] * weight.shape[1],
            bytes_accessed=weight.size * 2,
            transcendentals=0,
        ),
        name="gradient_blocks",
    )(yl, cot, weight, slope, silu, proj, proj_x, block_d, queries)


def score_kernel(scale, rows_ref, query_ref, out_ref):
    copies, sessions, width = out_ref.shape
    groups = query_ref.shape[1] // width
    left = (rows_ref[:, 0] + rows_ref[:, 1]).reshape(sessions, -1)
    terms = []
    for _ in range(3):
        terms.append(left.astype(jnp.bfloat16).astype(jnp.float32))
        left = left - terms[-1]
    products = dot(jnp.concatenate(terms, axis=0).astype(jnp.bfloat16), query_ref[...])
    scores = products[:sessions] + (products[sessions : 2 * sessions] + products[2 * sessions :])
    scores = scores * scale
    for i in range(copies):
        first = i % groups * width
        out_ref[i] = scores[:, first : first + width]


def score_blocks(rows, query, copies, width, scale):
    return pl.pallas_call(
        functools.partial(score_kernel, scale),
        out_shape=jax.ShapeDtypeStruct((copies, rows.shape[0], width), jnp.float32),
        in_specs=[VMEM, VMEM],
        out_specs=VMEM,
        name="score_blocks",
    )(rows, query)


def give_all(block, axes):
    n = lax.axis_size(axes)
    return lax.all_to_all(jnp.broadcast_to(block[None], (n,) + block.shape), axes, 0, 0)


def on_device(
    inputs,
    cotangent,
    gate_pre,
    up_pre,
    down_weight,
    proj_in_x,
    proj_in_h,
    proj_out_ff,
    proj_out_d,
    queries,
    lengths,
):
    rows, width = cotangent.shape
    hid = gate_pre.shape[1]
    rank = proj_in_h.shape[1]
    own_yl = lax.axis_index("yl")
    tensor_size = lax.axis_size(TENSOR)

    weight = lax.all_gather(down_weight.T, ("zh", "zl", "c"), axis=0, tiled=True)

    per_half = cotangent.reshape(rows, -1, 2, 2 * down_weight.shape[1]).transpose(2, 0, 1, 3)
    per_half = per_half.reshape(2, 1, rows, width // 2)
    per_half = jnp.broadcast_to(per_half, (2, lax.axis_size("yh"), rows, width // 2))
    along_y = lax.all_to_all(per_half.reshape(-1, rows, width // 2), ("yl", "yh"), 0, 0)

    own_gate = gate_pre.astype(jnp.float32)
    hidden = (own_gate * jax.nn.sigmoid(own_gate) * up_pre.astype(jnp.float32)).astype(jnp.bfloat16)
    parts = jnp.concatenate(
        [dot(inputs, proj_in_x), dot(hidden, proj_in_h), dot(cotangent, proj_out_d)], axis=1
    )

    both_pre = jnp.concatenate([gate_pre, up_pre], axis=0)
    along_y = jnp.broadcast_to(along_y[None], (lax.axis_size("x"),) + along_y.shape)
    along_y, both_pre, queries = lax.optimization_barrier((along_y, both_pre, queries))
    along_x = lax.all_to_all(along_y, "x", 0, 0).reshape(-1, 2, lax.axis_size("yh"), rows, width // 2)

    groups = lax.axis_size(QUERY_GROUP)
    member = lax.axis_index(QUERY_GROUP)
    quarters = queries.reshape(queries.shape[0], groups, -1).transpose(1, 0, 2)
    arrivals = []
    for flip in range(groups):
        piece = lax.dynamic_index_in_dim(quarters, member ^ flip, 0, keepdims=False)
        pairs = [(i, i ^ flip) for i in range(groups)]
        arrivals.append(lax.ppermute(piece, QUERY_GROUP, pairs) if flip else piece)

    partner_pre = lax.ppermute(both_pre, "yl", SWAP)
    yl = own_yl.reshape(1)
    full_cot, gate_slope, silu = prepare(yl, along_x, both_pre, partner_pre)

    some = rows // tensor_size
    parts, along_x = lax.optimization_barrier((parts, along_x))
    sums = lax.all_to_all(parts.reshape(tensor_size, some, 4 * rank), TENSOR, 0, 0).sum(axis=0)

    first_event = lax.axis_index(DP) * rows + lax.axis_index(TENSOR) * some
    positions = first_event % LEN + jnp.arange(some, dtype=jnp.int32)
    live = (positions < lengths[first_event // LEN]).astype(jnp.float32)[:, None]
    sums_x, sums_h, sums_d = sums[:, : 2 * rank] * live, sums[:, 2 * rank : 3 * rank], sums[:, 3 * rank :]
    block_d = jnp.einsum("tr,ts->rs", sums_h, sums_d * live, precision=HIGHEST)
    proj_x = give_all(sums_x, ("yl",) + TENSOR).reshape(2, rows, 2 * rank).transpose(0, 2, 1)

    proj_x, arrivals = lax.optimization_barrier((proj_x, arrivals))
    for bit in (1, 2):
        arrivals = [jnp.where(member & bit, arrivals[i ^ bit], arrivals[i]) for i in range(groups)]
    own_queries = jnp.concatenate(arrivals, axis=0).T

    members = tensor_size * groups
    blocks = gradient_blocks(
        yl, full_cot, weight, gate_slope, silu, proj_out_ff, proj_x, block_d, own_queries, members
    )

    entries = lax.all_to_all(blocks, SHARE, 0, 0).sum(axis=0)
    entries = give_all(entries, ("zh", "zl"))
    entries = entries.reshape(-1, lax.axis_size("zl"), *entries.shape[1:])
    partial_scores = score_blocks(entries, own_queries, members, queries.shape[0], 1.0 / math.sqrt(LEN))
    return lax.all_to_all(partial_scores, SHARE, 0, 0).sum(axis=0)


def solution(mesh):
    fine = Mesh(mesh.devices.reshape(8, 2, 2, 2, 4, 2), DP + TENSOR)
    return jax.shard_map(
        on_device,
        mesh=fine,
        in_specs=(
            P(DP, TENSOR),
            P(DP, TENSOR),
            P(DP, TENSOR),
            P(DP, TENSOR),
            P(TENSOR, DP),
            P(TENSOR, None),
            P(TENSOR, None),
            P(TENSOR, None),
            P(TENSOR, None),
            P(DP, TENSOR),
            P(),
        ),
        out_specs=P(None, DP),
        check_vma=False,
    )
```

time: 199 us -> 172 us (0.86)
  waiting for transfers between devices: 37.5 us -> 26.6 us
  other arithmetic: 13.8 us -> 3.28 us
  local copies, waits for them, and re-layouts: 21.9 us -> 13.7 us
  Pallas kernels: 11.9 us -> 17.4 us
  blocking collectives: 57.9 us -> 54.3 us
    ppermute x3, waiting for transfers between devices: 30.5 us -> 0.01 us  [on_device(): arrivals.append(lax.ppermute(piece, QUERY_GROUP, pairs) if flip else piece)]
    all_to_all x1 -> x2, waiting for transfers between devices: 0.01 us -> 20.9 us  [the longest x1 15 us: on_device(): lax.all_to_all(along_y, 'x', 0, 0)]
    unnamed x20 -> x17, local copies, waits for them, and re-layouts: 11.4 us -> 1.8 us
    all_to_all x1, starting transfers between devices: 10.4 us -> 4.05 us  [on_device(): lax.all_to_all(parts.reshape(tensor_size, some, 4 * rank), TENSOR, 0, 0)]
    pallas_call x0 -> x1, Pallas kernels: none -> 6.34 us  [prepare(): pl.pallas_call(prepare_kernel, out_shape=(jax.ShapeDtypeStruct((2 * rows,...]
    convert_element_type x1 -> x0, other arithmetic: 4.75 us -> none  [on_device(): silu = (gate_float * sig).astype(jnp.bfloat16)]
    ppermute x3, starting transfers between devices: 10.6 us -> 14.8 us  [on_device(): arrivals.append(lax.ppermute(piece, QUERY_GROUP, pairs) if flip else piece)]
    all_to_all x1 -> x2, starting transfers between devices: 7.72 us -> 11.7 us  [the longest x1 6.65 us: on_device(): lax.all_to_all(along_y, 'x', 0, 0)]
  transfers between devices with their start and end apart: 8 -> 9, of which waited for: 3 -> 3; matrix products, arithmetic and copies ran while one was open for 20% -> 12% of each run, Pallas kernels for 0% -> 4%
where the time goes in v4:
time: 172 us; the launch traced here: 171 us
  blocking collectives  54.3 us (32%)
  starting transfers between devices  36.6 us (21%)
  waiting for transfers between devices  26.6 us (15%)
  Pallas kernels  17.4 us (10%)
  local copies, waits for them, and re-layouts  13.7 us (8%)
  between operations  13.7 us (8%)
  matrix products  5.08 us (3%)
  other arithmetic  3.28 us (2%)
    all_to_all x1, blocking collectives, give_all(): lax.all_to_all(jnp.broadcast_to(block[None], (n,) + block.shape), axes, 0...  26.4 us
    all_to_all x1, waiting for transfers between devices, on_device(): lax.all_to_all(along_y, 'x', 0, 0)  15 us
    all_to_all x1, blocking collectives, on_device(): entries = lax.all_to_all(blocks, SHARE, 0, 0).sum(axis=0)  14.8 us
    ppermute x3, starting transfers between devices, on_device(): arrivals.append(lax.ppermute(piece, QUERY_GROUP, pairs) if flip else piece)  14.8 us
    all_to_all x1, blocking collectives, on_device(): return lax.all_to_all(partial_scores, SHARE, 0, 0).sum(axis=0)  13.1 us
    pallas_call x1, Pallas kernels, gradient_blocks(): pl.pallas_call(gradient_kernel, out_shape=jax.ShapeDtypeStruct((members,...  9.15 us
    all_to_all x1, starting transfers between devices, on_device(): lax.all_to_all(along_y, 'x', 0, 0)  6.65 us
    pallas_call x1, Pallas kernels, prepare(): pl.pallas_call(prepare_kernel, out_shape=(jax.ShapeDtypeStruct((2 * rows,...  6.34 us
  transfers between devices with their start and end apart: 9, of which 3 were waited for; matrix products, arithmetic and copies ran while one was open for 12% of the time, Pallas kernels for 4%

profile of v4, /device:TPU:1, one launch (start us, length us, event | category | flops | bytes accessed | tf_op | source)
XLA Modules:
  0.0 170.6 jit_solution(1057650362001603521)
XLA Ops:
  7.3 1.1 copy.38
  8.5 0.8 broadcast_in_dim.11
  9.4 5.0 %all-to-all-start = ((bf16[4,256,256]{2,1,0:T(8,128)(2,1)}), bf16[4,256,256]{2,1,0:T(8,128)(2,1)}, u32[]{:S(2)}, u32[]{:S(2)}) async-start(bf16[4,256,256]{2,1,0:T(8,128)(2,1)} %bitcast.4), calls=%async_computation | async-start | bytes 1048576 | tf_op jit(solution)/shard_map/all_to_all | solution.py:193
  15.2 5.9 %all-to-all-done = bf16[4,256,256]{2,1,0:T(8,128)(2,1)} async-done(((bf16[4,256,256]{2,1,0:T(8,128)(2,1)}), bf16[4,256,256]{2,1,0:T(8,128)(2,1)}, u32[]{:S(2)}, u32[]{:S(2)}) %all-to-all-start) | async-done | bytes 524320 | tf_op jit(solution)/shard_map/all_to_all | solution.py:193
  21.2 2.6 %broadcast_in_dim.12 = bf16[4,4,256,256]{3,2,1,0:T(8,128)(2,1)} broadcast(bf16[4,256,256]{2,1,0:T(8,128)(2,1)} %all-to-all-done), dimensions={1,2,3} | broadcast | bytes 2621440 | tf_op jit(solution)/shard_map/broadcast_in_dim | solution.py:202
  23.8 6.7 %all-to-all-start.1 = ((bf16[4,4,256,256]{3,2,1,0:T(8,128)(2,1)}), bf16[4,4,256,256]{3,2,1,0:T(8,128)(2,1)}, u32[]{:S(2)}, u32[]{:S(2)}) async-start(bf16[4,4,256,256]{3,2,1,0:T(8,128)(2,1)} %broadcast_in_dim.12), calls=%async_computation.1 | async-start | bytes 4194304 | tf_op jit(solution)/shard_map/all_to_all | solution.py:204
  31.1 1.9 %collective-permute-start = (bf16[512,1376]{0,1:T(8,128)(2,1)S(1)}, bf16[512,1376]{0,1:T(8,128)(2,1)S(1)}, u32[]{:S(2)}, u32[]{:S(2)}) collective-permute-start(bf16[512,1376]{0,1:T(8,128)(2,1)S(1)} %copy.43), channel_id=1, source_target_pairs={{0,16},{16,0},{1,17},{17,1},{2,18},{18,2},{3,19},{19,3},{4,20},{20... | collective-permute-start | bytes 4227080 | tf_op jit(solution)/shard_map/ppermute | solution.py:215
  33.1 1.2 fusion.12
  34.2 1.1 fusion.11
  35.4 1.9 %fusion.5 = f32[256,64]{0,1:T(8,128)S(1)} fusion(bf16[1376,64]{0,1:T(8,128)(2,1)} %param.17, bf16[256,1376]{0,1:T(8,128)(2,1)} %param.14, bf16[256,1376]{0,1:T(8,128)(2,1)} %param.13), kind=kOutput, calls=%fused_computation.8 | convolution fusion | flops 47906816 | bytes 1650688 | tf_op jit(solution)/shard_map/dot_general | solution.py:25
  37.4 15.0 %all-to-all-done.1 = bf16[4,4,256,256]{3,2,1,0:T(8,128)(2,1)} async-done(((bf16[4,4,256,256]{3,2,1,0:T(8,128)(2,1)}), bf16[4,4,256,256]{3,2,1,0:T(8,128)(2,1)}, u32[]{:S(2)}, u32[]{:S(2)}) %all-to-all-start.1) | async-done | bytes 2097184 | tf_op jit(solution)/shard_map/all_to_all | solution.py:204
  52.4 0.9 copy.45
  53.2 4.1 %all-to-all-start.2 = ((f32[8,32,256]{2,1,0:T(8,128)}), f32[8,32,256]{2,1,0:T(8,128)}, u32[]{:S(2)}, u32[]{:S(2)}) async-start(f32[8,32,256]{2,1,0:T(8,128)} %bitcast.7), calls=%async_computation.2 | async-start | bytes 524288 | tf_op jit(solution)/shard_map/all_to_all | solution.py:221
  58.5 1.2 copy.51
  59.7 4.9 %all-to-all-done.2 = f32[8,32,256]{2,1,0:T(8,128)} async-done(((f32[8,32,256]{2,1,0:T(8,128)}), f32[8,32,256]{2,1,0:T(8,128)}, u32[]{:S(2)}, u32[]{:S(2)}) %all-to-all-start.2) | async-done | bytes 262176 | tf_op jit(solution)/shard_map/all_to_all | solution.py:221
  64.7 1.0 reduce_sum.27
  65.7 0.7 broadcast_in_dim.13
  66.4 4.2 %all-to-all-start.3 = ((f32[16,32,128]{2,1,0:T(8,128)}), f32[16,32,128]{2,1,0:T(8,128)}, u32[]{:S(2)}, u32[]{:S(2)}) async-start(f32[16,32,128]{2,1,0:T(8,128)} %broadcast_in_dim.13), calls=%async_computation.3 | async-start | bytes 524288 | tf_op jit(solution)/shard_map/all_to_all | solution.py:166
  70.6 0.8 dynamic-slice_bitcast_fusion
  71.4 9.3 %collective-permute-start.1 = (bf16[128,384]{0,1:T(8,128)(2,1)}, bf16[128,384]{0,1:T(8,128)(2,1)S(1)}, u32[]{:S(2)}, u32[]{:S(2)}) collective-permute-start(bf16[128,384]{0,1:T(8,128)(2,1)} %get-tuple-element.35), channel_id=1, source_target_pairs={{0,8},{8,0},{16,24},{24,16},{1,9},{9,1},{17,25},{25,17},{2,10},{10... | collective-permute-start | bytes 294920 | tf_op jit(solution)/shard_map/ppermute | solution.py:213
  80.7 3.5 %collective-permute-start.2 = (bf16[128,384]{0,1:T(8,128)(2,1)}, bf16[128,384]{0,1:T(8,128)(2,1)S(1)}, u32[]{:S(2)}, u32[]{:S(2)}) collective-permute-start(bf16[128,384]{0,1:T(8,128)(2,1)} %get-tuple-element.34), channel_id=1, source_target_pairs={{0,16},{8,24},{16,0},{24,8},{1,17},{9,25},{17,1},{25,9},{2,18},{10... | collective-permute-start | bytes 294920 | tf_op jit(solution)/shard_map/ppermute | solution.py:213
  84.2 2.0 %collective-permute-start.3 = (bf16[128,384]{0,1:T(8,128)(2,1)}, bf16[128,384]{0,1:T(8,128)(2,1)S(1)}, u32[]{:S(2)}, u32[]{:S(2)}) collective-permute-start(bf16[128,384]{0,1:T(8,128)(2,1)} %get-tuple-element.33), channel_id=1, source_target_pairs={{0,24},{8,16},{16,8},{24,0},{1,25},{9,17},{17,9},{25,1},{2,26},{10... | collective-permute-start | bytes 294920 | tf_op jit(solution)/shard_map/ppermute | solution.py:213
  86.2 1.6 copy.44.partner_ref
  87.8 6.3 %prepare.1 = (bf16[512,2048]{1,0:T(8,128)(2,1)}, bf16[512,1376]{1,0:T(8,128)(2,1)}, bf16[512,1376]{1,0:T(8,128)(2,1)}) custom-call(s32[1]{0:T(128)} %bitcast.yl_ref, bf16[4,2,2,256,256]{4,3,2,1,0:T(8,128)(2,1)} %bitcast.5.blocks_ref, bf16[512,1376]{1,0:T(8,128)(2,1)} %copy-done.1, bf16[512,1376]{1,0:T(8,128)(2,1)} %copy.44.partner_ref), custom_call_target="tpu_custom_call" | custom-call | flops 7045120 | bytes 2818048 | tf_op jit(solution)/shard_map/prepare/pallas_call | solution.py:54
  94.1 0.9 fusion.7.down_ref
  95.0 1.8 %copy.46 = f32[2,256,128]{1,2,0:T(8,128)} copy(f32[2,256,128]{2,1,0:T(8,128)} %bitcast.9) | data formatting | bytes 524288 | tf_op jit(solution)/shard_map/reshape | solution.py:228
  96.9 0.8 maximum_bitcast_fusion._.query_ref
  97.7 9.2 %gradient_blocks.1 = f32[32,1,384]{2,1,0:T(1,128)} custom-call(s32[1]{0:T(128)} %bitcast.yl_ref, bf16[512,2048]{1,0:T(8,128)(2,1)} %get-tuple-element.19.cot_hbm, bf16[2048,1376]{1,0:T(8,128)(2,1)} %all-gather.2.cloned.1.call-done.weight_hbm, bf16[512,1376]{1,0:T(8,128)(2,1)} %get-tuple-element.20.slope_hbm, bf16[512,1376]{1,0:T(8,128)(2,1)} %get-tuple-element.21.silu_hbm, ...), custom_call_target="tpu_custom_call" | custom-call | flops 2885681152 | bytes 5636096 | tf_op jit(solution)/shard_map/gradient_blocks/pallas_call | solution.py:114
  106.8 14.8 %all_to_all.35 = f32[32,1,384]{2,1,0:T(1,128)S(1)} all-to-all(f32[32,1,384]{2,1,0:T(1,128)} %gradient_blocks.1), channel_id=1, replica_groups=mesh['zh'=8,'zl'=2,'yl'=2,'c'=2,'x'=4,'yh'=2] {'x','yh','yl','c'}, dimensions={0} | all-to-all | bytes 98304 | tf_op jit(solution)/shard_map/all_to_all | solution.py:240
  121.7 26.4 %all_to_all.36 = f32[16,1,384]{2,1,0:T(1,128)} all-to-all(f32[16,1,384]{2,1,0:T(1,128)S(1)} %broadcast_in_dim.14), channel_id=1, replica_groups=mesh['zh'=8,'zl'=2,'yl'=2,'c'=2,'x'=4,'yh'=2] {'zh','zl'}, dimensions={0} | all-to-all | bytes 49152 | tf_op jit(solution)/shard_map/all_to_all | solution.py:166
  148.1 1.9 %score_blocks.1 = f32[32,8,128]{2,1,0:T(8,128)} custom-call(f32[8,2,1,384]{3,2,1,0:T(1,128)} %bitcast.34, bf16[384,512]{1,0:T(8,128)(2,1)} %maximum_bitcast_fusion._.query_ref), custom_call_target="tpu_custom_call" | custom-call | tf_op jit(solution)/shard_map/score_blocks/pallas_call | solution.py:155
  150.0 13.1 %all_to_all.37 = f32[32,8,128]{2,1,0:T(8,128)S(1)} all-to-all(f32[32,8,128]{2,1,0:T(8,128)} %score_blocks.1), channel_id=1, replica_groups=mesh['zh'=8,'zl'=2,'yl'=2,'c'=2,'x'=4,'yh'=2] {'x','yh','yl','c'}, dimensions={0} | all-to-all | bytes 262144 | tf_op jit(solution)/shard_map/all_to_all | solution.py:244
  (36 shorter events, 4.4 us)
Async XLA Ops:
  6.5 27.7 %copy-start = (bf16[256,512]{1,0:T(8,128)(2,1)S(1)}, bf16[256,512]{1,0:T(8,128)(2,1)}, u32[]{:S(2)}) copy-start(bf16[256,512]{1,0:T(8,128)(2,1)} %param.11) | copy-start | bytes 786436
  6.5 91.1 %all-gather.2.cloned.1.call-start = ((), (), s32[]{:S(2)}) async-start(), calls=%async_computation.7 | async-start | bytes 5947392 | tf_op jit(solution)/shard_map/all_gather | solution.py:188
  8.3 6.1 %copy-start.3 = (bf16[256,1376]{0,1:T(8,128)(2,1)S(1)}, bf16[256,1376]{0,1:T(8,128)(2,1)}, u32[]{:S(2)}) copy-start(bf16[256,1376]{0,1:T(8,128)(2,1)} %param.13) | copy-start | bytes 2113540
  8.5 6.2 %copy-start.2 = (bf16[256,1376]{0,1:T(8,128)(2,1)S(1)}, bf16[256,1376]{0,1:T(8,128)(2,1)}, u32[]{:S(2)}) copy-start(bf16[256,1376]{0,1:T(8,128)(2,1)} %param.14) | copy-start | bytes 2113540
  9.4 11.8 %all-to-all-start = ((bf16[4,256,256]{2,1,0:T(8,128)(2,1)}), bf16[4,256,256]{2,1,0:T(8,128)(2,1)}, u32[]{:S(2)}, u32[]{:S(2)}) async-start(bf16[4,256,256]{2,1,0:T(8,128)(2,1)} %bitcast.4), calls=%async_computation | async-start | bytes 1048576 | tf_op jit(solution)/shard_map/all_to_all | solution.py:193
  15.2 15.2 %copy-start.1 = (bf16[512,1376]{1,0:T(8,128)(2,1)}, bf16[512,1376]{1,0:T(8,128)(2,1)S(1)}, u32[]{:S(2)}) copy-start(bf16[512,1376]{1,0:T(8,128)(2,1)S(1)} %pad_maximum_fusion.own_ref) | copy-start | bytes 4227076
  23.8 28.6 %all-to-all-start.1 = ((bf16[4,4,256,256]{3,2,1,0:T(8,128)(2,1)}), bf16[4,4,256,256]{3,2,1,0:T(8,128)(2,1)}, u32[]{:S(2)}, u32[]{:S(2)}) async-start(bf16[4,4,256,256]{3,2,1,0:T(8,128)(2,1)} %broadcast_in_dim.12), calls=%async_computation.1 | async-start | bytes 4194304 | tf_op jit(solution)/shard_map/all_to_all | solution.py:204
  30.4 2.6 %copy-start.5 = (bf16[512,64]{0,1:T(8,128)(2,1)S(1)}, bf16[512,64]{0,1:T(8,128)(2,1)}, u32[]{:S(2)}) copy-start(bf16[512,64]{0,1:T(8,128)(2,1)} %param.19) | copy-start | bytes 196612
  31.1 55.1 %collective-permute-start = (bf16[512,1376]{0,1:T(8,128)(2,1)S(1)}, bf16[512,1376]{0,1:T(8,128)(2,1)S(1)}, u32[]{:S(2)}, u32[]{:S(2)}) collective-permute-start(bf16[512,1376]{0,1:T(8,128)(2,1)S(1)} %copy.43), channel_id=1, source_target_pairs={{0,16},{16,0},{1,17},{17,1},{2,18},{18,2},{3,19},{19,3},{4,20},{20... | collective-permute-start | bytes 4227080 | tf_op jit(solution)/shard_map/ppermute | solution.py:215
  37.3 20.0 %copy-start.6 = (s32[8]{0:T(128)S(1)}, s32[8]{0:T(128)}, u32[]{:S(2)}) copy-start(s32[8]{0:T(128)} %param.21) | copy-start | bytes 100
  53.2 11.4 %all-to-all-start.2 = ((f32[8,32,256]{2,1,0:T(8,128)}), f32[8,32,256]{2,1,0:T(8,128)}, u32[]{:S(2)}, u32[]{:S(2)}) async-start(f32[8,32,256]{2,1,0:T(8,128)} %bitcast.7), calls=%async_computation.2 | async-start | bytes 524288 | tf_op jit(solution)/shard_map/all_to_all | solution.py:221
  66.4 28.5 %all-to-all-start.3 = ((f32[16,32,128]{2,1,0:T(8,128)}), f32[16,32,128]{2,1,0:T(8,128)}, u32[]{:S(2)}, u32[]{:S(2)}) async-start(f32[16,32,128]{2,1,0:T(8,128)} %broadcast_in_dim.13), calls=%async_computation.3 | async-start | bytes 524288 | tf_op jit(solution)/shard_map/all_to_all | solution.py:166
  71.4 25.4 %collective-permute-start.1 = (bf16[128,384]{0,1:T(8,128)(2,1)}, bf16[128,384]{0,1:T(8,128)(2,1)S(1)}, u32[]{:S(2)}, u32[]{:S(2)}) collective-permute-start(bf16[128,384]{0,1:T(8,128)(2,1)} %get-tuple-element.35), channel_id=1, source_target_pairs={{0,8},{8,0},{16,24},{24,16},{1,9},{9,1},{17,25},{25,17},{2,10},{10... | collective-permute-start | bytes 294920 | tf_op jit(solution)/shard_map/ppermute | solution.py:213
  80.7 16.0 %collective-permute-start.2 = (bf16[128,384]{0,1:T(8,128)(2,1)}, bf16[128,384]{0,1:T(8,128)(2,1)S(1)}, u32[]{:S(2)}, u32[]{:S(2)}) collective-permute-start(bf16[128,384]{0,1:T(8,128)(2,1)} %get-tuple-element.34), channel_id=1, source_target_pairs={{0,16},{8,24},{16,0},{24,8},{1,17},{9,25},{17,1},{25,9},{2,18},{10... | collective-permute-start | bytes 294920 | tf_op jit(solution)/shard_map/ppermute | solution.py:213
  84.2 12.5 %collective-permute-start.3 = (bf16[128,384]{0,1:T(8,128)(2,1)}, bf16[128,384]{0,1:T(8,128)(2,1)S(1)}, u32[]{:S(2)}, u32[]{:S(2)}) collective-permute-start(bf16[128,384]{0,1:T(8,128)(2,1)} %get-tuple-element.33), channel_id=1, source_target_pairs={{0,24},{8,16},{16,8},{24,0},{1,25},{9,17},{17,9},{25,1},{2,26},{10... | collective-permute-start | bytes 294920 | tf_op jit(solution)/shard_map/ppermute | solution.py:213
  87.8 9.0 %copy-start.4 = (bf16[128,384]{0,1:T(8,128)(2,1)S(1)}, bf16[128,384]{0,1:T(8,128)(2,1)}, u32[]{:S(2)}) copy-start(bf16[128,384]{0,1:T(8,128)(2,1)} %get-tuple-element.28) | copy-start | bytes 294916
Sparse Core Ops, SparseCore 0:
  9.5 82.3 all-gather.1

commit v5 on v4

v5 whole, which is shorter than its diff:
```python
import functools
import math

import jax
import jax.numpy as jnp
from jax import lax
from jax.experimental import pallas as pl
from jax.experimental.pallas import tpu as pltpu
from jax.sharding import Mesh
from jax.sharding import PartitionSpec as P

LEN = 2048
STEP = 32
CHUNKS = 4
DP = ("zh", "zl", "yl", "c")
TENSOR = ("x", "yh")
QUERY_GROUP = ("yl", "c")
SHARE = TENSOR + QUERY_GROUP
SWAP = [(0, 1), (1, 0)]
HIGHEST = lax.Precision.HIGHEST
VMEM = pl.BlockSpec(memory_space=pltpu.VMEM)


def dot(a, b):
    return jnp.dot(a, b, preferred_element_type=jnp.float32)


def local_kernel(pre_ref, in_ref, in_proj_ref, hid_proj_ref, cot_ref, out_proj_ref, slopes_ref, parts_ref, hidden_ref):
    rows = hidden_ref.shape[0]
    rank = out_proj_ref.shape[1]

    def some_rows(step, _):
        first = pl.multiple_of(step * STEP, STEP)
        above, below = pl.ds(first, STEP), pl.ds(rows + first, STEP)
        gate = pre_ref[above, :].astype(jnp.float32)
        up = pre_ref[below, :].astype(jnp.float32)
        sig = 1.0 / (1.0 + jnp.exp(-gate))
        silu = gate * sig
        slopes_ref[above, :] = (up * sig * (1.0 + gate * (1.0 - sig))).astype(jnp.bfloat16)
        slopes_ref[below, :] = silu.astype(jnp.bfloat16)
        hidden_ref[above, :] = (silu * up).astype(jnp.bfloat16)
        return 0

    lax.fori_loop(0, rows // STEP, some_rows, 0)
    parts_ref[:, : 2 * rank] = dot(in_ref[...], in_proj_ref[...])
    parts_ref[:, 2 * rank : 3 * rank] = dot(hidden_ref[...], hid_proj_ref[...])
    parts_ref[:, 3 * rank :] = dot(cot_ref[...], out_proj_ref[...])


def local_terms(pre, inputs, proj_in_x, proj_in_h, cotangent, proj_out_d):
    rows, hid = pre.shape[0] // 2, pre.shape[1]
    return pl.pallas_call(
        local_kernel,
        out_shape=(
            jax.ShapeDtypeStruct((2 * rows, hid), jnp.bfloat16),
            jax.ShapeDtypeStruct((rows, 4 * proj_out_d.shape[1]), jnp.float32),
        ),
        in_specs=[VMEM] * 6,
        out_specs=(VMEM, VMEM),
        scratch_shapes=[pltpu.VMEM((rows, hid), jnp.bfloat16)],
        compiler_params=pltpu.CompilerParams(vmem_limit_bytes=56 * 2**20),
        cost_estimate=pl.CostEstimate(flops=800 * rows * hid, bytes_accessed=8 * rows * hid, transcendentals=2 * rows * hid),
        name="local_terms",
    )(pre, inputs, proj_in_x, proj_in_h, cotangent, proj_out_d)


def gradient_kernel(
    yl_ref, blocks_hbm, weight_hbm, own_slopes, partner_slopes, proj_ref, x_ref, down_ref, _,
    out_ref, cot, weight, slope, silu, total, rows_ref, sems,
):
    rank = down_ref.shape[0]
    across, _, along, events, depth = blocks_hbm.shape
    span = weight.shape[0] // CHUNKS
    chunks = [pl.ds(i * span, span) for i in range(CHUNKS)]
    yl = yl_ref[0]
    own, partner = pl.ds(0, events), pl.ds(events, events)
    cot_moves = [
        (blocks_hbm.at[x, source, y], cot.at[rows, pl.ds((x * along + y) * depth, depth)])
        for x in range(across)
        for y in range(along)
        for source, rows in ((yl, own), (1 - yl, partner))
    ]
    weight_moves = [(weight_hbm.at[chunk], weight.at[chunk]) for chunk in chunks]
    above, below = own, partner
    slope_moves = [(own_slopes.at[above], slope.at[own]), (partner_slopes.at[above], slope.at[partner])]
    slope_moves += [(own_slopes.at[below], silu.at[own]), (partner_slopes.at[below], silu.at[partner])]
    per_chunk = len(cot_moves) // CHUNKS
    copies = []
    for source, target in cot_moves + weight_moves + slope_moves:
        copies.append(pltpu.make_async_copy(source, target, sems.at[len(copies)]))
    of_cot, of_weight = copies[: len(cot_moves)], copies[len(cot_moves) :][:CHUNKS]
    of_slopes = copies[len(cot_moves) + CHUNKS :]
    for i in range(CHUNKS):
        for copy in of_cot[i * per_chunk :][:per_chunk]:
            copy.start()
        of_weight[i].start()
    for copy in of_slopes:
        copy.start()
    for i, chunk in enumerate(chunks):
        for copy in of_cot[i * per_chunk :][:per_chunk]:
            copy.wait()
        of_weight[i].wait()
        term = dot(cot[:, chunk], weight[chunk, :])
        if i == 0:
            total[...] = term
        elif i < CHUNKS - 1:
            total[...] += term
    grad = total[...] + term
    for copy in of_slopes:
        copy.wait()
    gate_sum = dot((grad * slope[...].astype(jnp.float32)).astype(jnp.bfloat16), proj_ref[...])
    up_sum = dot((grad * silu[...].astype(jnp.float32)).astype(jnp.bfloat16), proj_ref[...])
    lane = lax.broadcasted_iota(jnp.int32, gate_sum.shape, 1)
    both = jnp.where(lane < rank, gate_sum, up_sum)
    square = outer(x_ref[yl], both[:events]) + outer(x_ref[1 - yl], both[events:])
    rows_ref[:rank, :rank] = square[:rank, :rank]
    rows_ref[rank : 2 * rank, :rank] = square[rank:, rank:]
    rows_ref[2 * rank :, :rank] = down_ref[...]
    rows_ref[:, rank:] = jnp.zeros_like(rows_ref[:, rank:])
    members = out_ref.shape[0]
    each = rows_ref.shape[0] // members
    for i in range(each):
        row = rows_ref[pl.ds(i, members, stride=each), :]
        out_ref[:, :, i * rank : (i + 1) * rank] = row[:, None, :rank]


def gradient_blocks(yl, blocks, weight, own_slopes, partner_slopes, proj, proj_x, block_d, arrival, members):
    rank = block_d.shape[0]
    rows, hid = 2 * blocks.shape[3], weight.shape[1]
    depth = weight.shape[0]
    anywhere = pl.BlockSpec(memory_space=pl.ANY)
    return pl.pallas_call(
        gradient_kernel,
        out_shape=jax.ShapeDtypeStruct((members, 1, 3 * rank * rank // members), jnp.float32),
        in_specs=[pl.BlockSpec(memory_space=pltpu.SMEM)] + [anywhere] * 4 + [VMEM] * 3 + [anywhere],
        out_specs=VMEM,
        scratch_shapes=[
            pltpu.VMEM((rows, depth), jnp.bfloat16),
            pltpu.VMEM((depth, hid), jnp.bfloat16),
            pltpu.VMEM((rows, hid), jnp.bfloat16),
            pltpu.VMEM((rows, hid), jnp.bfloat16),
            pltpu.VMEM((rows, hid), jnp.float32),
            pltpu.VMEM((3 * rank, 2 * rank), jnp.float32),
            pltpu.SemaphoreType.DMA((blocks.shape[0] * 2 * blocks.shape[2] + CHUNKS + 4,)),
        ],
        compiler_params=pltpu.CompilerParams(vmem_limit_bytes=56 * 2**20),
        cost_estimate=pl.CostEstimate(
            flops=2 * rows * depth * hid,
            bytes_accessed=weight.size * 2,
            transcendentals=0,
        ),
        name="gradient_blocks",
    )(yl, blocks, weight, own_slopes, partner_slopes, proj, proj_x, block_d, arrival)


def score_kernel(scale, member_ref, rows_ref, query_ref, out_ref):
    copies, sessions, _ = out_ref.shape
    groups = query_ref.shape[0]
    left = (rows_ref[:, 0] + rows_ref[:, 1]).reshape(sessions, -1)
    terms = []
    for _ in range(3):
        terms.append(left.astype(jnp.bfloat16).astype(jnp.float32))
        left = left - terms[-1]
    terms = jnp.concatenate(terms, axis=0).astype(jnp.bfloat16)
    for group in range(groups):
        products = dot(terms, query_ref[member_ref[0] ^ group])
        scores = products[:sessions] + (products[sessions : 2 * sessions] + products[2 * sessions :])
        for i in range(group, copies, groups):
            out_ref[i] = scores * scale


def score_blocks(member, rows, query, copies, scale):
    return pl.pallas_call(
        functools.partial(score_kernel, scale),
        out_shape=jax.ShapeDtypeStruct((copies, rows.shape[0], query.shape[2]), jnp.float32),
        in_specs=[pl.BlockSpec(memory_space=pltpu.SMEM), VMEM, VMEM],
        out_specs=VMEM,
        name="score_blocks",
    )(member, rows, query)


def outer(a, b):
    return lax.dot_general(
        a, b, (((0,), (0,)), ((), ())), precision=HIGHEST, preferred_element_type=jnp.float32
    )


def give_all(block, axes):
    n = lax.axis_size(axes)
    return lax.all_to_all(jnp.broadcast_to(block[None], (n,) + block.shape), axes, 0, 0)


def on_device(
    inputs,
    cotangent,
    gate_pre,
    up_pre,
    down_weight,
    proj_in_x,
    proj_in_h,
    proj_out_ff,
    proj_out_d,
    queries,
    lengths,
):
    rows, width = cotangent.shape
    hid = gate_pre.shape[1]
    rank = proj_in_h.shape[1]
    own_yl = lax.axis_index("yl")
    tensor_size = lax.axis_size(TENSOR)

    weight = lax.all_gather(down_weight.T, ("zh", "zl", "c"), axis=0, tiled=True)

    per_half = cotangent.reshape(rows, -1, 2, 2 * down_weight.shape[1]).transpose(2, 0, 1, 3)
    per_half = per_half.reshape(2, 1, rows, width // 2)
    per_half = jnp.broadcast_to(per_half, (2, lax.axis_size("yh"), rows, width // 2))
    along_y = lax.all_to_all(per_half.reshape(-1, rows, width // 2), ("yl", "yh"), 0, 0)

    both_pre = jnp.concatenate([gate_pre, up_pre], axis=0)
    own_slopes, parts = local_terms(both_pre, inputs, proj_in_x, proj_in_h, cotangent, proj_out_d)

    along_y = jnp.broadcast_to(along_y[None], (lax.axis_size("x"),) + along_y.shape)
    along_y, own_slopes = lax.optimization_barrier((along_y, own_slopes))
    along_x = lax.all_to_all(along_y, "x", 0, 0).reshape(-1, 2, lax.axis_size("yh"), rows, width // 2)

    partner_slopes = lax.ppermute(own_slopes, "yl", SWAP)

    groups = lax.axis_size(QUERY_GROUP)
    member = lax.axis_index(QUERY_GROUP)
    quarters = queries.T.reshape(groups, -1, queries.shape[0])
    arrivals = []
    for flip in range(groups):
        piece = lax.dynamic_index_in_dim(quarters, member ^ flip, 0, keepdims=False)
        pairs = [(i, i ^ flip) for i in range(groups)]
        arrivals.append(lax.ppermute(piece, QUERY_GROUP, pairs) if flip else piece)

    yl = own_yl.reshape(1)

    some = rows // tensor_size
    parts, along_x = lax.optimization_barrier((parts, along_x))
    sums = lax.all_to_all(parts.reshape(tensor_size, some, 4 * rank), TENSOR, 0, 0).sum(axis=0)

    sums, arrivals[1], arrivals[2] = lax.optimization_barrier((sums, arrivals[1], arrivals[2]))
    first_event = lax.axis_index(DP) * rows + lax.axis_index(TENSOR) * some
    positions = first_event % LEN + jnp.arange(some, dtype=jnp.int32)
    live = (positions < lengths[first_event // LEN]).astype(jnp.float32)[:, None]
    sums_x, sums_h, sums_d = sums[:, : 2 * rank] * live, sums[:, 2 * rank : 3 * rank], sums[:, 3 * rank :]
    block_d = jnp.einsum("tr,ts->rs", sums_h, sums_d * live, precision=HIGHEST)
    proj_x = give_all(sums_x, ("yl",) + TENSOR).reshape(2, rows, 2 * rank)

    proj_x, arrivals[3] = lax.optimization_barrier((proj_x, arrivals[3]))

    members = tensor_size * groups
    blocks = gradient_blocks(
        yl, along_x, weight, own_slopes, partner_slopes, proj_out_ff, proj_x, block_d, arrivals[3], members
    )

    entries = lax.all_to_all(blocks, SHARE, 0, 0).sum(axis=0)
    entries = give_all(entries, ("zh", "zl"))
    entries = entries.reshape(-1, lax.axis_size("zl"), *entries.shape[1:])
    partial_scores = score_blocks(member.reshape(1), entries, jnp.stack(arrivals), members, 1.0 / math.sqrt(LEN))
    return lax.all_to_all(partial_scores, SHARE, 0, 0).sum(axis=0)


def solution(mesh):
    fine = Mesh(mesh.devices.reshape(8, 2, 2, 2, 4, 2), DP + TENSOR)
    return jax.shard_map(
        on_device,
        mesh=fine,
        in_specs=(
            P(DP, TENSOR),
            P(DP, TENSOR),
            P(DP, TENSOR),
            P(DP, TENSOR),
            P(TENSOR, DP),
            P(TENSOR, None),
            P(TENSOR, None),
            P(TENSOR, None),
            P(TENSOR, None),
            P(DP, TENSOR),
            P(),
        ),
        out_specs=P(None, DP),
        check_vma=False,
    )
```

time: 172 us -> 160 us (0.930)
  blocking collectives: 54.3 us -> 27.7 us
  waiting for transfers between devices: 26.6 us -> 38.9 us
  starting transfers between devices: 36.6 us -> 45 us
  matrix products: 5.08 us -> 0.86 us
  Pallas kernels: 17.4 us -> 14.6 us
    all_to_all x1 -> x0, blocking collectives: 26.4 us -> none  [give_all(): lax.all_to_all(jnp.broadcast_to(block[None], (n,) + block.shape), axes, 0...]
    all_to_all x1 -> x2, starting transfers between devices: 4.19 us -> 15.6 us  [give_all(): lax.all_to_all(jnp.broadcast_to(block[None], (n,) + block.shape), axes, 0...]
    all_to_all x1 -> x2, waiting for transfers between devices: 0.01 us -> 9.73 us  [give_all(): lax.all_to_all(jnp.broadcast_to(block[None], (n,) + block.shape), axes, 0...]
    all_to_all x1, waiting for transfers between devices: 5.92 us -> 0.01 us  [on_device(): lax.all_to_all(per_half.reshape(-1, rows, width // 2), ('yl', 'yh'), 0, 0)]
    all_gather x1, waiting for transfers between devices: 0.01 us -> 5.82 us  [on_device(): lax.all_gather(down_weight.T, ('zh', 'zl', 'c'), axis=0, tiled=True)]
    all_to_all x1, waiting for transfers between devices: 4.91 us -> 0.01 us  [on_device(): lax.all_to_all(parts.reshape(tensor_size, some, 4 * rank), TENSOR, 0, 0)]
    ppermute x3, waiting for transfers between devices: 0.01 us -> 4.51 us  [on_device(): arrivals.append(lax.ppermute(piece, QUERY_GROUP, pairs) if flip else piece)]
    dot_general x3 -> x0, matrix products: 4.22 us -> none  [dot(): return jnp.dot(a, b, preferred_element_type=jnp.float32)]
  transfers between devices with their start and end apart: 9 -> 10, of which waited for: 3 -> 5; matrix products, arithmetic and copies ran while one was open for 12% -> 11% of each run, Pallas kernels for 4% -> 2%
where the time goes in v5:
time: 160 us; the launch traced here: 159 us
  starting transfers between devices  45 us (28%)
  waiting for transfers between devices  38.9 us (24%)
  blocking collectives  27.7 us (17%)
  Pallas kernels  14.6 us (9%)
  local copies, waits for them, and re-layouts  14.1 us (9%)
  between operations  13.7 us (9%)
  other arithmetic  4.33 us (3%)
    all_to_all x1, waiting for transfers between devices, on_device(): lax.all_to_all(along_y, 'x', 0, 0)  18.1 us
    all_to_all x2, starting transfers between devices, give_all(): lax.all_to_all(jnp.broadcast_to(block[None], (n,) + block.shape), axes, 0...  15.6 us
    all_to_all x1, blocking collectives, on_device(): entries = lax.all_to_all(blocks, SHARE, 0, 0).sum(axis=0)  14.6 us
    all_to_all x1, blocking collectives, on_device(): return lax.all_to_all(partial_scores, SHARE, 0, 0).sum(axis=0)  13.1 us
    ppermute x3, starting transfers between devices, on_device(): arrivals.append(lax.ppermute(piece, QUERY_GROUP, pairs) if flip else piece)  13.1 us
    all_to_all x2, waiting for transfers between devices, give_all(): lax.all_to_all(jnp.broadcast_to(block[None], (n,) + block.shape), axes, 0...  9.73 us
    pallas_call x1, Pallas kernels, gradient_blocks(): pl.pallas_call(gradient_kernel, out_shape=jax.ShapeDtypeStruct((members,...  8.97 us
    all_gather x1, waiting for transfers between devices, on_device(): lax.all_gather(down_weight.T, ('zh', 'zl', 'c'), axis=0, tiled=True)  5.82 us
  transfers between devices with their start and end apart: 10, of which 5 were waited for; matrix products, arithmetic and copies ran while one was open for 11% of the time, Pallas kernels for 2%

profile of v5, /device:TPU:1, one launch (start us, length us, event | category | flops | bytes accessed | tf_op | source)
XLA Modules:
  0.0 159.3 jit_solution(4449578741187537868)
XLA Ops:
  6.5 0.7 all-gather.2.cloned.1.call-update
  7.3 1.1 copy.35
  8.5 0.8 broadcast_in_dim.11
  9.4 5.0 %all-to-all-start = ((bf16[4,256,256]{2,1,0:T(8,128)(2,1)}), bf16[4,256,256]{2,1,0:T(8,128)(2,1)S(1)}, u32[]{:S(2)}, u32[]{:S(2)}) async-start(bf16[4,256,256]{2,1,0:T(8,128)(2,1)} %bitcast.5), calls=%async_computation | async-start | bytes 1048576 | tf_op jit(solution)/shard_map/all_to_all | solution.py:217
  15.3 0.9 copy.33.hid_proj_ref
  16.2 0.8 copy.34.out_proj_ref
  17.0 1.2 pad_maximum_fusion.pre_ref
  18.2 3.8 %local_terms.1 = (bf16[512,1376]{1,0:T(8,128)(2,1)}, f32[256,256]{1,0:T(8,128)}) custom-call(bf16[512,1376]{1,0:T(8,128)(2,1)} %pad_maximum_fusion.pre_ref, bf16[256,512]{1,0:T(8,128)(2,1)} %in_ref.1, bf16[512,128]{1,0:T(8,128)(2,1)} %in_proj_ref.1, bf16[1376,64]{1,0:T(8,128)(2,1)} %copy.33.hid_proj_ref, bf16[256,512]{1,0:T(8,128)(2,1)} %cot_ref.1, ...), custom_call_target="tpu_custom_call" | custom-call | flops 281804800 | bytes 2818048 | tf_op jit(solution)/shard_map/local_terms/pallas_call | solution.py:52
  22.0 1.5 broadcast_in_dim.12
  23.5 5.8 %all-to-all-start.1 = ((bf16[4,4,256,256]{3,2,1,0:T(8,128)(2,1)}), bf16[4,4,256,256]{3,2,1,0:T(8,128)(2,1)S(1)}, u32[]{:S(2)}, u32[]{:S(2)}) async-start(bf16[4,4,256,256]{3,2,1,0:T(8,128)(2,1)} %broadcast_in_dim.12), calls=%async_computation.1 | async-start | bytes 4194304 | tf_op jit(solution)/shard_map/all_to_all | solution.py:224
  29.3 1.6 copy.38
  30.9 2.0 %collective-permute-start = (bf16[512,1376]{0,1:T(8,128)(2,1)}, bf16[512,1376]{0,1:T(8,128)(2,1)}, u32[]{:S(2)}, u32[]{:S(2)}) collective-permute-start(bf16[512,1376]{0,1:T(8,128)(2,1)} %copy.38), channel_id=1, source_target_pairs={{0,16},{16,0},{1,17},{17,1},{2,18},{18,2},{3,19},{19,3},{4,20},{20... | collective-permute-start | bytes 4227080 | tf_op jit(solution)/shard_map/ppermute | solution.py:226
  33.0 1.2 copy.39
  34.2 18.1 %all-to-all-done.1 = bf16[4,4,256,256]{3,2,1,0:T(8,128)(2,1)S(1)} async-done(((bf16[4,4,256,256]{3,2,1,0:T(8,128)(2,1)}), bf16[4,4,256,256]{3,2,1,0:T(8,128)(2,1)S(1)}, u32[]{:S(2)}, u32[]{:S(2)}) %all-to-all-start.1) | async-done | bytes 2097184 | tf_op jit(solution)/shard_map/all_to_all | solution.py:224
  52.3 3.4 %all-to-all-start.2 = ((f32[8,32,256]{2,1,0:T(8,128)}), f32[8,32,256]{2,1,0:T(8,128)S(1)}, u32[]{:S(2)}, u32[]{:S(2)}) async-start(f32[8,32,256]{2,1,0:T(8,128)} %bitcast.31), calls=%async_computation.2 | async-start | bytes 524288 | tf_op jit(solution)/shard_map/all_to_all | solution.py:241
  55.8 6.2 %collective-permute-start.1 = (bf16[384,128]{1,0:T(8,128)(2,1)S(1)}, bf16[384,128]{1,0:T(8,128)(2,1)S(1)}, u32[]{:S(2)}, u32[]{:S(2)}) collective-permute-start(bf16[384,128]{1,0:T(8,128)(2,1)S(1)} %get-tuple-element.30), channel_id=1, source_target_pairs={{0,8},{8,0},{16,24},{24,16},{1,9},{9,1},{17,25},{25,17},{2,10},{10... | collective-permute-start | bytes 294920 | tf_op jit(solution)/shard_map/ppermute | solution.py:235
  62.0 2.2 %collective-permute-start.2 = (bf16[384,128]{1,0:T(8,128)(2,1)S(1)}, bf16[384,128]{1,0:T(8,128)(2,1)S(1)}, u32[]{:S(2)}, u32[]{:S(2)}) collective-permute-start(bf16[384,128]{1,0:T(8,128)(2,1)S(1)} %get-tuple-element.29), channel_id=1, source_target_pairs={{0,16},{8,24},{16,0},{24,8},{1,17},{9,25},{17,1},{25,9},{2,18},{10... | collective-permute-start | bytes 294920 | tf_op jit(solution)/shard_map/ppermute | solution.py:235
  65.6 3.3 %collective-permute-done.2 = bf16[384,128]{1,0:T(8,128)(2,1)S(1)} collective-permute-done((bf16[384,128]{1,0:T(8,128)(2,1)S(1)}, bf16[384,128]{1,0:T(8,128)(2,1)S(1)}, u32[]{:S(2)}, u32[]{:S(2)}) %collective-permute-start.2) | collective-permute-done | bytes 98336 | tf_op jit(solution)/shard_map/ppermute | solution.py:235
  69.0 0.7 broadcast_in_dim.13
  69.7 6.9 %all-to-all-start.3 = ((f32[16,32,128]{2,1,0:T(8,128)}), f32[16,32,128]{2,1,0:T(8,128)S(1)}, u32[]{:S(2)}, u32[]{:S(2)}) async-start(f32[16,32,128]{2,1,0:T(8,128)} %broadcast_in_dim.13), calls=%async_computation.3 | async-start | bytes 524288 | tf_op jit(solution)/shard_map/all_to_all | solution.py:190
  76.6 4.7 %collective-permute-start.3 = (bf16[384,128]{1,0:T(8,128)(2,1)S(1)}, bf16[384,128]{1,0:T(8,128)(2,1)S(1)}, u32[]{:S(2)}, u32[]{:S(2)}) collective-permute-start(bf16[384,128]{1,0:T(8,128)(2,1)S(1)} %get-tuple-element.28), channel_id=1, source_target_pairs={{0,24},{8,16},{16,8},{24,0},{1,25},{9,17},{17,9},{25,1},{2,26},{10... | collective-permute-start | bytes 294920 | tf_op jit(solution)/shard_map/ppermute | solution.py:235
  81.3 2.6 %copy.40.partner_slopes = bf16[512,1376]{1,0:T(8,128)(2,1)} copy(bf16[512,1376]{0,1:T(8,128)(2,1)} %collective-permute-done) | data formatting | bytes 2818048 | tf_op jit(solution)/shard_map/ppermute | solution.py:226
  83.9 0.9 fusion.down_ref
  84.8 1.2 collective-permute-done.3._
  85.9 5.8 %all-gather.2.cloned.1.call-done.weight_hbm = bf16[2048,1376]{1,0:T(8,128)(2,1)} async-done(((bf16[64,1376]{1,0:T(8,128)(2,1)}), bf16[2048,1376]{1,0:T(8,128)(2,1)}) %all-gather.2.cloned.1.call-update) | async-done | bytes 5636112 | tf_op jit(solution)/shard_map/all_gather | solution.py:212
  91.8 9.0 %gradient_blocks.1 = f32[32,1,384]{2,1,0:T(1,128)} custom-call(s32[1]{0:T(128)} %bitcast.1.yl_ref, bf16[4,2,2,256,256]{4,3,2,1,0:T(8,128)(2,1)} %bitcast.24, bf16[2048,1376]{1,0:T(8,128)(2,1)} %all-gather.2.cloned.1.call-done.weight_hbm, bf16[512,1376]{1,0:T(8,128)(2,1)} %get-tuple-element.20.own_slopes, bf16[512,1376]{1,0:T(8,128)(2,1)} %copy.40.partner_slopes, ...), custom_call_target="tpu_custom_call" | custom-call | flops 2885681152 | bytes 5636096 | tf_op jit(solution)/shard_map/gradient_blocks/pallas_call | solution.py:132
  100.7 14.6 %all_to_all.35 = f32[32,1,384]{2,1,0:T(1,128)S(1)} all-to-all(f32[32,1,384]{2,1,0:T(1,128)} %gradient_blocks.1), channel_id=1, replica_groups=mesh['zh'=8,'zl'=2,'yl'=2,'c'=2,'x'=4,'yh'=2] {'x','yh','yl','c'}, dimensions={0} | all-to-all | bytes 98304 | tf_op jit(solution)/shard_map/all_to_all | solution.py:258
  116.0 8.7 %all-to-all-start.5 = ((f32[16,1,384]{2,1,0:T(1,128)}), f32[16,1,384]{2,1,0:T(1,128)S(1)}, u32[]{:S(2)}, u32[]{:S(2)}) async-start(f32[16,1,384]{2,1,0:T(1,128)} %broadcast_in_dim.14), calls=%async_computation.5 | async-start | bytes 49152 | tf_op jit(solution)/shard_map/all_to_all | solution.py:190
  124.7 1.7 %pad_maximum_fusion.1.query_ref = bf16[4,384,128]{2,1,0:T(8,128)(2,1)} fusion(bf16[1,384,128]{2,1,0:T(8,128)(2,1)} %bitcast.29, bf16[1,384,128]{2,1,0:T(8,128)(2,1)S(1)} %bitcast.35, bf16[1,384,128]{2,1,0:T(8,128)(2,1)S(1)} %bitcast.34, bf16[1,384,128]{2,1,0:T(8,128)(2,1)S(1)} %get-tuple-element.27), kind=kLoop, calls=%fused_computation.1 | loop fusion | flops 589824 | bytes 786432 | tf_op jit(solution)/shard_map/stack | solution.py:261
  126.4 9.7 %all-to-all-done.5 = f32[16,1,384]{2,1,0:T(1,128)S(1)} async-done(((f32[16,1,384]{2,1,0:T(1,128)}), f32[16,1,384]{2,1,0:T(1,128)S(1)}, u32[]{:S(2)}, u32[]{:S(2)}) %all-to-all-start.5) | async-done | bytes 24608 | tf_op jit(solution)/shard_map/all_to_all | solution.py:190
  136.8 1.9 %score_blocks.1 = f32[32,8,128]{2,1,0:T(8,128)} custom-call(s32[1]{0:T(128)} %bitcast.member_ref, f32[8,2,1,384]{3,2,1,0:T(1,128)} %bitcast.33, bf16[4,384,128]{2,1,0:T(8,128)(2,1)} %pad_maximum_fusion.1.query_ref), custom_call_target="tpu_custom_call" | custom-call | tf_op jit(solution)/shard_map/score_blocks/pallas_call | solution.py:173
  138.7 13.1 %all_to_all.36 = f32[32,8,128]{2,1,0:T(8,128)S(1)} all-to-all(f32[32,8,128]{2,1,0:T(8,128)} %score_blocks.1), channel_id=1, replica_groups=mesh['zh'=8,'zl'=2,'yl'=2,'c'=2,'x'=4,'yh'=2] {'x','yh','yl','c'}, dimensions={0} | all-to-all | bytes 262144 | tf_op jit(solution)/shard_map/all_to_all | solution.py:262
  (38 shorter events, 4.4 us)
Async XLA Ops:
  6.5 85.2 %all-gather.2.cloned.1.call-start = ((), (), s32[]{:S(2)}) async-start(), calls=%async_computation.7 | async-start | bytes 5947392 | tf_op jit(solution)/shard_map/all_gather | solution.py:212
  8.3 6.1 %copy-start.3 = (bf16[256,1376]{0,1:T(8,128)(2,1)S(1)}, bf16[256,1376]{0,1:T(8,128)(2,1)}, u32[]{:S(2)}) copy-start(bf16[256,1376]{0,1:T(8,128)(2,1)} %param.13) | copy-start | bytes 2113540
  8.5 6.2 %copy-start.4 = (bf16[256,1376]{0,1:T(8,128)(2,1)S(1)}, bf16[256,1376]{0,1:T(8,128)(2,1)}, u32[]{:S(2)}) copy-start(bf16[256,1376]{0,1:T(8,128)(2,1)} %param.14) | copy-start | bytes 2113540
  9.4 12.7 %all-to-all-start = ((bf16[4,256,256]{2,1,0:T(8,128)(2,1)}), bf16[4,256,256]{2,1,0:T(8,128)(2,1)S(1)}, u32[]{:S(2)}, u32[]{:S(2)}) async-start(bf16[4,256,256]{2,1,0:T(8,128)(2,1)} %bitcast.5), calls=%async_computation | async-start | bytes 1048576 | tf_op jit(solution)/shard_map/all_to_all | solution.py:217
  14.4 0.9 copy-start.6
  14.8 1.5 copy-start.8
  23.5 5.8 %copy-start.1 = (bf16[512,1376]{1,0:T(8,128)(2,1)S(1)}, bf16[512,1376]{1,0:T(8,128)(2,1)}, u32[]{:S(2)}) copy-start(bf16[512,1376]{1,0:T(8,128)(2,1)} %get-tuple-element.20.own_slopes) | copy-start | bytes 4227076
  23.5 28.8 %all-to-all-start.1 = ((bf16[4,4,256,256]{3,2,1,0:T(8,128)(2,1)}), bf16[4,4,256,256]{3,2,1,0:T(8,128)(2,1)S(1)}, u32[]{:S(2)}, u32[]{:S(2)}) async-start(bf16[4,4,256,256]{3,2,1,0:T(8,128)(2,1)} %broadcast_in_dim.12), calls=%async_computation.1 | async-start | bytes 4194304 | tf_op jit(solution)/shard_map/all_to_all | solution.py:224
  30.9 33.4 %copy-start.9 = (s32[8]{0:T(128)S(1)}, s32[8]{0:T(128)}, u32[]{:S(2)}) copy-start(s32[8]{0:T(128)} %param.21) | copy-start | bytes 100
  30.9 50.4 %collective-permute-start = (bf16[512,1376]{0,1:T(8,128)(2,1)}, bf16[512,1376]{0,1:T(8,128)(2,1)}, u32[]{:S(2)}, u32[]{:S(2)}) collective-permute-start(bf16[512,1376]{0,1:T(8,128)(2,1)} %copy.38), channel_id=1, source_target_pairs={{0,16},{16,0},{1,17},{17,1},{2,18},{18,2},{3,19},{19,3},{4,20},{20... | collective-permute-start | bytes 4227080 | tf_op jit(solution)/shard_map/ppermute | solution.py:226
  52.3 31.6 %copy-start = (bf16[4,4,256,256]{3,2,1,0:T(8,128)(2,1)}, bf16[4,4,256,256]{3,2,1,0:T(8,128)(2,1)S(1)}, u32[]{:S(2)}) copy-start(bf16[4,4,256,256]{3,2,1,0:T(8,128)(2,1)S(1)} %all-to-all-done.1) | copy-start | bytes 6291460
  52.3 13.2 %all-to-all-start.2 = ((f32[8,32,256]{2,1,0:T(8,128)}), f32[8,32,256]{2,1,0:T(8,128)S(1)}, u32[]{:S(2)}, u32[]{:S(2)}) async-start(f32[8,32,256]{2,1,0:T(8,128)} %bitcast.31), calls=%async_computation.2 | async-start | bytes 524288 | tf_op jit(solution)/shard_map/all_to_all | solution.py:241
  55.8 9.8 %collective-permute-start.1 = (bf16[384,128]{1,0:T(8,128)(2,1)S(1)}, bf16[384,128]{1,0:T(8,128)(2,1)S(1)}, u32[]{:S(2)}, u32[]{:S(2)}) collective-permute-start(bf16[384,128]{1,0:T(8,128)(2,1)S(1)} %get-tuple-element.30), channel_id=1, source_target_pairs={{0,8},{8,0},{16,24},{24,16},{1,9},{9,1},{17,25},{25,17},{2,10},{10... | collective-permute-start | bytes 294920 | tf_op jit(solution)/shard_map/ppermute | solution.py:235
  62.0 6.9 %collective-permute-start.2 = (bf16[384,128]{1,0:T(8,128)(2,1)S(1)}, bf16[384,128]{1,0:T(8,128)(2,1)S(1)}, u32[]{:S(2)}, u32[]{:S(2)}) collective-permute-start(bf16[384,128]{1,0:T(8,128)(2,1)S(1)} %get-tuple-element.29), channel_id=1, source_target_pairs={{0,16},{8,24},{16,0},{24,8},{1,17},{9,25},{17,1},{25,9},{2,18},{10... | collective-permute-start | bytes 294920 | tf_op jit(solution)/shard_map/ppermute | solution.py:235
  69.7 16.2 %all-to-all-start.3 = ((f32[16,32,128]{2,1,0:T(8,128)}), f32[16,32,128]{2,1,0:T(8,128)S(1)}, u32[]{:S(2)}, u32[]{:S(2)}) async-start(f32[16,32,128]{2,1,0:T(8,128)} %broadcast_in_dim.13), calls=%async_computation.3 | async-start | bytes 524288 | tf_op jit(solution)/shard_map/all_to_all | solution.py:190
  76.6 9.3 %collective-permute-start.3 = (bf16[384,128]{1,0:T(8,128)(2,1)S(1)}, bf16[384,128]{1,0:T(8,128)(2,1)S(1)}, u32[]{:S(2)}, u32[]{:S(2)}) collective-permute-start(bf16[384,128]{1,0:T(8,128)(2,1)S(1)} %get-tuple-element.28), channel_id=1, source_target_pairs={{0,24},{8,16},{16,8},{24,0},{1,25},{9,17},{17,9},{25,1},{2,26},{10... | collective-permute-start | bytes 294920 | tf_op jit(solution)/shard_map/ppermute | solution.py:235
  85.9 5.8 %copy-start.5 = (bf16[384,128]{1,0:T(8,128)(2,1)}, bf16[384,128]{1,0:T(8,128)(2,1)S(1)}, u32[]{:S(2)}) copy-start(bf16[384,128]{1,0:T(8,128)(2,1)S(1)} %collective-permute-done.3._) | copy-start | bytes 294916
  85.9 5.8 %copy-start.2 = (f32[16,32,128]{2,1,0:T(8,128)}, f32[16,32,128]{2,1,0:T(8,128)S(1)}, u32[]{:S(2)}) copy-start(f32[16,32,128]{2,1,0:T(8,128)S(1)} %all-to-all-done.3) | copy-start | bytes 786436
  116.0 20.1 %all-to-all-start.5 = ((f32[16,1,384]{2,1,0:T(1,128)}), f32[16,1,384]{2,1,0:T(1,128)S(1)}, u32[]{:S(2)}, u32[]{:S(2)}) async-start(f32[16,1,384]{2,1,0:T(1,128)} %broadcast_in_dim.14), calls=%async_computation.5 | async-start | bytes 49152 | tf_op jit(solution)/shard_map/all_to_all | solution.py:190
  136.1 0.6 copy-start.7
Sparse Core Ops, SparseCore 0:
  9.5 82.2 all-gather.1

commit v6 on v5

--- a/solution.py
+++ b/solution.py
@@ -65,13 +65,14 @@
 
 
 def gradient_kernel(
-    yl_ref, blocks_hbm, weight_hbm, own_slopes, partner_slopes, proj_ref, x_ref, down_ref, _,
-    out_ref, cot, weight, slope, silu, total, rows_ref, sems,
+    yl_ref, blocks_hbm, weight_hbm, own_slopes, partner_slopes, proj_hbm, x_hbm, down_hbm, _,
+    out_ref, cot, weight, slope, silu, proj_ref, x_ref, down_ref, total, rows_ref, sems,
 ):
-    rank = down_ref.shape[0]
+    rank = down_hbm.shape[0]
     across, _, along, events, depth = blocks_hbm.shape
-    span = weight.shape[0] // CHUNKS
-    chunks = [pl.ds(i * span, span) for i in range(CHUNKS)]
+    cores, layers, _, hid = weight_hbm.shape
+    layers = layers // CHUNKS
+    span = cot.shape[1] // CHUNKS
     yl = yl_ref[0]
     own, partner = pl.ds(0, events), pl.ds(events, events)
     cot_moves = [
@@ -80,27 +81,31 @@
         for y in range(along)
         for source, rows in ((yl, own), (1 - yl, partner))
     ]
-    weight_moves = [(weight_hbm.at[chunk], weight.at[chunk]) for chunk in chunks]
+    weight_moves = [
+        (weight_hbm.at[core, pl.ds(i * layers, layers)], weight.at[pl.ds(i * layers, layers), core])
+        for i in range(CHUNKS)
+        for core in range(cores)
+    ]
     above, below = own, partner
     slope_moves = [(own_slopes.at[above], slope.at[own]), (partner_slopes.at[above], slope.at[partner])]
     slope_moves += [(own_slopes.at[below], silu.at[own]), (partner_slopes.at[below], silu.at[partner])]
+    slope_moves += [(proj_hbm, proj_ref), (x_hbm, x_ref), (down_hbm, down_ref)]
     per_chunk = len(cot_moves) // CHUNKS
     copies = []
     for source, target in cot_moves + weight_moves + slope_moves:
         copies.append(pltpu.make_async_copy(source, target, sems.at[len(copies)]))
-    of_cot, of_weight = copies[: len(cot_moves)], copies[len(cot_moves) :][:CHUNKS]
-    of_slopes = copies[len(cot_moves) + CHUNKS :]
+    of_cot, of_weight = copies[: len(cot_moves)], copies[len(cot_moves) :][: len(weight_moves)]
+    of_slopes = copies[len(cot_moves) + len(weight_moves) :]
+    of_chunk = [
+        of_cot[i * per_chunk :][:per_chunk] + of_weight[i * cores :][:cores] for i in range(CHUNKS)
+    ]
+    for copy in sum(of_chunk, []) + of_slopes:
+        copy.start()
     for i in range(CHUNKS):
-        for copy in of_cot[i * per_chunk :][:per_chunk]:
-            copy.start()
-        of_weight[i].start()
-    for copy in of_slopes:
-        copy.start()
-    for i, chunk in enumerate(chunks):
-        for copy in of_cot[i * per_chunk :][:per_chunk]:
+        for copy in of_chunk[i]:
             copy.wait()
-        of_weight[i].wait()
-        term = dot(cot[:, chunk], weight[chunk, :])
+        rows_of_chunk = weight[pl.ds(i * layers, layers)].reshape(span, hid)
+        term = dot(cot[:, pl.ds(i * span, span)], rows_of_chunk)
         if i == 0:
             total[...] = term
         elif i < CHUNKS - 1:
@@ -126,22 +131,25 @@
 
 def gradient_blocks(yl, blocks, weight, own_slopes, partner_slopes, proj, proj_x, block_d, arrival, members):
     rank = block_d.shape[0]
-    rows, hid = 2 * blocks.shape[3], weight.shape[1]
-    depth = weight.shape[0]
+    cores, layers, features, hid = weight.shape
+    rows, depth = 2 * blocks.shape[3], cores * layers * features
     anywhere = pl.BlockSpec(memory_space=pl.ANY)
     return pl.pallas_call(
         gradient_kernel,
         out_shape=jax.ShapeDtypeStruct((members, 1, 3 * rank * rank // members), jnp.float32),
-        in_specs=[pl.BlockSpec(memory_space=pltpu.SMEM)] + [anywhere] * 4 + [VMEM] * 3 + [anywhere],
+        in_specs=[pl.BlockSpec(memory_space=pltpu.SMEM)] + [anywhere] * 8,
         out_specs=VMEM,
         scratch_shapes=[
             pltpu.VMEM((rows, depth), jnp.bfloat16),
-            pltpu.VMEM((depth, hid), jnp.bfloat16),
+            pltpu.VMEM((layers, cores, features, hid), jnp.bfloat16),
             pltpu.VMEM((rows, hid), jnp.bfloat16),
             pltpu.VMEM((rows, hid), jnp.bfloat16),
+            pltpu.VMEM(proj.shape, jnp.bfloat16),
+            pltpu.VMEM(proj_x.shape, jnp.float32),
+            pltpu.VMEM(block_d.shape, jnp.float32),
             pltpu.VMEM((rows, hid), jnp.float32),
             pltpu.VMEM((3 * rank, 2 * rank), jnp.float32),
-            pltpu.SemaphoreType.DMA((blocks.shape[0] * 2 * blocks.shape[2] + CHUNKS + 4,)),
+            pltpu.SemaphoreType.DMA((blocks.shape[0] * 2 * blocks.shape[2] + CHUNKS * cores + 7,)),
         ],
         compiler_params=pltpu.CompilerParams(vmem_limit_bytes=56 * 2**20),
         cost_estimate=pl.CostEstimate(
@@ -153,30 +161,31 @@
     )(yl, blocks, weight, own_slopes, partner_slopes, proj, proj_x, block_d, arrival)
 
 
-def score_kernel(scale, member_ref, rows_ref, query_ref, out_ref):
+def score_kernel(scale, member_ref, rows_ref, *refs):
+    *query_refs, out_ref = refs
     copies, sessions, _ = out_ref.shape
-    groups = query_ref.shape[0]
+    groups = len(query_refs)
     left = (rows_ref[:, 0] + rows_ref[:, 1]).reshape(sessions, -1)
     terms = []
     for _ in range(3):
         terms.append(left.astype(jnp.bfloat16).astype(jnp.float32))
         left = left - terms[-1]
     terms = jnp.concatenate(terms, axis=0).astype(jnp.bfloat16)
-    for group in range(groups):
-        products = dot(terms, query_ref[member_ref[0] ^ group])
+    for flip, query_ref in enumerate(query_refs):
+        products = dot(terms, query_ref[...])
         scores = products[:sessions] + (products[sessions : 2 * sessions] + products[2 * sessions :])
-        for i in range(group, copies, groups):
-            out_ref[i] = scores * scale
-
-
-def score_blocks(member, rows, query, copies, scale):
+        for i in range(0, copies, groups):
+            out_ref[i + (member_ref[0] ^ flip)] = scores * scale
+
+
+def score_blocks(member, rows, queries, copies, scale):
     return pl.pallas_call(
         functools.partial(score_kernel, scale),
-        out_shape=jax.ShapeDtypeStruct((copies, rows.shape[0], query.shape[2]), jnp.float32),
-        in_specs=[pl.BlockSpec(memory_space=pltpu.SMEM), VMEM, VMEM],
+        out_shape=jax.ShapeDtypeStruct((copies, rows.shape[0], queries[0].shape[1]), jnp.float32),
+        in_specs=[pl.BlockSpec(memory_space=pltpu.SMEM)] + [VMEM] * (1 + len(queries)),
         out_specs=VMEM,
         name="score_blocks",
-    )(member, rows, query)
+    )(member, rows, *queries)
 
 
 def outer(a, b):
@@ -209,7 +218,8 @@
     own_yl = lax.axis_index("yl")
     tensor_size = lax.axis_size(TENSOR)
 
-    weight = lax.all_gather(down_weight.T, ("zh", "zl", "c"), axis=0, tiled=True)
+    weight = lax.all_gather(down_weight.T, ("c", "zh", "zl"), axis=0)
+    weight = weight.reshape(lax.axis_size("c"), -1, *weight.shape[1:])
 
     per_half = cotangent.reshape(rows, -1, 2, 2 * down_weight.shape[1]).transpose(2, 0, 1, 3)
     per_half = per_half.reshape(2, 1, rows, width // 2)
@@ -258,7 +268,7 @@
     entries = lax.all_to_all(blocks, SHARE, 0, 0).sum(axis=0)
     entries = give_all(entries, ("zh", "zl"))
     entries = entries.reshape(-1, lax.axis_size("zl"), *entries.shape[1:])
-    partial_scores = score_blocks(member.reshape(1), entries, jnp.stack(arrivals), members, 1.0 / math.sqrt(LEN))
+    partial_scores = score_blocks(member.reshape(1), entries, arrivals, members, 1.0 / math.sqrt(LEN))
     return lax.all_to_all(partial_scores, SHARE, 0, 0).sum(axis=0)
 
 

time: 160 us -> 158 us (0.988)
  blocking collectives: 27.7 us -> 48.1 us
  waiting for transfers between devices: 38.9 us -> 28.3 us
  starting transfers between devices: 45 us -> 36.1 us
  other arithmetic: 4.33 us -> 2.69 us
    all_to_all x0 -> x1, blocking collectives: none -> 20.2 us  [give_all(): lax.all_to_all(jnp.broadcast_to(block[None], (n,) + block.shape), axes, 0...]
    all_to_all x2 -> x1, waiting for transfers between devices: 9.73 us -> 0.01 us  [give_all(): lax.all_to_all(jnp.broadcast_to(block[None], (n,) + block.shape), axes, 0...]
    all_to_all x2 -> x1, starting transfers between devices: 15.6 us -> 6.57 us  [give_all(): lax.all_to_all(jnp.broadcast_to(block[None], (n,) + block.shape), axes, 0...]
    another operation x1 -> x0, other arithmetic: 1.7 us -> none  [on_device(): jnp.stack(arrivals)]
    unnamed x25 -> x27, local copies, waits for them, and re-layouts: 4.3 us -> 4.05 us
  transfers between devices with their start and end apart: 10 -> 9, of which waited for: 5 -> 4; matrix products, arithmetic and copies ran while one was open for 11% -> 10% of each run, Pallas kernels for 2% -> 2%
where the time goes in v6:
time: 158 us; the launch traced here: 157 us
  blocking collectives  48.1 us (30%)
  starting transfers between devices  36.1 us (23%)
  waiting for transfers between devices  28.3 us (18%)
  local copies, waits for them, and re-layouts  14 us (9%)
  Pallas kernels  13.7 us (9%)
  between operations  13.7 us (9%)
  other arithmetic  2.69 us (2%)
    all_to_all x1, blocking collectives, give_all(): lax.all_to_all(jnp.broadcast_to(block[None], (n,) + block.shape), axes, 0...  20.2 us
    all_to_all x1, waiting for transfers between devices, on_device(): lax.all_to_all(along_y, 'x', 0, 0)  17.8 us
    all_to_all x1, blocking collectives, on_device(): entries = lax.all_to_all(blocks, SHARE, 0, 0).sum(axis=0)  14.6 us
    ppermute x3, starting transfers between devices, on_device(): arrivals.append(lax.ppermute(piece, QUERY_GROUP, pairs) if flip else piece)  13.5 us
    all_to_all x1, blocking collectives, on_device(): return lax.all_to_all(partial_scores, SHARE, 0, 0).sum(axis=0)  13.3 us
    pallas_call x1, Pallas kernels, gradient_blocks(): pl.pallas_call(gradient_kernel, out_shape=jax.ShapeDtypeStruct((members,...  7.94 us
    all_to_all x1, starting transfers between devices, give_all(): lax.all_to_all(jnp.broadcast_to(block[None], (n,) + block.shape), axes, 0...  6.57 us
    all_to_all x1, starting transfers between devices, on_device(): lax.all_to_all(along_y, 'x', 0, 0)  5.47 us
  transfers between devices with their start and end apart: 9, of which 4 were waited for; matrix products, arithmetic and copies ran while one was open for 10% of the time, Pallas kernels for 2%

profile of v6, /device:TPU:1, one launch (start us, length us, event | category | flops | bytes accessed | tf_op | source)
XLA Modules:
  0.0 157.3 jit_solution(2345234839078243917)
XLA Ops:
  6.5 0.7 all-gather.3.cloned.1.call-update
  7.3 1.1 copy.44
  8.5 0.8 broadcast_in_dim.11
  9.4 5.0 %all-to-all-start = ((bf16[4,256,256]{2,1,0:T(8,128)(2,1)}), bf16[4,256,256]{2,1,0:T(8,128)(2,1)S(1)}, u32[]{:S(2)}, u32[]{:S(2)}) async-start(bf16[4,256,256]{2,1,0:T(8,128)(2,1)} %bitcast.5), calls=%async_computation | async-start | bytes 1048576 | tf_op jit(solution)/shard_map/all_to_all | solution.py:227
  15.7 0.9 copy.42.hid_proj_ref
  16.6 0.8 copy.43.out_proj_ref
  17.3 1.2 pad_maximum_fusion.pre_ref
  18.6 3.8 %local_terms.1 = (bf16[512,1376]{1,0:T(8,128)(2,1)}, f32[256,256]{1,0:T(8,128)}) custom-call(bf16[512,1376]{1,0:T(8,128)(2,1)} %pad_maximum_fusion.pre_ref, bf16[256,512]{1,0:T(8,128)(2,1)} %in_ref.1, bf16[512,128]{1,0:T(8,128)(2,1)} %in_proj_ref.1, bf16[1376,64]{1,0:T(8,128)(2,1)} %copy.42.hid_proj_ref, bf16[256,512]{1,0:T(8,128)(2,1)} %cot_ref.1, ...), custom_call_target="tpu_custom_call" | custom-call | flops 281804800 | bytes 2818048 | tf_op jit(solution)/shard_map/local_terms/pallas_call | solution.py:52
  22.3 1.5 broadcast_in_dim.12
  23.9 5.5 %all-to-all-start.1 = ((bf16[4,4,256,256]{3,2,1,0:T(8,128)(2,1)}), bf16[4,4,256,256]{3,2,1,0:T(8,128)(2,1)S(1)}, u32[]{:S(2)}, u32[]{:S(2)}) async-start(bf16[4,4,256,256]{3,2,1,0:T(8,128)(2,1)} %broadcast_in_dim.12), calls=%async_computation.1 | async-start | bytes 4194304 | tf_op jit(solution)/shard_map/all_to_all | solution.py:234
  29.4 1.6 copy.47
  30.9 2.2 %collective-permute-start = (bf16[512,1376]{0,1:T(8,128)(2,1)}, bf16[512,1376]{0,1:T(8,128)(2,1)}, u32[]{:S(2)}, u32[]{:S(2)}) collective-permute-start(bf16[512,1376]{0,1:T(8,128)(2,1)} %copy.47), channel_id=1, source_target_pairs={{0,16},{16,0},{1,17},{17,1},{2,18},{18,2},{3,19},{19,3},{4,20},{20... | collective-permute-start | bytes 4227080 | tf_op jit(solution)/shard_map/ppermute | solution.py:236
  33.1 1.2 copy.53
  34.3 17.8 %all-to-all-done.1 = bf16[4,4,256,256]{3,2,1,0:T(8,128)(2,1)S(1)} async-done(((bf16[4,4,256,256]{3,2,1,0:T(8,128)(2,1)}), bf16[4,4,256,256]{3,2,1,0:T(8,128)(2,1)S(1)}, u32[]{:S(2)}, u32[]{:S(2)}) %all-to-all-start.1) | async-done | bytes 2097184 | tf_op jit(solution)/shard_map/all_to_all | solution.py:234
  52.1 3.4 %all-to-all-start.2 = ((f32[8,32,256]{2,1,0:T(8,128)}), f32[8,32,256]{2,1,0:T(8,128)S(1)}, u32[]{:S(2)}, u32[]{:S(2)}) async-start(f32[8,32,256]{2,1,0:T(8,128)} %bitcast.31), calls=%async_computation.2 | async-start | bytes 524288 | tf_op jit(solution)/shard_map/all_to_all | solution.py:251
  55.5 0.7 dynamic-slice_bitcast_fusion
  56.2 6.8 %collective-permute-start.1 = (bf16[384,128]{1,0:T(8,128)(2,1)S(1)}, bf16[384,128]{1,0:T(8,128)(2,1)S(1)}, u32[]{:S(2)}, u32[]{:S(2)}) collective-permute-start(bf16[384,128]{1,0:T(8,128)(2,1)S(1)} %get-tuple-element.30), channel_id=1, source_target_pairs={{0,8},{8,0},{16,24},{24,16},{1,9},{9,1},{17,25},{25,17},{2,10},{10... | collective-permute-start | bytes 294920 | tf_op jit(solution)/shard_map/ppermute | solution.py:245
  63.0 2.2 %collective-permute-start.2 = (bf16[384,128]{1,0:T(8,128)(2,1)S(1)}, bf16[384,128]{1,0:T(8,128)(2,1)S(1)}, u32[]{:S(2)}, u32[]{:S(2)}) collective-permute-start(bf16[384,128]{1,0:T(8,128)(2,1)S(1)} %get-tuple-element.29), channel_id=1, source_target_pairs={{0,16},{8,24},{16,0},{24,8},{1,17},{9,25},{17,1},{25,9},{2,18},{10... | collective-permute-start | bytes 294920 | tf_op jit(solution)/shard_map/ppermute | solution.py:245
  65.9 0.7 compare_convert_fusion
  66.6 3.1 %collective-permute-done.2.refs_2_ = bf16[384,128]{1,0:T(8,128)(2,1)S(1)} collective-permute-done((bf16[384,128]{1,0:T(8,128)(2,1)S(1)}, bf16[384,128]{1,0:T(8,128)(2,1)S(1)}, u32[]{:S(2)}, u32[]{:S(2)}) %collective-permute-start.2) | collective-permute-done | bytes 98336 | tf_op jit(solution)/shard_map/ppermute | solution.py:245
  69.8 0.7 broadcast_in_dim.13
  70.6 6.6 %all-to-all-start.3 = ((f32[16,32,128]{2,1,0:T(8,128)}), f32[16,32,128]{2,1,0:T(8,128)S(1)}, u32[]{:S(2)}, u32[]{:S(2)}) async-start(f32[16,32,128]{2,1,0:T(8,128)} %broadcast_in_dim.13), calls=%async_computation.3 | async-start | bytes 524288 | tf_op jit(solution)/shard_map/all_to_all | solution.py:199
  77.1 4.5 %collective-permute-start.3 = (bf16[384,128]{1,0:T(8,128)(2,1)S(1)}, bf16[384,128]{1,0:T(8,128)(2,1)S(1)}, u32[]{:S(2)}, u32[]{:S(2)}) collective-permute-start(bf16[384,128]{1,0:T(8,128)(2,1)S(1)} %get-tuple-element.28), channel_id=1, source_target_pairs={{0,24},{8,16},{16,8},{24,0},{1,25},{9,17},{17,9},{25,1},{2,26},{10... | collective-permute-start | bytes 294920 | tf_op jit(solution)/shard_map/ppermute | solution.py:245
  81.7 2.6 %copy.51.partner_slopes = bf16[512,1376]{1,0:T(8,128)(2,1)} copy(bf16[512,1376]{0,1:T(8,128)(2,1)} %collective-permute-done) | data formatting | bytes 2818048 | tf_op jit(solution)/shard_map/ppermute | solution.py:236
  84.2 0.9 fusion.down_hbm
  85.1 1.2 collective-permute-done.3._.refs_3_
  86.3 5.4 %all-gather.3.cloned.1.call-done = bf16[2048,1376]{1,0:T(8,128)(2,1)} async-done(((bf16[64,1376]{1,0:T(8,128)(2,1)}), bf16[2048,1376]{1,0:T(8,128)(2,1)}) %all-gather.3.cloned.1.call-update) | async-done | bytes 5636112 | tf_op jit(solution)/shard_map/all_gather | solution.py:221
  91.7 7.9 %gradient_blocks.1 = f32[32,1,384]{2,1,0:T(1,128)} custom-call(s32[1]{0:T(128)} %bitcast.1.yl_ref, bf16[4,2,2,256,256]{4,3,2,1,0:T(8,128)(2,1)} %bitcast.24, bf16[2,16,64,1376]{3,2,1,0:T(8,128)(2,1)} %bitcast.25, bf16[512,1376]{1,0:T(8,128)(2,1)} %get-tuple-element.20.own_slopes, bf16[512,1376]{1,0:T(8,128)(2,1)} %copy.51.partner_slopes, ...), custom_call_target="tpu_custom_call" | custom-call | flops 2885681152 | bytes 5636096 | tf_op jit(solution)/shard_map/gradient_blocks/pallas_call | solution.py:137
  99.7 14.6 %all_to_all.35 = f32[32,1,384]{2,1,0:T(1,128)S(1)} all-to-all(f32[32,1,384]{2,1,0:T(1,128)} %gradient_blocks.1), channel_id=1, replica_groups=mesh['zh'=8,'zl'=2,'yl'=2,'c'=2,'x'=4,'yh'=2] {'x','yh','yl','c'}, dimensions={0} | all-to-all | bytes 98304 | tf_op jit(solution)/shard_map/all_to_all | solution.py:268
  114.4 20.2 %all_to_all.36 = f32[16,1,384]{2,1,0:T(1,128)} all-to-all(f32[16,1,384]{2,1,0:T(1,128)S(1)} %broadcast_in_dim.14), channel_id=1, replica_groups=mesh['zh'=8,'zl'=2,'yl'=2,'c'=2,'x'=4,'yh'=2] {'zh','zl'}, dimensions={0} | all-to-all | bytes 49152 | tf_op jit(solution)/shard_map/all_to_all | solution.py:199
  134.6 1.9 %score_blocks.1 = f32[32,8,128]{2,1,0:T(8,128)} custom-call(s32[1]{0:T(128)} %bitcast.member_ref, f32[8,2,1,384]{3,2,1,0:T(1,128)} %bitcast.33, bf16[384,128]{1,0:T(8,128)(2,1)} %get-tuple-element.27.refs_0_, bf16[384,128]{1,0:T(8,128)(2,1)} %copy-done.7, bf16[384,128]{1,0:T(8,128)(2,1)} %copy-done.8, bf16[384,128]{1,0:T(8,128)(2,1)} %copy-done.5), custom_call_target="tpu_custom_call" | custom-call | tf_op jit(solution)/shard_map/score_blocks/pallas_call | solution.py:182
  136.5 13.3 %all_to_all.37 = f32[32,8,128]{2,1,0:T(8,128)S(1)} all-to-all(f32[32,8,128]{2,1,0:T(8,128)} %score_blocks.1), channel_id=1, replica_groups=mesh['zh'=8,'zl'=2,'yl'=2,'c'=2,'x'=4,'yh'=2] {'x','yh','yl','c'}, dimensions={0} | all-to-all | bytes 262144 | tf_op jit(solution)/shard_map/all_to_all | solution.py:272
  (38 shorter events, 2.9 us)
Async XLA Ops:
  6.5 85.2 %all-gather.3.cloned.1.call-start = ((), (), s32[]{:S(2)}) async-start(), calls=%async_computation.7 | async-start | bytes 5947392 | tf_op jit(solution)/shard_map/all_gather | solution.py:221
  8.3 6.0 %copy-start.3 = (bf16[256,1376]{0,1:T(8,128)(2,1)S(1)}, bf16[256,1376]{0,1:T(8,128)(2,1)}, u32[]{:S(2)}) copy-start(bf16[256,1376]{0,1:T(8,128)(2,1)} %param.13) | copy-start | bytes 2113540
  8.5 6.2 %copy-start.4 = (bf16[256,1376]{0,1:T(8,128)(2,1)S(1)}, bf16[256,1376]{0,1:T(8,128)(2,1)}, u32[]{:S(2)}) copy-start(bf16[256,1376]{0,1:T(8,128)(2,1)} %param.14) | copy-start | bytes 2113540
  9.4 13.0 %all-to-all-start = ((bf16[4,256,256]{2,1,0:T(8,128)(2,1)}), bf16[4,256,256]{2,1,0:T(8,128)(2,1)S(1)}, u32[]{:S(2)}, u32[]{:S(2)}) async-start(bf16[4,256,256]{2,1,0:T(8,128)(2,1)} %bitcast.5), calls=%async_computation | async-start | bytes 1048576 | tf_op jit(solution)/shard_map/all_to_all | solution.py:227
  14.4 2.2 %copy-start.9 = (bf16[512,64]{0,1:T(8,128)(2,1)S(1)}, bf16[512,64]{0,1:T(8,128)(2,1)}, u32[]{:S(2)}) copy-start(bf16[512,64]{0,1:T(8,128)(2,1)} %param.19) | copy-start | bytes 196612
  14.7 0.9 copy-start.6
  23.9 5.5 %copy-start.1 = (bf16[512,1376]{1,0:T(8,128)(2,1)S(1)}, bf16[512,1376]{1,0:T(8,128)(2,1)}, u32[]{:S(2)}) copy-start(bf16[512,1376]{1,0:T(8,128)(2,1)} %get-tuple-element.20.own_slopes) | copy-start | bytes 4227076
  23.9 28.2 %all-to-all-start.1 = ((bf16[4,4,256,256]{3,2,1,0:T(8,128)(2,1)}), bf16[4,4,256,256]{3,2,1,0:T(8,128)(2,1)S(1)}, u32[]{:S(2)}, u32[]{:S(2)}) async-start(bf16[4,4,256,256]{3,2,1,0:T(8,128)(2,1)} %broadcast_in_dim.12), calls=%async_computation.1 | async-start | bytes 4194304 | tf_op jit(solution)/shard_map/all_to_all | solution.py:234
  30.9 34.3 %copy-start.10 = (s32[8]{0:T(128)S(1)}, s32[8]{0:T(128)}, u32[]{:S(2)}) copy-start(s32[8]{0:T(128)} %param.21) | copy-start | bytes 100
  30.9 50.7 %collective-permute-start = (bf16[512,1376]{0,1:T(8,128)(2,1)}, bf16[512,1376]{0,1:T(8,128)(2,1)}, u32[]{:S(2)}, u32[]{:S(2)}) collective-permute-start(bf16[512,1376]{0,1:T(8,128)(2,1)} %copy.47), channel_id=1, source_target_pairs={{0,16},{16,0},{1,17},{17,1},{2,18},{18,2},{3,19},{19,3},{4,20},{20... | collective-permute-start | bytes 4227080 | tf_op jit(solution)/shard_map/ppermute | solution.py:236
  52.1 32.1 %copy-start = (bf16[4,4,256,256]{3,2,1,0:T(8,128)(2,1)}, bf16[4,4,256,256]{3,2,1,0:T(8,128)(2,1)S(1)}, u32[]{:S(2)}) copy-start(bf16[4,4,256,256]{3,2,1,0:T(8,128)(2,1)S(1)} %all-to-all-done.1) | copy-start | bytes 6291460
  52.1 14.4 %all-to-all-start.2 = ((f32[8,32,256]{2,1,0:T(8,128)}), f32[8,32,256]{2,1,0:T(8,128)S(1)}, u32[]{:S(2)}, u32[]{:S(2)}) async-start(f32[8,32,256]{2,1,0:T(8,128)} %bitcast.31), calls=%async_computation.2 | async-start | bytes 524288 | tf_op jit(solution)/shard_map/all_to_all | solution.py:251
  56.2 10.4 %collective-permute-start.1 = (bf16[384,128]{1,0:T(8,128)(2,1)S(1)}, bf16[384,128]{1,0:T(8,128)(2,1)S(1)}, u32[]{:S(2)}, u32[]{:S(2)}) collective-permute-start(bf16[384,128]{1,0:T(8,128)(2,1)S(1)} %get-tuple-element.30), channel_id=1, source_target_pairs={{0,8},{8,0},{16,24},{24,16},{1,9},{9,1},{17,25},{25,17},{2,10},{10... | collective-permute-start | bytes 294920 | tf_op jit(solution)/shard_map/ppermute | solution.py:245
  63.0 6.8 %collective-permute-start.2 = (bf16[384,128]{1,0:T(8,128)(2,1)S(1)}, bf16[384,128]{1,0:T(8,128)(2,1)S(1)}, u32[]{:S(2)}, u32[]{:S(2)}) collective-permute-start(bf16[384,128]{1,0:T(8,128)(2,1)S(1)} %get-tuple-element.29), channel_id=1, source_target_pairs={{0,16},{8,24},{16,0},{24,8},{1,17},{9,25},{17,1},{25,9},{2,18},{10... | collective-permute-start | bytes 294920 | tf_op jit(solution)/shard_map/ppermute | solution.py:245
  66.6 17.6 %copy-start.7 = (bf16[384,128]{1,0:T(8,128)(2,1)}, bf16[384,128]{1,0:T(8,128)(2,1)S(1)}, u32[]{:S(2)}) copy-start(bf16[384,128]{1,0:T(8,128)(2,1)S(1)} %collective-permute-done.1.refs_1_) | copy-start | bytes 294916
  69.8 14.5 %copy-start.8 = (bf16[384,128]{1,0:T(8,128)(2,1)}, bf16[384,128]{1,0:T(8,128)(2,1)S(1)}, u32[]{:S(2)}) copy-start(bf16[384,128]{1,0:T(8,128)(2,1)S(1)} %collective-permute-done.2.refs_2_) | copy-start | bytes 294916
  70.6 15.7 %all-to-all-start.3 = ((f32[16,32,128]{2,1,0:T(8,128)}), f32[16,32,128]{2,1,0:T(8,128)S(1)}, u32[]{:S(2)}, u32[]{:S(2)}) async-start(f32[16,32,128]{2,1,0:T(8,128)} %broadcast_in_dim.13), calls=%async_computation.3 | async-start | bytes 524288 | tf_op jit(solution)/shard_map/all_to_all | solution.py:199
  77.1 9.1 %collective-permute-start.3 = (bf16[384,128]{1,0:T(8,128)(2,1)S(1)}, bf16[384,128]{1,0:T(8,128)(2,1)S(1)}, u32[]{:S(2)}, u32[]{:S(2)}) collective-permute-start(bf16[384,128]{1,0:T(8,128)(2,1)S(1)} %get-tuple-element.28), channel_id=1, source_target_pairs={{0,24},{8,16},{16,8},{24,0},{1,25},{9,17},{17,9},{25,1},{2,26},{10... | collective-permute-start | bytes 294920 | tf_op jit(solution)/shard_map/ppermute | solution.py:245
  86.3 5.4 %copy-start.5 = (bf16[384,128]{1,0:T(8,128)(2,1)}, bf16[384,128]{1,0:T(8,128)(2,1)S(1)}, u32[]{:S(2)}) copy-start(bf16[384,128]{1,0:T(8,128)(2,1)S(1)} %collective-permute-done.3._.refs_3_) | copy-start | bytes 294916
  86.3 5.4 %copy-start.2 = (f32[16,32,128]{2,1,0:T(8,128)}, f32[16,32,128]{2,1,0:T(8,128)S(1)}, u32[]{:S(2)}) copy-start(f32[16,32,128]{2,1,0:T(8,128)S(1)} %all-to-all-done.3) | copy-start | bytes 786436
Sparse Core Ops, SparseCore 0:
  9.5 82.2 all-gather.2

commit v7 on v6

--- a/solution.py
+++ b/solution.py
@@ -1,4 +1,3 @@
-import functools
 import math
 
 import jax
@@ -161,33 +160,6 @@
     )(yl, blocks, weight, own_slopes, partner_slopes, proj, proj_x, block_d, arrival)
 
 
-def score_kernel(scale, member_ref, rows_ref, *refs):
-    *query_refs, out_ref = refs
-    copies, sessions, _ = out_ref.shape
-    groups = len(query_refs)
-    left = (rows_ref[:, 0] + rows_ref[:, 1]).reshape(sessions, -1)
-    terms = []
-    for _ in range(3):
-        terms.append(left.astype(jnp.bfloat16).astype(jnp.float32))
-        left = left - terms[-1]
-    terms = jnp.concatenate(terms, axis=0).astype(jnp.bfloat16)
-    for flip, query_ref in enumerate(query_refs):
-        products = dot(terms, query_ref[...])
-        scores = products[:sessions] + (products[sessions : 2 * sessions] + products[2 * sessions :])
-        for i in range(0, copies, groups):
-            out_ref[i + (member_ref[0] ^ flip)] = scores * scale
-
-
-def score_blocks(member, rows, queries, copies, scale):
-    return pl.pallas_call(
-        functools.partial(score_kernel, scale),
-        out_shape=jax.ShapeDtypeStruct((copies, rows.shape[0], queries[0].shape[1]), jnp.float32),
-        in_specs=[pl.BlockSpec(memory_space=pltpu.SMEM)] + [VMEM] * (1 + len(queries)),
-        out_specs=VMEM,
-        name="score_blocks",
-    )(member, rows, *queries)
-
-
 def outer(a, b):
     return lax.dot_general(
         a, b, (((0,), (0,)), ((), ())), precision=HIGHEST, preferred_element_type=jnp.float32
@@ -268,8 +240,14 @@
     entries = lax.all_to_all(blocks, SHARE, 0, 0).sum(axis=0)
     entries = give_all(entries, ("zh", "zl"))
     entries = entries.reshape(-1, lax.axis_size("zl"), *entries.shape[1:])
-    partial_scores = score_blocks(member.reshape(1), entries, arrivals, members, 1.0 / math.sqrt(LEN))
-    return lax.all_to_all(partial_scores, SHARE, 0, 0).sum(axis=0)
+    for bit in (1, 2):
+        arrivals = [jnp.where(member & bit, arrivals[i ^ bit], arrivals[i]) for i in range(groups)]
+    ordered = jnp.concatenate([arrivals[i] for i in (0, 2, 1, 3)], axis=1)
+    partial_scores = jnp.dot(entries.sum(axis=1)[:, 0], ordered.astype(jnp.float32), precision=HIGHEST) * (1.0 / math.sqrt(LEN))
+    partial_scores = partial_scores.reshape(-1, groups, queries.shape[0]).transpose(1, 0, 2)[:, None]
+    partial_scores = jnp.broadcast_to(partial_scores, (groups, tensor_size) + partial_scores.shape[2:])
+    partial_scores = partial_scores.reshape(members, *partial_scores.shape[2:])
+    return lax.all_to_all(partial_scores, ("c", "yl", "yh", "x"), 0, 0).sum(axis=0)
 
 
 def solution(mesh):

time: 158 us -> 156 us (0.987)
  blocking collectives: 48.1 us -> 12.5 us
  waiting for transfers between devices: 28.3 us -> 47 us
  starting transfers between devices: 36.1 us -> 52.3 us
  Pallas kernels: 13.7 us -> 11.7 us
    all_to_all x3 -> x1, blocking collectives: 48.1 us -> 12.5 us  [on_device(): lax.all_to_all(partial_scores, ('c', 'yl', 'yh', 'x'), 0, 0).sum(axis=0)]
    all_to_all x1 -> x2, waiting for transfers between devices: 0.01 us -> 10.5 us  [give_all(): lax.all_to_all(jnp.broadcast_to(block[None], (n,) + block.shape), axes, 0...]
    all_to_all x1 -> x2, starting transfers between devices: 6.57 us -> 15.7 us  [give_all(): lax.all_to_all(jnp.broadcast_to(block[None], (n,) + block.shape), axes, 0...]
    all_to_all x0 -> x1, waiting for transfers between devices: none -> 7.3 us  [on_device(): entries = lax.all_to_all(blocks, SHARE, 0, 0).sum(axis=0)]
    all_to_all x0 -> x1, starting transfers between devices: none -> 7.22 us  [on_device(): entries = lax.all_to_all(blocks, SHARE, 0, 0).sum(axis=0)]
    pallas_call x1 -> x0, Pallas kernels: 1.95 us -> none  [score_blocks(): pl.pallas_call(functools.partial(score_kernel, scale), out_shape=jax.Shap...]
    unnamed x27 -> x23, local copies, waits for them, and re-layouts: 4.05 us -> 3.7 us
  transfers between devices with their start and end apart: 9 -> 11, of which waited for: 4 -> 6; matrix products, arithmetic and copies ran while one was open for 10% -> 11% of each run, Pallas kernels for 2% -> 2%
where the time goes in v7:
time: 156 us; the launch traced here: 155 us
  starting transfers between devices  52.3 us (34%)
  waiting for transfers between devices  47 us (30%)
  between operations  13.7 us (9%)
  local copies, waits for them, and re-layouts  13.6 us (9%)
  blocking collectives  12.5 us (8%)
  Pallas kernels  11.7 us (8%)
  other arithmetic  3.62 us (2%)
    all_to_all x1, waiting for transfers between devices, on_device(): lax.all_to_all(along_y, 'x', 0, 0)  18.1 us
    all_to_all x2, starting transfers between devices, give_all(): lax.all_to_all(jnp.broadcast_to(block[None], (n,) + block.shape), axes, 0...  15.7 us
    ppermute x3, starting transfers between devices, on_device(): arrivals.append(lax.ppermute(piece, QUERY_GROUP, pairs) if flip else piece)  13.1 us
    all_to_all x1, blocking collectives, on_device(): lax.all_to_all(partial_scores, ('c', 'yl', 'yh', 'x'), 0, 0).sum(axis=0)  12.5 us
    all_to_all x2, waiting for transfers between devices, give_all(): lax.all_to_all(jnp.broadcast_to(block[None], (n,) + block.shape), axes, 0...  10.5 us
    pallas_call x1, Pallas kernels, gradient_blocks(): pl.pallas_call(gradient_kernel, out_shape=jax.ShapeDtypeStruct((members,...  7.93 us
    all_to_all x1, waiting for transfers between devices, on_device(): entries = lax.all_to_all(blocks, SHARE, 0, 0).sum(axis=0)  7.3 us
    all_to_all x1, starting transfers between devices, on_device(): entries = lax.all_to_all(blocks, SHARE, 0, 0).sum(axis=0)  7.22 us
  transfers between devices with their start and end apart: 11, of which 6 were waited for; matrix products, arithmetic and copies ran while one was open for 11% of the time, Pallas kernels for 2%

profile of v7, /device:TPU:1, one launch (start us, length us, event | category | flops | bytes accessed | tf_op | source)
XLA Modules:
  0.0 155.5 jit_solution(4369989473314179150)
XLA Ops:
  6.5 0.7 all-gather.3.cloned.1.call-update
  7.3 1.1 copy.84
  8.5 0.8 broadcast_in_dim.13
  9.4 5.0 %all-to-all-start = ((bf16[4,256,256]{2,1,0:T(8,128)(2,1)}), bf16[4,256,256]{2,1,0:T(8,128)(2,1)S(1)}, u32[]{:S(2)}, u32[]{:S(2)}) async-start(bf16[4,256,256]{2,1,0:T(8,128)(2,1)} %bitcast.4), calls=%async_computation | async-start | bytes 1048576 | tf_op jit(solution)/shard_map/all_to_all | solution.py:199
  15.3 0.9 copy.82.hid_proj_ref
  16.2 0.8 copy.83.out_proj_ref
  17.0 1.3 pad_maximum_fusion.pre_ref
  18.2 3.8 %local_terms.1 = (bf16[512,1376]{1,0:T(8,128)(2,1)}, f32[256,256]{1,0:T(8,128)}) custom-call(bf16[512,1376]{1,0:T(8,128)(2,1)} %pad_maximum_fusion.pre_ref, bf16[256,512]{1,0:T(8,128)(2,1)} %in_ref.1, bf16[512,128]{1,0:T(8,128)(2,1)} %in_proj_ref.1, bf16[1376,64]{1,0:T(8,128)(2,1)} %copy.82.hid_proj_ref, bf16[256,512]{1,0:T(8,128)(2,1)} %cot_ref.1, ...), custom_call_target="tpu_custom_call" | custom-call | flops 281804800 | bytes 2818048 | tf_op jit(solution)/shard_map/local_terms/pallas_call | solution.py:51
  22.0 1.5 broadcast_in_dim.14
  23.5 5.8 %all-to-all-start.1 = ((bf16[4,4,256,256]{3,2,1,0:T(8,128)(2,1)}), bf16[4,4,256,256]{3,2,1,0:T(8,128)(2,1)S(1)}, u32[]{:S(2)}, u32[]{:S(2)}) async-start(bf16[4,4,256,256]{3,2,1,0:T(8,128)(2,1)} %broadcast_in_dim.14), calls=%async_computation.1 | async-start | bytes 4194304 | tf_op jit(solution)/shard_map/all_to_all | solution.py:206
  29.3 1.6 %copy.87 = bf16[512,1376]{0,1:T(8,128)(2,1)} copy(bf16[512,1376]{1,0:T(8,128)(2,1)S(1)} %copy-done.1) | data formatting | bytes 2818048 | tf_op jit(solution)/shard_map/optimization_barrier | solution.py:205
  30.9 2.0 %collective-permute-start = (bf16[512,1376]{0,1:T(8,128)(2,1)}, bf16[512,1376]{0,1:T(8,128)(2,1)}, u32[]{:S(2)}, u32[]{:S(2)}) collective-permute-start(bf16[512,1376]{0,1:T(8,128)(2,1)} %copy.87), channel_id=1, source_target_pairs={{0,16},{16,0},{1,17},{17,1},{2,18},{18,2},{3,19},{19,3},{4,20},{20... | collective-permute-start | bytes 4227080 | tf_op jit(solution)/shard_map/ppermute | solution.py:208
  33.0 1.2 copy.94
  34.2 18.1 %all-to-all-done.1 = bf16[4,4,256,256]{3,2,1,0:T(8,128)(2,1)S(1)} async-done(((bf16[4,4,256,256]{3,2,1,0:T(8,128)(2,1)}), bf16[4,4,256,256]{3,2,1,0:T(8,128)(2,1)S(1)}, u32[]{:S(2)}, u32[]{:S(2)}) %all-to-all-start.1) | async-done | bytes 2097184 | tf_op jit(solution)/shard_map/all_to_all | solution.py:206
  52.3 3.4 %all-to-all-start.2 = ((f32[8,32,256]{2,1,0:T(8,128)}), f32[8,32,256]{2,1,0:T(8,128)S(1)}, u32[]{:S(2)}, u32[]{:S(2)}) async-start(f32[8,32,256]{2,1,0:T(8,128)} %bitcast.46), calls=%async_computation.2 | async-start | bytes 524288 | tf_op jit(solution)/shard_map/all_to_all | solution.py:223
  55.8 6.2 %collective-permute-start.1 = (bf16[384,128]{1,0:T(8,128)(2,1)S(1)}, bf16[384,128]{1,0:T(8,128)(2,1)S(1)}, u32[]{:S(2)}, u32[]{:S(2)}) collective-permute-start(bf16[384,128]{1,0:T(8,128)(2,1)S(1)} %get-tuple-element.33), channel_id=1, source_target_pairs={{0,8},{8,0},{16,24},{24,16},{1,9},{9,1},{17,25},{25,17},{2,10},{10... | collective-permute-start | bytes 294920 | tf_op jit(solution)/shard_map/ppermute | solution.py:217
  62.0 2.2 %collective-permute-start.2 = (bf16[384,128]{1,0:T(8,128)(2,1)S(1)}, bf16[384,128]{1,0:T(8,128)(2,1)S(1)}, u32[]{:S(2)}, u32[]{:S(2)}) collective-permute-start(bf16[384,128]{1,0:T(8,128)(2,1)S(1)} %get-tuple-element.32), channel_id=1, source_target_pairs={{0,16},{8,24},{16,0},{24,8},{1,17},{9,25},{17,1},{25,9},{2,18},{10... | collective-permute-start | bytes 294920 | tf_op jit(solution)/shard_map/ppermute | solution.py:217
  65.5 3.4 %collective-permute-done.2 = bf16[384,128]{1,0:T(8,128)(2,1)S(1)} collective-permute-done((bf16[384,128]{1,0:T(8,128)(2,1)S(1)}, bf16[384,128]{1,0:T(8,128)(2,1)S(1)}, u32[]{:S(2)}, u32[]{:S(2)}) %collective-permute-start.2) | collective-permute-done | bytes 98336 | tf_op jit(solution)/shard_map/ppermute | solution.py:217
  69.0 0.7 broadcast_in_dim.15
  69.7 6.9 %all-to-all-start.3 = ((f32[16,32,128]{2,1,0:T(8,128)}), f32[16,32,128]{2,1,0:T(8,128)S(1)}, u32[]{:S(2)}, u32[]{:S(2)}) async-start(f32[16,32,128]{2,1,0:T(8,128)} %broadcast_in_dim.15), calls=%async_computation.3 | async-start | bytes 524288 | tf_op jit(solution)/shard_map/all_to_all | solution.py:171
  76.7 4.7 %collective-permute-start.3 = (bf16[384,128]{1,0:T(8,128)(2,1)S(1)}, bf16[384,128]{1,0:T(8,128)(2,1)S(1)}, u32[]{:S(2)}, u32[]{:S(2)}) collective-permute-start(bf16[384,128]{1,0:T(8,128)(2,1)S(1)} %get-tuple-element.31), channel_id=1, source_target_pairs={{0,24},{8,16},{16,8},{24,0},{1,25},{9,17},{17,9},{25,1},{2,26},{10... | collective-permute-start | bytes 294920 | tf_op jit(solution)/shard_map/ppermute | solution.py:217
  81.3 2.6 %copy.91.partner_slopes = bf16[512,1376]{1,0:T(8,128)(2,1)} copy(bf16[512,1376]{0,1:T(8,128)(2,1)} %collective-permute-done) | data formatting | bytes 2818048 | tf_op jit(solution)/shard_map/ppermute | solution.py:208
  83.9 0.9 fusion.8.down_hbm
  84.8 1.1 collective-permute-done.3._
  85.9 5.8 %all-gather.3.cloned.1.call-done = bf16[2048,1376]{1,0:T(8,128)(2,1)} async-done(((bf16[64,1376]{1,0:T(8,128)(2,1)}), bf16[2048,1376]{1,0:T(8,128)(2,1)}) %all-gather.3.cloned.1.call-update) | async-done | bytes 5636112 | tf_op jit(solution)/shard_map/all_gather | solution.py:193
  91.7 7.9 %gradient_blocks.1 = f32[32,1,384]{2,1,0:T(1,128)} custom-call(s32[1]{0:T(128)} %bitcast.yl_ref, bf16[4,2,2,256,256]{4,3,2,1,0:T(8,128)(2,1)} %bitcast.37, bf16[2,16,64,1376]{3,2,1,0:T(8,128)(2,1)} %bitcast.38, bf16[512,1376]{1,0:T(8,128)(2,1)} %get-tuple-element.20.own_slopes, bf16[512,1376]{1,0:T(8,128)(2,1)} %copy.91.partner_slopes, ...), custom_call_target="tpu_custom_call" | custom-call | flops 2885681152 | bytes 5636096 | tf_op jit(solution)/shard_map/gradient_blocks/pallas_call | solution.py:136
  99.7 7.2 %all-to-all-start.4 = ((f32[32,1,384]{2,1,0:T(1,128)}), f32[32,1,384]{2,1,0:T(1,128)S(1)}, u32[]{:S(2)}, u32[]{:S(2)}) async-start(f32[32,1,384]{2,1,0:T(1,128)} %gradient_blocks.1), calls=%async_computation.4 | async-start | bytes 98304 | tf_op jit(solution)/shard_map/all_to_all | solution.py:240
  106.9 7.3 %all-to-all-done.4 = f32[32,1,384]{2,1,0:T(1,128)S(1)} async-done(((f32[32,1,384]{2,1,0:T(1,128)}), f32[32,1,384]{2,1,0:T(1,128)S(1)}, u32[]{:S(2)}, u32[]{:S(2)}) %all-to-all-start.4) | async-done | bytes 49184 | tf_op jit(solution)/shard_map/all_to_all | solution.py:240
  114.9 8.8 %all-to-all-start.5 = ((f32[16,1,384]{2,1,0:T(1,128)}), f32[16,1,384]{2,1,0:T(1,128)S(1)}, u32[]{:S(2)}, u32[]{:S(2)}) async-start(f32[16,1,384]{2,1,0:T(1,128)} %broadcast_in_dim.16), calls=%async_computation.5 | async-start | bytes 49152 | tf_op jit(solution)/shard_map/all_to_all | solution.py:171
  123.7 0.9 broadcast_select_fusion.5
  124.6 10.5 %all-to-all-done.5 = f32[16,1,384]{2,1,0:T(1,128)S(1)} async-done(((f32[16,1,384]{2,1,0:T(1,128)}), f32[16,1,384]{2,1,0:T(1,128)S(1)}, u32[]{:S(2)}, u32[]{:S(2)}) %all-to-all-start.5) | async-done | bytes 24608 | tf_op jit(solution)/shard_map/all_to_all | solution.py:171
  135.5 12.5 %all_to_all.35 = f32[32,8,128]{2,1,0:T(8,128)S(1)} all-to-all(f32[32,8,128]{2,1,0:T(8,128)S(1)} %bitcast.44), channel_id=1, replica_groups=mesh['zh'=8,'zl'=2,'yl'=2,'c'=2,'x'=4,'yh'=2] {'c','yl','yh','x'}, dimensions={0} | all-to-all | bytes 262144 | tf_op jit(solution)/shard_map/all_to_all | solution.py:250
  (41 shorter events, 4.1 us)
Async XLA Ops:
  6.5 85.2 %all-gather.3.cloned.1.call-start = ((), (), s32[]{:S(2)}) async-start(), calls=%async_computation.7 | async-start | bytes 5947392 | tf_op jit(solution)/shard_map/all_gather | solution.py:193
  8.3 6.0 %copy-start.3 = (bf16[256,1376]{0,1:T(8,128)(2,1)S(1)}, bf16[256,1376]{0,1:T(8,128)(2,1)}, u32[]{:S(2)}) copy-start(bf16[256,1376]{0,1:T(8,128)(2,1)} %param.13) | copy-start | bytes 2113540
  8.5 6.2 %copy-start.4 = (bf16[256,1376]{0,1:T(8,128)(2,1)S(1)}, bf16[256,1376]{0,1:T(8,128)(2,1)}, u32[]{:S(2)}) copy-start(bf16[256,1376]{0,1:T(8,128)(2,1)} %param.14) | copy-start | bytes 2113540
  9.4 12.7 %all-to-all-start = ((bf16[4,256,256]{2,1,0:T(8,128)(2,1)}), bf16[4,256,256]{2,1,0:T(8,128)(2,1)S(1)}, u32[]{:S(2)}, u32[]{:S(2)}) async-start(bf16[4,256,256]{2,1,0:T(8,128)(2,1)} %bitcast.4), calls=%async_computation | async-start | bytes 1048576 | tf_op jit(solution)/shard_map/all_to_all | solution.py:199
  14.4 0.9 copy-start.6
  14.4 1.8 %copy-start.7 = (bf16[512,64]{0,1:T(8,128)(2,1)S(1)}, bf16[512,64]{0,1:T(8,128)(2,1)}, u32[]{:S(2)}) copy-start(bf16[512,64]{0,1:T(8,128)(2,1)} %param.19) | copy-start | bytes 196612
  23.5 5.8 %copy-start.1 = (bf16[512,1376]{1,0:T(8,128)(2,1)S(1)}, bf16[512,1376]{1,0:T(8,128)(2,1)}, u32[]{:S(2)}) copy-start(bf16[512,1376]{1,0:T(8,128)(2,1)} %get-tuple-element.20.own_slopes) | copy-start | bytes 4227076
  23.5 28.8 %all-to-all-start.1 = ((bf16[4,4,256,256]{3,2,1,0:T(8,128)(2,1)}), bf16[4,4,256,256]{3,2,1,0:T(8,128)(2,1)S(1)}, u32[]{:S(2)}, u32[]{:S(2)}) async-start(bf16[4,4,256,256]{3,2,1,0:T(8,128)(2,1)} %broadcast_in_dim.14), calls=%async_computation.1 | async-start | bytes 4194304 | tf_op jit(solution)/shard_map/all_to_all | solution.py:206
  30.9 33.4 %copy-start.8 = (s32[8]{0:T(128)S(1)}, s32[8]{0:T(128)}, u32[]{:S(2)}) copy-start(s32[8]{0:T(128)} %param.21) | copy-start | bytes 100
  30.9 50.4 %collective-permute-start = (bf16[512,1376]{0,1:T(8,128)(2,1)}, bf16[512,1376]{0,1:T(8,128)(2,1)}, u32[]{:S(2)}, u32[]{:S(2)}) collective-permute-start(bf16[512,1376]{0,1:T(8,128)(2,1)} %copy.87), channel_id=1, source_target_pairs={{0,16},{16,0},{1,17},{17,1},{2,18},{18,2},{3,19},{19,3},{4,20},{20... | collective-permute-start | bytes 4227080 | tf_op jit(solution)/shard_map/ppermute | solution.py:208
  52.3 31.6 %copy-start = (bf16[4,4,256,256]{3,2,1,0:T(8,128)(2,1)}, bf16[4,4,256,256]{3,2,1,0:T(8,128)(2,1)S(1)}, u32[]{:S(2)}) copy-start(bf16[4,4,256,256]{3,2,1,0:T(8,128)(2,1)S(1)} %all-to-all-done.1) | copy-start | bytes 6291460
  52.3 13.1 %all-to-all-start.2 = ((f32[8,32,256]{2,1,0:T(8,128)}), f32[8,32,256]{2,1,0:T(8,128)S(1)}, u32[]{:S(2)}, u32[]{:S(2)}) async-start(f32[8,32,256]{2,1,0:T(8,128)} %bitcast.46), calls=%async_computation.2 | async-start | bytes 524288 | tf_op jit(solution)/shard_map/all_to_all | solution.py:223
  55.8 9.7 %collective-permute-start.1 = (bf16[384,128]{1,0:T(8,128)(2,1)S(1)}, bf16[384,128]{1,0:T(8,128)(2,1)S(1)}, u32[]{:S(2)}, u32[]{:S(2)}) collective-permute-start(bf16[384,128]{1,0:T(8,128)(2,1)S(1)} %get-tuple-element.33), channel_id=1, source_target_pairs={{0,8},{8,0},{16,24},{24,16},{1,9},{9,1},{17,25},{25,17},{2,10},{10... | collective-permute-start | bytes 294920 | tf_op jit(solution)/shard_map/ppermute | solution.py:217
  62.0 6.9 %collective-permute-start.2 = (bf16[384,128]{1,0:T(8,128)(2,1)S(1)}, bf16[384,128]{1,0:T(8,128)(2,1)S(1)}, u32[]{:S(2)}, u32[]{:S(2)}) collective-permute-start(bf16[384,128]{1,0:T(8,128)(2,1)S(1)} %get-tuple-element.32), channel_id=1, source_target_pairs={{0,16},{8,24},{16,0},{24,8},{1,17},{9,25},{17,1},{25,9},{2,18},{10... | collective-permute-start | bytes 294920 | tf_op jit(solution)/shard_map/ppermute | solution.py:217
  69.7 16.2 %all-to-all-start.3 = ((f32[16,32,128]{2,1,0:T(8,128)}), f32[16,32,128]{2,1,0:T(8,128)S(1)}, u32[]{:S(2)}, u32[]{:S(2)}) async-start(f32[16,32,128]{2,1,0:T(8,128)} %broadcast_in_dim.15), calls=%async_computation.3 | async-start | bytes 524288 | tf_op jit(solution)/shard_map/all_to_all | solution.py:171
  76.7 9.3 %collective-permute-start.3 = (bf16[384,128]{1,0:T(8,128)(2,1)S(1)}, bf16[384,128]{1,0:T(8,128)(2,1)S(1)}, u32[]{:S(2)}, u32[]{:S(2)}) collective-permute-start(bf16[384,128]{1,0:T(8,128)(2,1)S(1)} %get-tuple-element.31), channel_id=1, source_target_pairs={{0,24},{8,16},{16,8},{24,0},{1,25},{9,17},{17,9},{25,1},{2,26},{10... | collective-permute-start | bytes 294920 | tf_op jit(solution)/shard_map/ppermute | solution.py:217
  85.9 5.8 %copy-start.5 = (bf16[384,128]{1,0:T(8,128)(2,1)}, bf16[384,128]{1,0:T(8,128)(2,1)S(1)}, u32[]{:S(2)}) copy-start(bf16[384,128]{1,0:T(8,128)(2,1)S(1)} %collective-permute-done.3._) | copy-start | bytes 294916
  85.9 5.8 %copy-start.2 = (f32[16,32,128]{2,1,0:T(8,128)}, f32[16,32,128]{2,1,0:T(8,128)S(1)}, u32[]{:S(2)}) copy-start(f32[16,32,128]{2,1,0:T(8,128)S(1)} %all-to-all-done.3) | copy-start | bytes 786436
  99.7 14.5 %all-to-all-start.4 = ((f32[32,1,384]{2,1,0:T(1,128)}), f32[32,1,384]{2,1,0:T(1,128)S(1)}, u32[]{:S(2)}, u32[]{:S(2)}) async-start(f32[32,1,384]{2,1,0:T(1,128)} %gradient_blocks.1), calls=%async_computation.4 | async-start | bytes 98304 | tf_op jit(solution)/shard_map/all_to_all | solution.py:240
  114.9 20.2 %all-to-all-start.5 = ((f32[16,1,384]{2,1,0:T(1,128)}), f32[16,1,384]{2,1,0:T(1,128)S(1)}, u32[]{:S(2)}, u32[]{:S(2)}) async-start(f32[16,1,384]{2,1,0:T(1,128)} %broadcast_in_dim.16), calls=%async_computation.5 | async-start | bytes 49152 | tf_op jit(solution)/shard_map/all_to_all | solution.py:171
Sparse Core Ops, SparseCore 0:
  9.5 82.2 all-gather.2

commit v8 on v7

--- a/solution.py
+++ b/solution.py
@@ -14,7 +14,7 @@
 DP = ("zh", "zl", "yl", "c")
 TENSOR = ("x", "yh")
 QUERY_GROUP = ("yl", "c")
-SHARE = TENSOR + QUERY_GROUP
+SHARE = ("c", "yl", "yh", "x")
 SWAP = [(0, 1), (1, 0)]
 HIGHEST = lax.Precision.HIGHEST
 VMEM = pl.BlockSpec(memory_space=pltpu.VMEM)
@@ -25,8 +25,9 @@
 
 
 def local_kernel(pre_ref, in_ref, in_proj_ref, hid_proj_ref, cot_ref, out_proj_ref, slopes_ref, parts_ref, hidden_ref):
-    rows = hidden_ref.shape[0]
+    rows, hid = hidden_ref.shape
     rank = out_proj_ref.shape[1]
+    slopes_ref[:, hid:] = jnp.zeros((2 * rows, slopes_ref.shape[1] - hid), jnp.bfloat16)
 
     def some_rows(step, _):
         first = pl.multiple_of(step * STEP, STEP)
@@ -35,8 +36,8 @@
         up = pre_ref[below, :].astype(jnp.float32)
         sig = 1.0 / (1.0 + jnp.exp(-gate))
         silu = gate * sig
-        slopes_ref[above, :] = (up * sig * (1.0 + gate * (1.0 - sig))).astype(jnp.bfloat16)
-        slopes_ref[below, :] = silu.astype(jnp.bfloat16)
+        slopes_ref[above, :hid] = (up * sig * (1.0 + gate * (1.0 - sig))).astype(jnp.bfloat16)
+        slopes_ref[below, :hid] = silu.astype(jnp.bfloat16)
         hidden_ref[above, :] = (silu * up).astype(jnp.bfloat16)
         return 0
 
@@ -51,7 +52,7 @@
     return pl.pallas_call(
         local_kernel,
         out_shape=(
-            jax.ShapeDtypeStruct((2 * rows, hid), jnp.bfloat16),
+            jax.ShapeDtypeStruct((2 * rows, -(-hid // 128) * 128), jnp.bfloat16),
             jax.ShapeDtypeStruct((rows, 4 * proj_out_d.shape[1]), jnp.float32),
         ),
         in_specs=[VMEM] * 6,
@@ -112,8 +113,8 @@
     grad = total[...] + term
     for copy in of_slopes:
         copy.wait()
-    gate_sum = dot((grad * slope[...].astype(jnp.float32)).astype(jnp.bfloat16), proj_ref[...])
-    up_sum = dot((grad * silu[...].astype(jnp.float32)).astype(jnp.bfloat16), proj_ref[...])
+    gate_sum = dot((grad * slope[:, :hid].astype(jnp.float32)).astype(jnp.bfloat16), proj_ref[...])
+    up_sum = dot((grad * silu[:, :hid].astype(jnp.float32)).astype(jnp.bfloat16), proj_ref[...])
     lane = lax.broadcasted_iota(jnp.int32, gate_sum.shape, 1)
     both = jnp.where(lane < rank, gate_sum, up_sum)
     square = outer(x_ref[yl], both[:events]) + outer(x_ref[1 - yl], both[events:])
@@ -123,15 +124,19 @@
     rows_ref[:, rank:] = jnp.zeros_like(rows_ref[:, rank:])
     members = out_ref.shape[0]
     each = rows_ref.shape[0] // members
-    for i in range(each):
-        row = rows_ref[pl.ds(i, members, stride=each), :]
-        out_ref[:, :, i * rank : (i + 1) * rank] = row[:, None, :rank]
+    for group in range(members // across):
+        core, low, high = group // 4, group // 2 % 2, group % 2
+        first = high * 4 + low * 2 + core
+        for i in range(each):
+            row = rows_ref[pl.ds(first * each + i, across, stride=members // across * each), :]
+            out_ref[group * across : (group + 1) * across, :, i * rank : (i + 1) * rank] = row[:, None, :rank]
 
 
 def gradient_blocks(yl, blocks, weight, own_slopes, partner_slopes, proj, proj_x, block_d, arrival, members):
     rank = block_d.shape[0]
     cores, layers, features, hid = weight.shape
     rows, depth = 2 * blocks.shape[3], cores * layers * features
+    padded = own_slopes.shape[1]
     anywhere = pl.BlockSpec(memory_space=pl.ANY)
     return pl.pallas_call(
         gradient_kernel,
@@ -141,8 +146,8 @@
         scratch_shapes=[
             pltpu.VMEM((rows, depth), jnp.bfloat16),
             pltpu.VMEM((layers, cores, features, hid), jnp.bfloat16),
-            pltpu.VMEM((rows, hid), jnp.bfloat16),
-            pltpu.VMEM((rows, hid), jnp.bfloat16),
+            pltpu.VMEM((rows, padded), jnp.bfloat16),
+            pltpu.VMEM((rows, padded), jnp.bfloat16),
             pltpu.VMEM(proj.shape, jnp.bfloat16),
             pltpu.VMEM(proj_x.shape, jnp.float32),
             pltpu.VMEM(block_d.shape, jnp.float32),
@@ -247,7 +252,7 @@
     partial_scores = partial_scores.reshape(-1, groups, queries.shape[0]).transpose(1, 0, 2)[:, None]
     partial_scores = jnp.broadcast_to(partial_scores, (groups, tensor_size) + partial_scores.shape[2:])
     partial_scores = partial_scores.reshape(members, *partial_scores.shape[2:])
-    return lax.all_to_all(partial_scores, ("c", "yl", "yh", "x"), 0, 0).sum(axis=0)
+    return lax.all_to_all(partial_scores, SHARE, 0, 0).sum(axis=0)
 
 
 def solution(mesh):

time: 156 us -> 156 us (level)
  waiting for transfers between devices: 47 us -> 52.5 us
  local copies, waits for them, and re-layouts: 13.6 us -> 8.28 us
    ppermute x3, waiting for transfers between devices: 4.57 us -> 7.31 us  [on_device(): arrivals.append(lax.ppermute(piece, QUERY_GROUP, pairs) if flip else piece)]
    all_to_all x1, waiting for transfers between devices: 18.1 us -> 20.8 us  [on_device(): lax.all_to_all(along_y, 'x', 0, 0)]
    ppermute x1 -> x0, local copies, waits for them, and re-layouts: 2.57 us -> none  [on_device(): partner_slopes = lax.ppermute(own_slopes, 'yl', SWAP)]
    optimization_barrier x1 -> x0, local copies, waits for them, and re-layouts: 1.57 us -> none  [on_device(): along_y, own_slopes = lax.optimization_barrier((along_y, own_slopes))]
  transfers between devices with their start and end apart: 11 -> 11, of which waited for: 6 -> 6; matrix products, arithmetic and copies ran while one was open for 11% -> 7% of each run, Pallas kernels for 2% -> 2%
where the time goes in v8:
time: 156 us; the launch traced here: 155 us
  waiting for transfers between devices  52.5 us (34%)
  starting transfers between devices  51 us (33%)
  between operations  13.7 us (9%)
  blocking collectives  12.8 us (8%)
  Pallas kernels  11.8 us (8%)
  local copies, waits for them, and re-layouts  8.28 us (5%)
  other arithmetic  3.74 us (2%)
    all_to_all x1, waiting for transfers between devices, on_device(): lax.all_to_all(along_y, 'x', 0, 0)  20.8 us
    all_to_all x2, starting transfers between devices, give_all(): lax.all_to_all(jnp.broadcast_to(block[None], (n,) + block.shape), axes, 0...  14.7 us
    all_to_all x1, blocking collectives, on_device(): return lax.all_to_all(partial_scores, SHARE, 0, 0).sum(axis=0)  12.8 us
    ppermute x3, starting transfers between devices, on_device(): arrivals.append(lax.ppermute(piece, QUERY_GROUP, pairs) if flip else piece)  12.7 us
    all_to_all x2, waiting for transfers between devices, give_all(): lax.all_to_all(jnp.broadcast_to(block[None], (n,) + block.shape), axes, 0...  10.5 us
    pallas_call x1, Pallas kernels, gradient_blocks(): pl.pallas_call(gradient_kernel, out_shape=jax.ShapeDtypeStruct((members,...  7.95 us
    ppermute x3, waiting for transfers between devices, on_device(): arrivals.append(lax.ppermute(piece, QUERY_GROUP, pairs) if flip else piece)  7.31 us
    all_to_all x1, starting transfers between devices, on_device(): entries = lax.all_to_all(blocks, SHARE, 0, 0).sum(axis=0)  7.2 us
  transfers between devices with their start and end apart: 11, of which 6 were waited for; matrix products, arithmetic and copies ran while one was open for 7% of the time, Pallas kernels for 2%

profile of v8, /device:TPU:1, one launch (start us, length us, event | category | flops | bytes accessed | tf_op | source)
XLA Modules:
  0.0 154.9 jit_solution(6258940506776618902)
XLA Ops:
  6.5 0.7 all-gather.3.cloned.1.call-update
  7.3 1.1 copy.67
  8.5 0.8 broadcast_in_dim.13
  9.4 5.1 %all-to-all-start = ((bf16[4,256,256]{2,1,0:T(8,128)(2,1)}), bf16[4,256,256]{2,1,0:T(8,128)(2,1)S(1)}, u32[]{:S(2)}, u32[]{:S(2)}) async-start(bf16[4,256,256]{2,1,0:T(8,128)(2,1)} %bitcast.4), calls=%async_computation | async-start | bytes 1048576 | tf_op jit(solution)/shard_map/all_to_all | solution.py:204
  15.2 0.9 copy.65.hid_proj_ref
  16.1 0.8 copy.66.out_proj_ref
  16.9 1.3 pad_maximum_fusion.pre_ref
  18.1 3.9 %local_terms.1 = (bf16[512,1408]{1,0:T(8,128)(2,1)}, f32[256,256]{1,0:T(8,128)}) custom-call(bf16[512,1376]{1,0:T(8,128)(2,1)} %pad_maximum_fusion.pre_ref, bf16[256,512]{1,0:T(8,128)(2,1)} %in_ref.1, bf16[512,128]{1,0:T(8,128)(2,1)} %in_proj_ref.1, bf16[1376,64]{1,0:T(8,128)(2,1)} %copy.65.hid_proj_ref, bf16[256,512]{1,0:T(8,128)(2,1)} %cot_ref.1, ...), custom_call_target="tpu_custom_call" | custom-call | flops 281804800 | bytes 2818048 | tf_op jit(solution)/shard_map/local_terms/pallas_call | solution.py:52
  22.0 1.5 broadcast_in_dim.14
  23.5 5.9 %all-to-all-start.1 = ((bf16[4,4,256,256]{3,2,1,0:T(8,128)(2,1)}), bf16[4,4,256,256]{3,2,1,0:T(8,128)(2,1)S(1)}, u32[]{:S(2)}, u32[]{:S(2)}) async-start(bf16[4,4,256,256]{3,2,1,0:T(8,128)(2,1)} %broadcast_in_dim.14), calls=%async_computation.1 | async-start | bytes 4194304 | tf_op jit(solution)/shard_map/all_to_all | solution.py:211
  29.5 1.9 %collective-permute-start = (bf16[512,1408]{1,0:T(8,128)(2,1)}, bf16[512,1408]{1,0:T(8,128)(2,1)}, u32[]{:S(2)}, u32[]{:S(2)}) collective-permute-start(bf16[512,1408]{1,0:T(8,128)(2,1)} %get-tuple-element.20.own_slopes), channel_id=1, source_target_pairs={{0,16},{16,0},{1,17},{17,1},{2,18},{18,2},{3,19},{19,3},{4,20},{20... | collective-permute-start | bytes 4325384 | tf_op jit(solution)/shard_map/ppermute | solution.py:213
  31.7 20.8 %all-to-all-done.1 = bf16[4,4,256,256]{3,2,1,0:T(8,128)(2,1)S(1)} async-done(((bf16[4,4,256,256]{3,2,1,0:T(8,128)(2,1)}), bf16[4,4,256,256]{3,2,1,0:T(8,128)(2,1)S(1)}, u32[]{:S(2)}, u32[]{:S(2)}) %all-to-all-start.1) | async-done | bytes 2097184 | tf_op jit(solution)/shard_map/all_to_all | solution.py:211
  52.5 3.4 %all-to-all-start.2 = ((f32[8,32,256]{2,1,0:T(8,128)}), f32[8,32,256]{2,1,0:T(8,128)S(1)}, u32[]{:S(2)}, u32[]{:S(2)}) async-start(f32[8,32,256]{2,1,0:T(8,128)} %bitcast.8), calls=%async_computation.2 | async-start | bytes 524288 | tf_op jit(solution)/shard_map/all_to_all | solution.py:228
  55.9 6.2 %collective-permute-start.1 = (bf16[384,128]{1,0:T(8,128)(2,1)S(1)}, bf16[384,128]{1,0:T(8,128)(2,1)S(1)}, u32[]{:S(2)}, u32[]{:S(2)}) collective-permute-start(bf16[384,128]{1,0:T(8,128)(2,1)S(1)} %get-tuple-element.33), channel_id=1, source_target_pairs={{0,8},{8,0},{16,24},{24,16},{1,9},{9,1},{17,25},{25,17},{2,10},{10... | collective-permute-start | bytes 294920 | tf_op jit(solution)/shard_map/ppermute | solution.py:222
  62.1 2.1 %collective-permute-start.2 = (bf16[384,128]{1,0:T(8,128)(2,1)S(1)}, bf16[384,128]{1,0:T(8,128)(2,1)S(1)}, u32[]{:S(2)}, u32[]{:S(2)}) collective-permute-start(bf16[384,128]{1,0:T(8,128)(2,1)S(1)} %get-tuple-element.32), channel_id=1, source_target_pairs={{0,16},{8,24},{16,0},{24,8},{1,17},{9,25},{17,1},{25,9},{2,18},{10... | collective-permute-start | bytes 294920 | tf_op jit(solution)/shard_map/ppermute | solution.py:222
  64.3 0.7 dynamic_slice.18
  64.9 0.7 compare_convert_fusion
  65.7 3.3 %collective-permute-done.2 = bf16[384,128]{1,0:T(8,128)(2,1)S(1)} collective-permute-done((bf16[384,128]{1,0:T(8,128)(2,1)S(1)}, bf16[384,128]{1,0:T(8,128)(2,1)S(1)}, u32[]{:S(2)}, u32[]{:S(2)}) %collective-permute-start.2) | collective-permute-done | bytes 98336 | tf_op jit(solution)/shard_map/ppermute | solution.py:222
  69.1 0.7 broadcast_in_dim.15
  69.8 6.5 %all-to-all-start.3 = ((f32[16,32,128]{2,1,0:T(8,128)}), f32[16,32,128]{2,1,0:T(8,128)S(1)}, u32[]{:S(2)}, u32[]{:S(2)}) async-start(f32[16,32,128]{2,1,0:T(8,128)} %broadcast_in_dim.15), calls=%async_computation.3 | async-start | bytes 524288 | tf_op jit(solution)/shard_map/all_to_all | solution.py:176
  76.3 4.4 %collective-permute-start.3 = (bf16[384,128]{1,0:T(8,128)(2,1)S(1)}, bf16[384,128]{1,0:T(8,128)(2,1)S(1)}, u32[]{:S(2)}, u32[]{:S(2)}) collective-permute-start(bf16[384,128]{1,0:T(8,128)(2,1)S(1)} %get-tuple-element.31), channel_id=1, source_target_pairs={{0,24},{8,16},{16,8},{24,0},{1,25},{9,17},{17,9},{25,1},{2,26},{10... | collective-permute-start | bytes 294920 | tf_op jit(solution)/shard_map/ppermute | solution.py:222
  80.7 0.9 fusion.8.down_hbm
  81.6 4.0 %collective-permute-done.3._ = bf16[384,128]{1,0:T(8,128)(2,1)S(1)} collective-permute-done((bf16[384,128]{1,0:T(8,128)(2,1)S(1)}, bf16[384,128]{1,0:T(8,128)(2,1)S(1)}, u32[]{:S(2)}, u32[]{:S(2)}) %collective-permute-start.3) | collective-permute-done | bytes 98336 | tf_op jit(solution)/shard_map/ppermute | solution.py:222
  85.6 6.2 %all-gather.3.cloned.1.call-done = bf16[2048,1376]{1,0:T(8,128)(2,1)} async-done(((bf16[64,1376]{1,0:T(8,128)(2,1)}), bf16[2048,1376]{1,0:T(8,128)(2,1)}) %all-gather.3.cloned.1.call-update) | async-done | bytes 5636112 | tf_op jit(solution)/shard_map/all_gather | solution.py:198
  91.7 8.0 %gradient_blocks.1 = f32[32,1,384]{2,1,0:T(1,128)} custom-call(s32[1]{0:T(128)} %bitcast.yl_ref, bf16[4,2,2,256,256]{4,3,2,1,0:T(8,128)(2,1)} %bitcast.37, bf16[2,16,64,1376]{3,2,1,0:T(8,128)(2,1)} %bitcast.38, bf16[512,1408]{1,0:T(8,128)(2,1)} %get-tuple-element.20.own_slopes, bf16[512,1408]{1,0:T(8,128)(2,1)} %collective-permute-done.partner_slopes, ...), custom_call_target="tpu_custom_call" | custom-call | flops 2885681152 | bytes 5636096 | tf_op jit(solution)/shard_map/gradient_blocks/pallas_call | solution.py:141
  99.7 7.2 %all-to-all-start.4 = ((f32[32,1,384]{2,1,0:T(1,128)}), f32[32,1,384]{2,1,0:T(1,128)S(1)}, u32[]{:S(2)}, u32[]{:S(2)}) async-start(f32[32,1,384]{2,1,0:T(1,128)} %gradient_blocks.1), calls=%async_computation.4 | async-start | bytes 98304 | tf_op jit(solution)/shard_map/all_to_all | solution.py:245
  106.9 7.0 %all-to-all-done.4 = f32[32,1,384]{2,1,0:T(1,128)S(1)} async-done(((f32[32,1,384]{2,1,0:T(1,128)}), f32[32,1,384]{2,1,0:T(1,128)S(1)}, u32[]{:S(2)}, u32[]{:S(2)}) %all-to-all-start.4) | async-done | bytes 49184 | tf_op jit(solution)/shard_map/all_to_all | solution.py:245
  114.6 8.2 %all-to-all-start.5 = ((f32[16,1,384]{2,1,0:T(1,128)}), f32[16,1,384]{2,1,0:T(1,128)S(1)}, u32[]{:S(2)}, u32[]{:S(2)}) async-start(f32[16,1,384]{2,1,0:T(1,128)} %broadcast_in_dim.16), calls=%async_computation.5 | async-start | bytes 49152 | tf_op jit(solution)/shard_map/all_to_all | solution.py:176
  122.8 0.9 broadcast_select_fusion.5
  123.8 10.5 %all-to-all-done.5 = f32[16,1,384]{2,1,0:T(1,128)S(1)} async-done(((f32[16,1,384]{2,1,0:T(1,128)}), f32[16,1,384]{2,1,0:T(1,128)S(1)}, u32[]{:S(2)}, u32[]{:S(2)}) %all-to-all-start.5) | async-done | bytes 24608 | tf_op jit(solution)/shard_map/all_to_all | solution.py:176
  134.7 12.8 %all_to_all.35 = f32[32,8,128]{2,1,0:T(8,128)S(1)} all-to-all(f32[32,8,128]{2,1,0:T(8,128)S(1)} %bitcast.44), channel_id=1, replica_groups=mesh['zh'=8,'zl'=2,'yl'=2,'c'=2,'x'=4,'yh'=2] {'c','yl','yh','x'}, dimensions={0} | all-to-all | bytes 262144 | tf_op jit(solution)/shard_map/all_to_all | solution.py:255
  147.4 0.6 reduce_sum.39
  (39 shorter events, 2.3 us)
Async XLA Ops:
  6.5 8.0 %copy-start.2 = (bf16[256,1376]{0,1:T(8,128)(2,1)S(1)}, bf16[256,1376]{0,1:T(8,128)(2,1)}, u32[]{:S(2)}) copy-start(bf16[256,1376]{0,1:T(8,128)(2,1)} %param.13) | copy-start | bytes 2113540
  6.5 85.2 %all-gather.3.cloned.1.call-start = ((), (), s32[]{:S(2)}) async-start(), calls=%async_computation.7 | async-start | bytes 5947392 | tf_op jit(solution)/shard_map/all_gather | solution.py:198
  8.3 6.5 %copy-start.3 = (bf16[256,1376]{0,1:T(8,128)(2,1)S(1)}, bf16[256,1376]{0,1:T(8,128)(2,1)}, u32[]{:S(2)}) copy-start(bf16[256,1376]{0,1:T(8,128)(2,1)} %param.14) | copy-start | bytes 2113540
  9.3 5.8 %copy-start.6 = (bf16[1376,64]{0,1:T(8,128)(2,1)S(1)}, bf16[1376,64]{0,1:T(8,128)(2,1)}, u32[]{:S(2)}) copy-start(bf16[1376,64]{0,1:T(8,128)(2,1)} %param.17) | copy-start | bytes 528388
  9.3 6.8 %copy-start.7 = (bf16[512,64]{0,1:T(8,128)(2,1)S(1)}, bf16[512,64]{0,1:T(8,128)(2,1)}, u32[]{:S(2)}) copy-start(bf16[512,64]{0,1:T(8,128)(2,1)} %param.19) | copy-start | bytes 196612
  9.4 12.7 %all-to-all-start = ((bf16[4,256,256]{2,1,0:T(8,128)(2,1)}), bf16[4,256,256]{2,1,0:T(8,128)(2,1)S(1)}, u32[]{:S(2)}, u32[]{:S(2)}) async-start(bf16[4,256,256]{2,1,0:T(8,128)(2,1)} %bitcast.4), calls=%async_computation | async-start | bytes 1048576 | tf_op jit(solution)/shard_map/all_to_all | solution.py:204
  23.5 7.9 %copy-start.5 = (bf16[128,1536]{1,0:T(8,128)(2,1)S(1)}, bf16[128,1536]{1,0:T(8,128)(2,1)}, u32[]{:S(2)}) copy-start(bf16[128,1536]{1,0:T(8,128)(2,1)} %param.20) | copy-start | bytes 1179652
  23.5 40.7 %copy-start.8 = (s32[8]{0:T(128)S(1)}, s32[8]{0:T(128)}, u32[]{:S(2)}) copy-start(s32[8]{0:T(128)} %param.21) | copy-start | bytes 100
  23.5 28.9 %all-to-all-start.1 = ((bf16[4,4,256,256]{3,2,1,0:T(8,128)(2,1)}), bf16[4,4,256,256]{3,2,1,0:T(8,128)(2,1)S(1)}, u32[]{:S(2)}, u32[]{:S(2)}) async-start(bf16[4,4,256,256]{3,2,1,0:T(8,128)(2,1)} %broadcast_in_dim.14), calls=%async_computation.1 | async-start | bytes 4194304 | tf_op jit(solution)/shard_map/all_to_all | solution.py:211
  29.5 56.1 %collective-permute-start = (bf16[512,1408]{1,0:T(8,128)(2,1)}, bf16[512,1408]{1,0:T(8,128)(2,1)}, u32[]{:S(2)}, u32[]{:S(2)}) collective-permute-start(bf16[512,1408]{1,0:T(8,128)(2,1)} %get-tuple-element.20.own_slopes), channel_id=1, source_target_pairs={{0,16},{16,0},{1,17},{17,1},{2,18},{18,2},{3,19},{19,3},{4,20},{20... | collective-permute-start | bytes 4325384 | tf_op jit(solution)/shard_map/ppermute | solution.py:213
  52.5 39.3 %copy-start = (bf16[4,4,256,256]{3,2,1,0:T(8,128)(2,1)}, bf16[4,4,256,256]{3,2,1,0:T(8,128)(2,1)S(1)}, u32[]{:S(2)}) copy-start(bf16[4,4,256,256]{3,2,1,0:T(8,128)(2,1)S(1)} %all-to-all-done.1) | copy-start | bytes 6291460
  52.5 13.2 %all-to-all-start.2 = ((f32[8,32,256]{2,1,0:T(8,128)}), f32[8,32,256]{2,1,0:T(8,128)S(1)}, u32[]{:S(2)}, u32[]{:S(2)}) async-start(f32[8,32,256]{2,1,0:T(8,128)} %bitcast.8), calls=%async_computation.2 | async-start | bytes 524288 | tf_op jit(solution)/shard_map/all_to_all | solution.py:228
  55.9 9.8 %collective-permute-start.1 = (bf16[384,128]{1,0:T(8,128)(2,1)S(1)}, bf16[384,128]{1,0:T(8,128)(2,1)S(1)}, u32[]{:S(2)}, u32[]{:S(2)}) collective-permute-start(bf16[384,128]{1,0:T(8,128)(2,1)S(1)} %get-tuple-element.33), channel_id=1, source_target_pairs={{0,8},{8,0},{16,24},{24,16},{1,9},{9,1},{17,25},{25,17},{2,10},{10... | collective-permute-start | bytes 294920 | tf_op jit(solution)/shard_map/ppermute | solution.py:222
  62.1 6.9 %collective-permute-start.2 = (bf16[384,128]{1,0:T(8,128)(2,1)S(1)}, bf16[384,128]{1,0:T(8,128)(2,1)S(1)}, u32[]{:S(2)}, u32[]{:S(2)}) collective-permute-start(bf16[384,128]{1,0:T(8,128)(2,1)S(1)} %get-tuple-element.32), channel_id=1, source_target_pairs={{0,16},{8,24},{16,0},{24,8},{1,17},{9,25},{17,1},{25,9},{2,18},{10... | collective-permute-start | bytes 294920 | tf_op jit(solution)/shard_map/ppermute | solution.py:222
  69.8 15.7 %all-to-all-start.3 = ((f32[16,32,128]{2,1,0:T(8,128)}), f32[16,32,128]{2,1,0:T(8,128)S(1)}, u32[]{:S(2)}, u32[]{:S(2)}) async-start(f32[16,32,128]{2,1,0:T(8,128)} %broadcast_in_dim.15), calls=%async_computation.3 | async-start | bytes 524288 | tf_op jit(solution)/shard_map/all_to_all | solution.py:176
  76.3 9.2 %collective-permute-start.3 = (bf16[384,128]{1,0:T(8,128)(2,1)S(1)}, bf16[384,128]{1,0:T(8,128)(2,1)S(1)}, u32[]{:S(2)}, u32[]{:S(2)}) collective-permute-start(bf16[384,128]{1,0:T(8,128)(2,1)S(1)} %get-tuple-element.31), channel_id=1, source_target_pairs={{0,24},{8,16},{16,8},{24,0},{1,25},{9,17},{17,9},{25,1},{2,26},{10... | collective-permute-start | bytes 294920 | tf_op jit(solution)/shard_map/ppermute | solution.py:222
  85.6 6.2 %copy-start.4 = (bf16[384,128]{1,0:T(8,128)(2,1)}, bf16[384,128]{1,0:T(8,128)(2,1)S(1)}, u32[]{:S(2)}) copy-start(bf16[384,128]{1,0:T(8,128)(2,1)S(1)} %collective-permute-done.3._) | copy-start | bytes 294916
  85.6 6.2 %copy-start.1 = (f32[16,32,128]{2,1,0:T(8,128)}, f32[16,32,128]{2,1,0:T(8,128)S(1)}, u32[]{:S(2)}) copy-start(f32[16,32,128]{2,1,0:T(8,128)S(1)} %all-to-all-done.3) | copy-start | bytes 786436
  99.7 14.2 %all-to-all-start.4 = ((f32[32,1,384]{2,1,0:T(1,128)}), f32[32,1,384]{2,1,0:T(1,128)S(1)}, u32[]{:S(2)}, u32[]{:S(2)}) async-start(f32[32,1,384]{2,1,0:T(1,128)} %gradient_blocks.1), calls=%async_computation.4 | async-start | bytes 98304 | tf_op jit(solution)/shard_map/all_to_all | solution.py:245
  114.6 19.6 %all-to-all-start.5 = ((f32[16,1,384]{2,1,0:T(1,128)}), f32[16,1,384]{2,1,0:T(1,128)S(1)}, u32[]{:S(2)}, u32[]{:S(2)}) async-start(f32[16,1,384]{2,1,0:T(1,128)} %broadcast_in_dim.16), calls=%async_computation.5 | async-start | bytes 49152 | tf_op jit(solution)/shard_map/all_to_all | solution.py:176
Sparse Core Ops, SparseCore 0:
  9.5 82.2 all-gather.2

commit v9 on v8

--- a/solution.py
+++ b/solution.py
@@ -97,7 +97,7 @@
     of_cot, of_weight = copies[: len(cot_moves)], copies[len(cot_moves) :][: len(weight_moves)]
     of_slopes = copies[len(cot_moves) + len(weight_moves) :]
     of_chunk = [
-        of_cot[i * per_chunk :][:per_chunk] + of_weight[i * cores :][:cores] for i in range(CHUNKS)
+        of_weight[i * cores :][:cores] + of_cot[i * per_chunk :][:per_chunk] for i in range(CHUNKS)
     ]
     for copy in sum(of_chunk, []) + of_slopes:
         copy.start()

time: 156 us -> 156 us (level)
  no operation moved by 1% of the time
where the time goes in v9:
time: 156 us; the launch traced here: 155 us
  waiting for transfers between devices  52.5 us (34%)
  starting transfers between devices  51 us (33%)
  between operations  13.7 us (9%)
  blocking collectives  12.8 us (8%)
  Pallas kernels  11.7 us (8%)
  local copies, waits for them, and re-layouts  8.28 us (5%)
  other arithmetic  3.74 us (2%)
    all_to_all x1, waiting for transfers between devices, on_device(): lax.all_to_all(along_y, 'x', 0, 0)  20.8 us
    all_to_all x2, starting transfers between devices, give_all(): lax.all_to_all(jnp.broadcast_to(block[None], (n,) + block.shape), axes, 0...  14.7 us
    all_to_all x1, blocking collectives, on_device(): return lax.all_to_all(partial_scores, SHARE, 0, 0).sum(axis=0)  12.8 us
    ppermute x3, starting transfers between devices, on_device(): arrivals.append(lax.ppermute(piece, QUERY_GROUP, pairs) if flip else piece)  12.7 us
    all_to_all x2, waiting for transfers between devices, give_all(): lax.all_to_all(jnp.broadcast_to(block[None], (n,) + block.shape), axes, 0...  10.5 us
    pallas_call x1, Pallas kernels, gradient_blocks(): pl.pallas_call(gradient_kernel, out_shape=jax.ShapeDtypeStruct((members,...  7.81 us
    ppermute x3, waiting for transfers between devices, on_device(): arrivals.append(lax.ppermute(piece, QUERY_GROUP, pairs) if flip else piece)  7.31 us
    all_to_all x1, starting transfers between devices, on_device(): entries = lax.all_to_all(blocks, SHARE, 0, 0).sum(axis=0)  7.2 us
  transfers between devices with their start and end apart: 11, of which 6 were waited for; matrix products, arithmetic and copies ran while one was open for 7% of the time, Pallas kernels for 2%

profile of v9, /device:TPU:1, one launch (start us, length us, event | category | flops | bytes accessed | tf_op | source)
XLA Modules:
  0.0 154.8 jit_solution(9671599011499250661)
XLA Ops:
  6.5 0.7 all-gather.3.cloned.1.call-update
  7.3 1.1 copy.67
  8.5 0.8 broadcast_in_dim.13
  9.4 5.1 %all-to-all-start = ((bf16[4,256,256]{2,1,0:T(8,128)(2,1)}), bf16[4,256,256]{2,1,0:T(8,128)(2,1)S(1)}, u32[]{:S(2)}, u32[]{:S(2)}) async-start(bf16[4,256,256]{2,1,0:T(8,128)(2,1)} %bitcast.4), calls=%async_computation | async-start | bytes 1048576 | tf_op jit(solution)/shard_map/all_to_all | solution.py:204
  15.2 0.9 copy.65.hid_proj_ref
  16.1 0.8 copy.66.out_proj_ref
  16.9 1.3 pad_maximum_fusion.pre_ref
  18.1 3.9 %local_terms.1 = (bf16[512,1408]{1,0:T(8,128)(2,1)}, f32[256,256]{1,0:T(8,128)}) custom-call(bf16[512,1376]{1,0:T(8,128)(2,1)} %pad_maximum_fusion.pre_ref, bf16[256,512]{1,0:T(8,128)(2,1)} %in_ref.1, bf16[512,128]{1,0:T(8,128)(2,1)} %in_proj_ref.1, bf16[1376,64]{1,0:T(8,128)(2,1)} %copy.65.hid_proj_ref, bf16[256,512]{1,0:T(8,128)(2,1)} %cot_ref.1, ...), custom_call_target="tpu_custom_call" | custom-call | flops 281804800 | bytes 2818048 | tf_op jit(solution)/shard_map/local_terms/pallas_call | solution.py:52
  22.0 1.5 broadcast_in_dim.14
  23.5 5.9 %all-to-all-start.1 = ((bf16[4,4,256,256]{3,2,1,0:T(8,128)(2,1)}), bf16[4,4,256,256]{3,2,1,0:T(8,128)(2,1)S(1)}, u32[]{:S(2)}, u32[]{:S(2)}) async-start(bf16[4,4,256,256]{3,2,1,0:T(8,128)(2,1)} %broadcast_in_dim.14), calls=%async_computation.1 | async-start | bytes 4194304 | tf_op jit(solution)/shard_map/all_to_all | solution.py:211
  29.5 1.9 %collective-permute-start = (bf16[512,1408]{1,0:T(8,128)(2,1)}, bf16[512,1408]{1,0:T(8,128)(2,1)}, u32[]{:S(2)}, u32[]{:S(2)}) collective-permute-start(bf16[512,1408]{1,0:T(8,128)(2,1)} %get-tuple-element.20.own_slopes), channel_id=1, source_target_pairs={{0,16},{16,0},{1,17},{17,1},{2,18},{18,2},{3,19},{19,3},{4,20},{20... | collective-permute-start | bytes 4325384 | tf_op jit(solution)/shard_map/ppermute | solution.py:213
  31.7 20.8 %all-to-all-done.1 = bf16[4,4,256,256]{3,2,1,0:T(8,128)(2,1)S(1)} async-done(((bf16[4,4,256,256]{3,2,1,0:T(8,128)(2,1)}), bf16[4,4,256,256]{3,2,1,0:T(8,128)(2,1)S(1)}, u32[]{:S(2)}, u32[]{:S(2)}) %all-to-all-start.1) | async-done | bytes 2097184 | tf_op jit(solution)/shard_map/all_to_all | solution.py:211
  52.5 3.4 %all-to-all-start.2 = ((f32[8,32,256]{2,1,0:T(8,128)}), f32[8,32,256]{2,1,0:T(8,128)S(1)}, u32[]{:S(2)}, u32[]{:S(2)}) async-start(f32[8,32,256]{2,1,0:T(8,128)} %bitcast.8), calls=%async_computation.2 | async-start | bytes 524288 | tf_op jit(solution)/shard_map/all_to_all | solution.py:228
  55.9 6.2 %collective-permute-start.1 = (bf16[384,128]{1,0:T(8,128)(2,1)S(1)}, bf16[384,128]{1,0:T(8,128)(2,1)S(1)}, u32[]{:S(2)}, u32[]{:S(2)}) collective-permute-start(bf16[384,128]{1,0:T(8,128)(2,1)S(1)} %get-tuple-element.33), channel_id=1, source_target_pairs={{0,8},{8,0},{16,24},{24,16},{1,9},{9,1},{17,25},{25,17},{2,10},{10... | collective-permute-start | bytes 294920 | tf_op jit(solution)/shard_map/ppermute | solution.py:222
  62.1 2.1 %collective-permute-start.2 = (bf16[384,128]{1,0:T(8,128)(2,1)S(1)}, bf16[384,128]{1,0:T(8,128)(2,1)S(1)}, u32[]{:S(2)}, u32[]{:S(2)}) collective-permute-start(bf16[384,128]{1,0:T(8,128)(2,1)S(1)} %get-tuple-element.32), channel_id=1, source_target_pairs={{0,16},{8,24},{16,0},{24,8},{1,17},{9,25},{17,1},{25,9},{2,18},{10... | collective-permute-start | bytes 294920 | tf_op jit(solution)/shard_map/ppermute | solution.py:222
  64.3 0.7 dynamic_slice.18
  64.9 0.7 compare_convert_fusion
  65.7 3.3 %collective-permute-done.2 = bf16[384,128]{1,0:T(8,128)(2,1)S(1)} collective-permute-done((bf16[384,128]{1,0:T(8,128)(2,1)S(1)}, bf16[384,128]{1,0:T(8,128)(2,1)S(1)}, u32[]{:S(2)}, u32[]{:S(2)}) %collective-permute-start.2) | collective-permute-done | bytes 98336 | tf_op jit(solution)/shard_map/ppermute | solution.py:222
  69.1 0.7 broadcast_in_dim.15
  69.8 6.5 %all-to-all-start.3 = ((f32[16,32,128]{2,1,0:T(8,128)}), f32[16,32,128]{2,1,0:T(8,128)S(1)}, u32[]{:S(2)}, u32[]{:S(2)}) async-start(f32[16,32,128]{2,1,0:T(8,128)} %broadcast_in_dim.15), calls=%async_computation.3 | async-start | bytes 524288 | tf_op jit(solution)/shard_map/all_to_all | solution.py:176
  76.3 4.4 %collective-permute-start.3 = (bf16[384,128]{1,0:T(8,128)(2,1)S(1)}, bf16[384,128]{1,0:T(8,128)(2,1)S(1)}, u32[]{:S(2)}, u32[]{:S(2)}) collective-permute-start(bf16[384,128]{1,0:T(8,128)(2,1)S(1)} %get-tuple-element.31), channel_id=1, source_target_pairs={{0,24},{8,16},{16,8},{24,0},{1,25},{9,17},{17,9},{25,1},{2,26},{10... | collective-permute-start | bytes 294920 | tf_op jit(solution)/shard_map/ppermute | solution.py:222
  80.7 0.9 fusion.8.down_hbm
  81.6 4.0 %collective-permute-done.3._ = bf16[384,128]{1,0:T(8,128)(2,1)S(1)} collective-permute-done((bf16[384,128]{1,0:T(8,128)(2,1)S(1)}, bf16[384,128]{1,0:T(8,128)(2,1)S(1)}, u32[]{:S(2)}, u32[]{:S(2)}) %collective-permute-start.3) | collective-permute-done | bytes 98336 | tf_op jit(solution)/shard_map/ppermute | solution.py:222
  85.6 6.2 %all-gather.3.cloned.1.call-done = bf16[2048,1376]{1,0:T(8,128)(2,1)} async-done(((bf16[64,1376]{1,0:T(8,128)(2,1)}), bf16[2048,1376]{1,0:T(8,128)(2,1)}) %all-gather.3.cloned.1.call-update) | async-done | bytes 5636112 | tf_op jit(solution)/shard_map/all_gather | solution.py:198
  91.7 7.8 %gradient_blocks.1 = f32[32,1,384]{2,1,0:T(1,128)} custom-call(s32[1]{0:T(128)} %bitcast.yl_ref, bf16[4,2,2,256,256]{4,3,2,1,0:T(8,128)(2,1)} %bitcast.37, bf16[2,16,64,1376]{3,2,1,0:T(8,128)(2,1)} %bitcast.38, bf16[512,1408]{1,0:T(8,128)(2,1)} %get-tuple-element.20.own_slopes, bf16[512,1408]{1,0:T(8,128)(2,1)} %collective-permute-done.partner_slopes, ...), custom_call_target="tpu_custom_call" | custom-call | flops 2885681152 | bytes 5636096 | tf_op jit(solution)/shard_map/gradient_blocks/pallas_call | solution.py:141
  99.6 7.2 %all-to-all-start.4 = ((f32[32,1,384]{2,1,0:T(1,128)}), f32[32,1,384]{2,1,0:T(1,128)S(1)}, u32[]{:S(2)}, u32[]{:S(2)}) async-start(f32[32,1,384]{2,1,0:T(1,128)} %gradient_blocks.1), calls=%async_computation.4 | async-start | bytes 98304 | tf_op jit(solution)/shard_map/all_to_all | solution.py:245
  106.8 7.0 %all-to-all-done.4 = f32[32,1,384]{2,1,0:T(1,128)S(1)} async-done(((f32[32,1,384]{2,1,0:T(1,128)}), f32[32,1,384]{2,1,0:T(1,128)S(1)}, u32[]{:S(2)}, u32[]{:S(2)}) %all-to-all-start.4) | async-done | bytes 49184 | tf_op jit(solution)/shard_map/all_to_all | solution.py:245
  114.5 8.2 %all-to-all-start.5 = ((f32[16,1,384]{2,1,0:T(1,128)}), f32[16,1,384]{2,1,0:T(1,128)S(1)}, u32[]{:S(2)}, u32[]{:S(2)}) async-start(f32[16,1,384]{2,1,0:T(1,128)} %broadcast_in_dim.16), calls=%async_computation.5 | async-start | bytes 49152 | tf_op jit(solution)/shard_map/all_to_all | solution.py:176
  122.7 0.9 broadcast_select_fusion.5
  123.6 10.5 %all-to-all-done.5 = f32[16,1,384]{2,1,0:T(1,128)S(1)} async-done(((f32[16,1,384]{2,1,0:T(1,128)}), f32[16,1,384]{2,1,0:T(1,128)S(1)}, u32[]{:S(2)}, u32[]{:S(2)}) %all-to-all-start.5) | async-done | bytes 24608 | tf_op jit(solution)/shard_map/all_to_all | solution.py:176
  134.5 12.8 %all_to_all.35 = f32[32,8,128]{2,1,0:T(8,128)S(1)} all-to-all(f32[32,8,128]{2,1,0:T(8,128)S(1)} %bitcast.44), channel_id=1, replica_groups=mesh['zh'=8,'zl'=2,'yl'=2,'c'=2,'x'=4,'yh'=2] {'c','yl','yh','x'}, dimensions={0} | all-to-all | bytes 262144 | tf_op jit(solution)/shard_map/all_to_all | solution.py:255
  147.3 0.6 reduce_sum.39
  (39 shorter events, 2.3 us)
Async XLA Ops:
  6.5 8.0 %copy-start.2 = (bf16[256,1376]{0,1:T(8,128)(2,1)S(1)}, bf16[256,1376]{0,1:T(8,128)(2,1)}, u32[]{:S(2)}) copy-start(bf16[256,1376]{0,1:T(8,128)(2,1)} %param.13) | copy-start | bytes 2113540
  6.5 85.2 %all-gather.3.cloned.1.call-start = ((), (), s32[]{:S(2)}) async-start(), calls=%async_computation.7 | async-start | bytes 5947392 | tf_op jit(solution)/shard_map/all_gather | solution.py:198
  8.3 6.5 %copy-start.3 = (bf16[256,1376]{0,1:T(8,128)(2,1)S(1)}, bf16[256,1376]{0,1:T(8,128)(2,1)}, u32[]{:S(2)}) copy-start(bf16[256,1376]{0,1:T(8,128)(2,1)} %param.14) | copy-start | bytes 2113540
  9.3 5.8 %copy-start.6 = (bf16[1376,64]{0,1:T(8,128)(2,1)S(1)}, bf16[1376,64]{0,1:T(8,128)(2,1)}, u32[]{:S(2)}) copy-start(bf16[1376,64]{0,1:T(8,128)(2,1)} %param.17) | copy-start | bytes 528388
  9.3 6.8 %copy-start.7 = (bf16[512,64]{0,1:T(8,128)(2,1)S(1)}, bf16[512,64]{0,1:T(8,128)(2,1)}, u32[]{:S(2)}) copy-start(bf16[512,64]{0,1:T(8,128)(2,1)} %param.19) | copy-start | bytes 196612
  9.4 12.7 %all-to-all-start = ((bf16[4,256,256]{2,1,0:T(8,128)(2,1)}), bf16[4,256,256]{2,1,0:T(8,128)(2,1)S(1)}, u32[]{:S(2)}, u32[]{:S(2)}) async-start(bf16[4,256,256]{2,1,0:T(8,128)(2,1)} %bitcast.4), calls=%async_computation | async-start | bytes 1048576 | tf_op jit(solution)/shard_map/all_to_all | solution.py:204
  23.5 7.9 %copy-start.5 = (bf16[128,1536]{1,0:T(8,128)(2,1)S(1)}, bf16[128,1536]{1,0:T(8,128)(2,1)}, u32[]{:S(2)}) copy-start(bf16[128,1536]{1,0:T(8,128)(2,1)} %param.20) | copy-start | bytes 1179652
  23.5 40.7 %copy-start.8 = (s32[8]{0:T(128)S(1)}, s32[8]{0:T(128)}, u32[]{:S(2)}) copy-start(s32[8]{0:T(128)} %param.21) | copy-start | bytes 100
  23.5 28.9 %all-to-all-start.1 = ((bf16[4,4,256,256]{3,2,1,0:T(8,128)(2,1)}), bf16[4,4,256,256]{3,2,1,0:T(8,128)(2,1)S(1)}, u32[]{:S(2)}, u32[]{:S(2)}) async-start(bf16[4,4,256,256]{3,2,1,0:T(8,128)(2,1)} %broadcast_in_dim.14), calls=%async_computation.1 | async-start | bytes 4194304 | tf_op jit(solution)/shard_map/all_to_all | solution.py:211
  29.5 56.1 %collective-permute-start = (bf16[512,1408]{1,0:T(8,128)(2,1)}, bf16[512,1408]{1,0:T(8,128)(2,1)}, u32[]{:S(2)}, u32[]{:S(2)}) collective-permute-start(bf16[512,1408]{1,0:T(8,128)(2,1)} %get-tuple-element.20.own_slopes), channel_id=1, source_target_pairs={{0,16},{16,0},{1,17},{17,1},{2,18},{18,2},{3,19},{19,3},{4,20},{20... | collective-permute-start | bytes 4325384 | tf_op jit(solution)/shard_map/ppermute | solution.py:213
  52.5 39.3 %copy-start = (bf16[4,4,256,256]{3,2,1,0:T(8,128)(2,1)}, bf16[4,4,256,256]{3,2,1,0:T(8,128)(2,1)S(1)}, u32[]{:S(2)}) copy-start(bf16[4,4,256,256]{3,2,1,0:T(8,128)(2,1)S(1)} %all-to-all-done.1) | copy-start | bytes 6291460
  52.5 13.2 %all-to-all-start.2 = ((f32[8,32,256]{2,1,0:T(8,128)}), f32[8,32,256]{2,1,0:T(8,128)S(1)}, u32[]{:S(2)}, u32[]{:S(2)}) async-start(f32[8,32,256]{2,1,0:T(8,128)} %bitcast.8), calls=%async_computation.2 | async-start | bytes 524288 | tf_op jit(solution)/shard_map/all_to_all | solution.py:228
  55.9 9.8 %collective-permute-start.1 = (bf16[384,128]{1,0:T(8,128)(2,1)S(1)}, bf16[384,128]{1,0:T(8,128)(2,1)S(1)}, u32[]{:S(2)}, u32[]{:S(2)}) collective-permute-start(bf16[384,128]{1,0:T(8,128)(2,1)S(1)} %get-tuple-element.33), channel_id=1, source_target_pairs={{0,8},{8,0},{16,24},{24,16},{1,9},{9,1},{17,25},{25,17},{2,10},{10... | collective-permute-start | bytes 294920 | tf_op jit(solution)/shard_map/ppermute | solution.py:222
  62.1 6.9 %collective-permute-start.2 = (bf16[384,128]{1,0:T(8,128)(2,1)S(1)}, bf16[384,128]{1,0:T(8,128)(2,1)S(1)}, u32[]{:S(2)}, u32[]{:S(2)}) collective-permute-start(bf16[384,128]{1,0:T(8,128)(2,1)S(1)} %get-tuple-element.32), channel_id=1, source_target_pairs={{0,16},{8,24},{16,0},{24,8},{1,17},{9,25},{17,1},{25,9},{2,18},{10... | collective-permute-start | bytes 294920 | tf_op jit(solution)/shard_map/ppermute | solution.py:222
  69.8 15.7 %all-to-all-start.3 = ((f32[16,32,128]{2,1,0:T(8,128)}), f32[16,32,128]{2,1,0:T(8,128)S(1)}, u32[]{:S(2)}, u32[]{:S(2)}) async-start(f32[16,32,128]{2,1,0:T(8,128)} %broadcast_in_dim.15), calls=%async_computation.3 | async-start | bytes 524288 | tf_op jit(solution)/shard_map/all_to_all | solution.py:176
  76.3 9.2 %collective-permute-start.3 = (bf16[384,128]{1,0:T(8,128)(2,1)S(1)}, bf16[384,128]{1,0:T(8,128)(2,1)S(1)}, u32[]{:S(2)}, u32[]{:S(2)}) collective-permute-start(bf16[384,128]{1,0:T(8,128)(2,1)S(1)} %get-tuple-element.31), channel_id=1, source_target_pairs={{0,24},{8,16},{16,8},{24,0},{1,25},{9,17},{17,9},{25,1},{2,26},{10... | collective-permute-start | bytes 294920 | tf_op jit(solution)/shard_map/ppermute | solution.py:222
  85.6 6.2 %copy-start.4 = (bf16[384,128]{1,0:T(8,128)(2,1)}, bf16[384,128]{1,0:T(8,128)(2,1)S(1)}, u32[]{:S(2)}) copy-start(bf16[384,128]{1,0:T(8,128)(2,1)S(1)} %collective-permute-done.3._) | copy-start | bytes 294916
  85.6 6.2 %copy-start.1 = (f32[16,32,128]{2,1,0:T(8,128)}, f32[16,32,128]{2,1,0:T(8,128)S(1)}, u32[]{:S(2)}) copy-start(f32[16,32,128]{2,1,0:T(8,128)S(1)} %all-to-all-done.3) | copy-start | bytes 786436
  99.6 14.2 %all-to-all-start.4 = ((f32[32,1,384]{2,1,0:T(1,128)}), f32[32,1,384]{2,1,0:T(1,128)S(1)}, u32[]{:S(2)}, u32[]{:S(2)}) async-start(f32[32,1,384]{2,1,0:T(1,128)} %gradient_blocks.1), calls=%async_computation.4 | async-start | bytes 98304 | tf_op jit(solution)/shard_map/all_to_all | solution.py:245
  114.5 19.6 %all-to-all-start.5 = ((f32[16,1,384]{2,1,0:T(1,128)}), f32[16,1,384]{2,1,0:T(1,128)S(1)}, u32[]{:S(2)}, u32[]{:S(2)}) async-start(f32[16,1,384]{2,1,0:T(1,128)} %broadcast_in_dim.16), calls=%async_computation.5 | async-start | bytes 49152 | tf_op jit(solution)/shard_map/all_to_all | solution.py:176
Sparse Core Ops, SparseCore 0:
  9.5 82.2 all-gather.2
